TPU v7x, 32 devices: a whole 2x2x4 slice. The times are simulated.
32 devices in a mesh: fsdp: 8 (over z, y), tp: 4 (over x, core).
Axes of the slice: x: 2, y: 2, z: 4, core: 2. Of those that a mesh axis runs over, the one named last changes fastest.
Arguments:
- tokens: bfloat16 [2, 16384, 768], P(None, ('fsdp', 'tp')), may hold values from -6 to 6
- cotangent: bfloat16 [2, 16384, 768], P(None, ('fsdp', 'tp')), may hold values from -6 to 6
- gain_attn: float32 [768], replicated, may hold values from 0.5 to 1.5
- gain_moe: float32 [768], replicated, may hold values from 0.5 to 1.5
- qkv_weight: bfloat16 [768, 2304], P('fsdp', 'tp'), may hold values from -0.21875 to 0.21875
- out_weight: bfloat16 [768, 768], P('tp', 'fsdp'), may hold values from -3.5 to 3.5
- router: bfloat16 [768, 8], replicated, may hold values from -0.15625 to 0.15625
- w_in: bfloat16 [8, 768, 3072], P(None, 'fsdp', 'tp'), may hold values from -0.21875 to 0.21875
- w_out: bfloat16 [8, 3072, 768], P(None, 'tp', 'fsdp'), may hold values from -0.109375 to 0.109375
- doc_lengths: int32 [2, 8, 4], P(None, 'fsdp'), may hold values from 1 to 1792, 2048 in all within a row
- routes: int32 [2, 16384, 2], P(None, 'fsdp'), may hold values from 0 to 7, all different within a row; in each aligned block of 2048 rows (0 to 2047, 2048 to 4095, ..., all dimensions but the last counted through in order) at most 768 rows name the same one
- capacity: int32 [8], replicated, may hold values from 384 to 768, as said below
Outputs:
- output: bfloat16 [2, 16384, 768], P(None, ('fsdp', 'tp'))
- grad_tokens: bfloat16 [2, 16384, 768], P(None, ('fsdp', 'tp'))
- grad_gain_attn: float32 [768], replicated
- grad_gain_moe: float32 [768], replicated
- grad_qkv: float32 [768, 2304], P('fsdp', 'tp')
- grad_out: float32 [768, 768], P('tp', 'fsdp')
- grad_router: float32 [768, 8], replicated
- grad_w_in: float32 [8, 768, 3072], P(None, 'fsdp', 'tp')
- grad_w_out: float32 [8, 3072, 768], P(None, 'tp', 'fsdp')
Inputs may be any that keep to these rules, and one draw needn't show every extreme that they name: `routes`: each row names two different experts. In each aligned block of 2048 rows (one sequence) no expert is named by more than 768 rows, a bound that some block reaches. `capacity`: each is at least 384, and one expert's is exactly 768. `doc_lengths`: the 4 lengths of a sequence sum to 2048; the longest is exactly 1792.
All inputs are finite; a program needn't handle non-finite values.
Results may differ from a plain program's by a relative error of at most 0.02.
Values may be sent and summed in bfloat16 or wider, within the bound.
A program may use at most 256 MiB of HBM per device.

v0:
```python
import math

import jax
import jax.numpy as jnp
from jax import lax
from jax.sharding import PartitionSpec as P

HEAD_DIM = 64
SEQ = 2048
WINDOW = 1024
QBLOCK = 512
CAP = 768


epsilon = 1e-06
neg_big = -1e30


def norm_scaled(values, gain):
    return values * lax.rsqrt(jnp.mean(values * values, axis=-1, keepdims=True) + epsilon) * gain


def doc_numbers(lengths, seq_len):
    ends = jnp.cumsum(lengths)
    places = jnp.arange(seq_len, dtype=jnp.int32)
    return jnp.sum((places[:, None] >= ends[None, :]).astype(jnp.int32), axis=1)


def block_mask(start, docs_pad):
    q_place = start + jnp.arange(QBLOCK, dtype=jnp.int32)
    k_place = start - WINDOW + jnp.arange(QBLOCK + WINDOW, dtype=jnp.int32)
    q_doc = lax.dynamic_slice_in_dim(docs_pad, start + WINDOW, QBLOCK, 0)
    k_doc = lax.dynamic_slice_in_dim(docs_pad, start, QBLOCK + WINDOW, 0)
    causal = k_place[None, :] <= q_place[:, None]
    inside = q_place[:, None] - k_place[None, :] < WINDOW
    return causal & inside & (q_doc[:, None] == k_doc[None, :])


def dispatch(picks, capacity, experts, seq_len):
    onehot = (picks[:, :, None] == jnp.arange(experts, dtype=jnp.int32)[None, None, :]).astype(
        jnp.int32
    )
    per_token = jnp.sum(onehot, axis=1)
    before = jnp.cumsum(per_token, axis=0) - per_token
    rank = jnp.sum(before[:, None, :] * onehot, axis=2)
    limit = jnp.sum(capacity[None, None, :] * onehot, axis=2)
    slot = jnp.where(rank < limit, picks * CAP + rank, experts * CAP)
    owner = jnp.broadcast_to(jnp.arange(seq_len, dtype=jnp.int32)[:, None], (seq_len, 2))
    token_of_slot = (
        jnp.full((experts * CAP,), seq_len, jnp.int32)
        .at[slot.reshape(-1)]
        .set(owner.reshape(-1), mode="drop")
    )
    return (slot, token_of_slot)


def dispatch_all(picks, capacity, experts, seqs):
    picks_seq = picks.reshape(seqs, SEQ, 2)
    slot_seq, owner_seq = jax.vmap(lambda chosen: dispatch(chosen, capacity, experts, SEQ))(
        picks_seq
    )
    seq_ids = jnp.arange(seqs, dtype=jnp.int32)
    each = seqs * CAP
    slot = jnp.where(
        slot_seq < experts * CAP,
        slot_seq // CAP * each + seq_ids[:, None, None] * CAP + slot_seq % CAP,
        experts * each,
    )
    owner = jnp.where(owner_seq < SEQ, owner_seq + seq_ids[:, None] * SEQ, seqs * SEQ)
    owner = owner.reshape(seqs, experts, CAP).transpose(1, 0, 2).reshape(-1)
    return (slot.reshape(seqs * SEQ, 2), owner)


def padded(values):
    zeros = jnp.zeros((WINDOW,) + values.shape[1:], values.dtype)
    return jnp.concatenate([zeros, values], axis=0)


def block_scores(queries, keys_pad, docs_pad, start, scale):
    q_blk = lax.dynamic_slice_in_dim(queries, start, QBLOCK, 0)
    k_blk = lax.dynamic_slice_in_dim(keys_pad, start, QBLOCK + WINDOW, 0)
    scores = jnp.einsum("qhd,khd->hqk", q_blk, k_blk, preferred_element_type=jnp.float32) * scale
    mask = block_mask(start, docs_pad)
    return (jnp.where(mask[None], scores, neg_big), q_blk, k_blk)


def attend_forward(queries, keys, values, docs_pad, scale):
    keys_pad = padded(keys)
    values_pad = padded(values)

    def one_block(start):
        scores, q_blk, k_blk = block_scores(queries, keys_pad, docs_pad, start, scale)
        v_blk = lax.dynamic_slice_in_dim(values_pad, start, QBLOCK + WINDOW, 0)
        top_score = jnp.max(scores, axis=-1, keepdims=True)
        expd = jnp.exp(scores - top_score)
        total = jnp.sum(expd, axis=-1, keepdims=True)
        probs = expd / total
        mixed = jnp.einsum(
            "hqk,khd->qhd", probs.astype(jnp.bfloat16), v_blk, preferred_element_type=jnp.float32
        )
        return (mixed.astype(jnp.bfloat16), (top_score + jnp.log(total))[..., 0])

    starts = jnp.arange(queries.shape[0] // QBLOCK, dtype=jnp.int32) * QBLOCK
    mixed, log_total = lax.map(one_block, starts)
    return (mixed.reshape(queries.shape), log_total, starts)


def attend_backward(queries, keys, values, docs_pad, scale, log_total, starts, grad_mixed):
    keys_pad = padded(keys)
    values_pad = padded(values)
    span = QBLOCK + WINDOW

    def one_block(carry, item):
        start, block_total = item
        grad_keys, grad_values = carry
        scores, q_blk, k_blk = block_scores(queries, keys_pad, docs_pad, start, scale)
        v_blk = lax.dynamic_slice_in_dim(values_pad, start, span, 0)
        g_blk = lax.dynamic_slice_in_dim(grad_mixed, start, QBLOCK, 0)
        probs = jnp.exp(scores - block_total[..., None])
        dprobs = jnp.einsum("qhd,khd->hqk", g_blk, v_blk, preferred_element_type=jnp.float32)
        dscores = (probs * (dprobs - jnp.sum(probs * dprobs, axis=-1, keepdims=True))).astype(
            jnp.bfloat16
        )
        grad_q = (
            jnp.einsum("hqk,khd->qhd", dscores, k_blk, preferred_element_type=jnp.float32) * scale
        )
        grad_k = (
            jnp.einsum("hqk,qhd->khd", dscores, q_blk, preferred_element_type=jnp.float32) * scale
        )
        grad_v = jnp.einsum(
            "hqk,qhd->khd", probs.astype(jnp.bfloat16), g_blk, preferred_element_type=jnp.float32
        )
        old_keys = lax.dynamic_slice_in_dim(grad_keys, start, span, 0)
        old_values = lax.dynamic_slice_in_dim(grad_values, start, span, 0)
        grad_keys = lax.dynamic_update_slice_in_dim(grad_keys, old_keys + grad_k, start, 0)
        grad_values = lax.dynamic_update_slice_in_dim(grad_values, old_values + grad_v, start, 0)
        return ((grad_keys, grad_values), grad_q)

    zeros = jnp.zeros(keys_pad.shape, jnp.float32)
    (grad_keys, grad_values), grad_q = lax.scan(one_block, (zeros, zeros), (starts, log_total))
    return (grad_q.reshape(queries.shape), grad_keys[WINDOW:], grad_values[WINDOW:])


def local(
    tokens,
    cotangent,
    gain_attn,
    gain_moe,
    qkv_weight,
    out_weight,
    router,
    w_in,
    w_out,
    doc_lengths,
    routes,
    capacity,
):
    group_size = lax.axis_size("tp")
    my_index = lax.axis_index("tp")
    row_count = tokens.shape[1]
    seq_len = row_count * group_size
    seqs = doc_lengths.shape[1]
    each = seqs * CAP
    experts = w_in.shape[0]
    width = tokens.shape[2]
    scale = 1.0 / math.sqrt(HEAD_DIM)
    router_float = router.astype(jnp.float32)
    start_big = tuple(
        (jnp.zeros(weight.shape, jnp.float32) for weight in (qkv_weight, out_weight, w_in, w_out))
    )
    start_small = (
        jnp.zeros(router.shape, jnp.float32),
        jnp.zeros(gain_attn.shape, jnp.float32),
        jnp.zeros(gain_moe.shape, jnp.float32),
    )

    def micro_step(carry, item):
        x_rows, cot_rows, lengths, picks = item
        x_float = x_rows.astype(jnp.float32)
        normed, norm_back_attn = jax.vjp(norm_scaled, x_float, gain_attn)
        normed_rows = normed.astype(jnp.bfloat16)
        w_qkv, w_attn, w_first, w_second = (
            lax.all_gather(qkv_weight, "fsdp", axis=0, tiled=True),
            lax.all_gather(out_weight, "fsdp", axis=1, tiled=True),
            lax.all_gather(w_in, "fsdp", axis=1, tiled=True),
            lax.all_gather(w_out, "fsdp", axis=2, tiled=True),
        )
        normed_all = lax.all_gather(normed_rows, "tp", axis=0, tiled=True)
        heads = w_qkv.shape[1] // (3 * HEAD_DIM)
        proj = jnp.dot(normed_all, w_qkv, preferred_element_type=jnp.float32).astype(jnp.bfloat16)
        proj = proj.reshape(seq_len, heads, 3, HEAD_DIM)
        queries = proj[:, :, 0]
        keys = proj[:, :, 1]
        values = proj[:, :, 2]
        docs = doc_numbers(lengths.reshape(-1), seq_len)
        docs_pad = jnp.concatenate([jnp.full((WINDOW,), -1, jnp.int32), docs])
        mixed, log_total, starts = attend_forward(queries, keys, values, docs_pad, scale)
        mixed_flat = mixed.reshape(seq_len, heads * HEAD_DIM)
        attn_rows = lax.psum_scatter(
            jnp.dot(mixed_flat, w_attn, preferred_element_type=jnp.float32).astype(jnp.bfloat16),
            "tp",
            scatter_dimension=0,
            tiled=True,
        ).astype(jnp.float32)
        hidden = x_float + attn_rows
        normed_two, norm_back_moe = jax.vjp(norm_scaled, hidden, gain_moe)
        moe_rows = normed_two.astype(jnp.bfloat16)
        logits = jnp.dot(moe_rows, router, preferred_element_type=jnp.float32)
        my_picks = lax.dynamic_slice_in_dim(picks, my_index * row_count, row_count, 0)
        onehot_rows = (
            my_picks[:, :, None] == jnp.arange(experts, dtype=jnp.int32)[None, None, :]
        ).astype(jnp.float32)
        chosen = jnp.sum(logits[:, None, :] * onehot_rows, axis=2)
        gates = jax.nn.softmax(chosen, axis=-1)
        moe_all, gates_all = (
            lax.all_gather(moe_rows, "tp", axis=0, tiled=True),
            lax.all_gather(gates.astype(jnp.bfloat16), "tp", axis=0, tiled=True).astype(
                gates.dtype
            ),
        )
        slot, token_of_slot = dispatch_all(picks, capacity, experts, seqs)
        gate_of_slot = (
            jnp.zeros((experts * each,), jnp.float32)
            .at[slot.reshape(-1)]
            .set(gates_all.reshape(-1), mode="drop")
        )
        moe_pad = jnp.concatenate([moe_all, jnp.zeros((1, width), jnp.bfloat16)], axis=0)
        buffer = moe_pad[token_of_slot].reshape(experts, each, width)
        pre = jnp.einsum("ecd,edf->ecf", buffer, w_first, preferred_element_type=jnp.float32)
        act_float, gelu_back = jax.vjp(jax.nn.gelu, pre)
        act = act_float.astype(jnp.bfloat16)
        expert_out = jnp.einsum("ecf,efd->ecd", act, w_second, preferred_element_type=jnp.float32)
        out_pad = jnp.concatenate(
            [expert_out.reshape(experts * each, width), jnp.zeros((1, width), jnp.float32)], axis=0
        )
        picked = out_pad[slot]
        combined = jnp.sum(gates_all[:, :, None] * picked, axis=1)
        expert_rows = lax.psum_scatter(
            combined.astype(jnp.bfloat16), "tp", scatter_dimension=0, tiled=True
        ).astype(jnp.float32)
        out_rows = (hidden + expert_rows).astype(jnp.bfloat16)
        w_qkv, w_attn, w_first, w_second = (
            lax.all_gather(qkv_weight, "fsdp", axis=0, tiled=True),
            lax.all_gather(out_weight, "fsdp", axis=1, tiled=True),
            lax.all_gather(w_in, "fsdp", axis=1, tiled=True),
            lax.all_gather(w_out, "fsdp", axis=2, tiled=True),
        )
        cot_float = cot_rows.astype(jnp.float32)
        cot_all = lax.all_gather(cot_rows, "tp", axis=0, tiled=True).astype(jnp.float32)
        cot_pad = jnp.concatenate([cot_all, jnp.zeros((1, width), jnp.float32)], axis=0)
        grad_expert = (
            (gate_of_slot[:, None] * cot_pad[token_of_slot])
            .astype(jnp.bfloat16)
            .reshape(experts, each, width)
        )
        grad_gates = jnp.sum(cot_all[:, None, :] * picked, axis=2)
        grad_act = jnp.einsum(
            "ecd,efd->ecf", grad_expert, w_second, preferred_element_type=jnp.float32
        )
        grad_pre = gelu_back(grad_act)[0].astype(jnp.bfloat16)
        grad_second = jnp.einsum(
            "ecf,ecd->efd", act, grad_expert, preferred_element_type=jnp.float32
        )
        grad_first = jnp.einsum(
            "ecd,ecf->edf", buffer, grad_pre, preferred_element_type=jnp.float32
        )
        grad_buffer = jnp.einsum(
            "ecf,edf->ecd", grad_pre, w_first, preferred_element_type=jnp.float32
        )
        grad_pad = jnp.concatenate(
            [grad_buffer.reshape(experts * each, width), jnp.zeros((1, width), jnp.float32)], axis=0
        )
        grad_moe_all = jnp.sum(grad_pad[slot], axis=1)
        grad_moe_rows, grad_gate_rows = (
            lax.psum_scatter(
                grad_moe_all.astype(jnp.bfloat16), "tp", scatter_dimension=0, tiled=True
            ).astype(jnp.float32),
            lax.psum_scatter(
                grad_gates.astype(jnp.bfloat16), "tp", scatter_dimension=0, tiled=True
            ).astype(jnp.float32),
        )
        grad_chosen = gates * (
            grad_gate_rows - jnp.sum(gates * grad_gate_rows, axis=-1, keepdims=True)
        )
        grad_logits = jnp.sum(grad_chosen[:, :, None] * onehot_rows, axis=1)
        grad_router = jnp.einsum(
            "td,te->de",
            moe_rows.astype(jnp.float32),
            grad_logits,
            precision=lax.Precision.HIGHEST,
            preferred_element_type=jnp.float32,
        )
        grad_moe_rows = grad_moe_rows + jnp.einsum(
            "te,de->td",
            grad_logits,
            router_float,
            precision=lax.Precision.HIGHEST,
            preferred_element_type=jnp.float32,
        )
        grad_hidden_norm, grad_gain_two = norm_back_moe(grad_moe_rows)
        grad_hidden = cot_float + grad_hidden_norm
        grad_attn_all = lax.all_gather(grad_hidden.astype(jnp.bfloat16), "tp", axis=0, tiled=True)
        grad_attn_weight = jnp.einsum(
            "sk,sd->kd", mixed_flat, grad_attn_all, preferred_element_type=jnp.float32
        )
        grad_mixed = jnp.einsum(
            "sd,kd->sk", grad_attn_all, w_attn, preferred_element_type=jnp.float32
        ).astype(jnp.bfloat16)
        grad_q, grad_k, grad_v = attend_backward(
            queries,
            keys,
            values,
            docs_pad,
            scale,
            log_total,
            starts,
            grad_mixed.reshape(seq_len, heads, HEAD_DIM),
        )
        grad_proj = (
            jnp.stack([grad_q, grad_k, grad_v], axis=2)
            .astype(jnp.bfloat16)
            .reshape(seq_len, heads * 3 * HEAD_DIM)
        )
        grad_qkv_weight = jnp.einsum(
            "sd,sk->dk", normed_all, grad_proj, preferred_element_type=jnp.float32
        )
        grad_normed_rows = lax.psum_scatter(
            jnp.einsum("sk,dk->sd", grad_proj, w_qkv, preferred_element_type=jnp.float32).astype(
                jnp.bfloat16
            ),
            "tp",
            scatter_dimension=0,
            tiled=True,
        ).astype(jnp.float32)
        grad_x_norm, grad_gain_one = norm_back_attn(grad_normed_rows)
        grad_rows = (grad_hidden + grad_x_norm).astype(jnp.bfloat16)
        local_grads = (grad_qkv_weight, grad_attn_weight, grad_first, grad_second)
        shares = (
            lax.psum_scatter(local_grads[0], "fsdp", scatter_dimension=0, tiled=True),
            lax.psum_scatter(local_grads[1], "fsdp", scatter_dimension=1, tiled=True),
            lax.psum_scatter(local_grads[2], "fsdp", scatter_dimension=1, tiled=True),
            lax.psum_scatter(local_grads[3], "fsdp", scatter_dimension=2, tiled=True),
        )
        big_sums, small_sums = carry
        big_sums = jax.tree.map(lambda older, newer: older + newer, big_sums, shares)
        small_sums = (
            small_sums[0] + grad_router,
            small_sums[1] + grad_gain_one,
            small_sums[2] + grad_gain_two,
        )
        return ((big_sums, small_sums), (out_rows, grad_rows))

    (big_sums, small_sums), (output, grad_tokens) = lax.scan(
        micro_step, (start_big, start_small), (tokens, cotangent, doc_lengths, routes)
    )
    grad_qkv, grad_out, grad_w_in, grad_w_out = big_sums
    grad_router, grad_gain_attn, grad_gain_moe = lax.psum(
        (small_sums[0], small_sums[1], small_sums[2]), ("fsdp", "tp")
    )
    return (
        output,
        grad_tokens,
        grad_gain_attn,
        grad_gain_moe,
        grad_qkv,
        grad_out,
        grad_router,
        grad_w_in,
        grad_w_out,
    )


def solution(mesh):
    in_specs = (
        P(None, ("fsdp", "tp"), None),
        P(None, ("fsdp", "tp"), None),
        P(),
        P(),
        P("fsdp", "tp"),
        P("tp", "fsdp"),
        P(),
        P(None, "fsdp", "tp"),
        P(None, "tp", "fsdp"),
        P(None, "fsdp", None),
        P(None, "fsdp", None),
        P(),
    )
    out_specs = (
        P(None, ("fsdp", "tp"), None),
        P(None, ("fsdp", "tp"), None),
        P(),
        P(),
        P("fsdp", "tp"),
        P("tp", "fsdp"),
        P(),
        P(None, "fsdp", "tp"),
        P(None, "tp", "fsdp"),
    )
    return jax.shard_map(local, mesh=mesh, in_specs=in_specs, out_specs=out_specs, check_vma=False)
```

profile of v0, /device:TPU:0, one launch (start us, length us, event | category | flops | bytes accessed | tf_op | source)
XLA Modules:
  0.0 3962.0 jit_solution(9704188759063106264)
XLA Ops:
  10.1 3904.3 %while.91 = (s32[]{:T(128)}, f32[96,576]{1,0:T(8,128)}, f32[192,96]{1,0:T(8,128)}, f32[8,96,768]{2,1,0:T(8,128)}, f32[8,768,96]{1,2,0:T(8,128)}, /*index=5*/f32[...) while((s32[]{:T(128)}, f32[96,576]{1,0:T(8,128)}, ...), condition=%wide.region_40.41_spmd.clone, body=%wide.region_0.40_spmd.clone.sunk | while | flops 53241786368 | bytes 1286897024 | solution.py:353
  86.9 71.7 %while.92 = (s32[]{:T(128)}, bf16[4,512,3,64]{1,3,2,0:T(8,128)(2,1)}, f32[4,3,512]{2,1,0:T(4,128)}, s32[4]{0:T(128)S(1)}, bf16[3072,3,64]{0,2,1:T(8,128)(2,1)}, ...) while((s32[]{:T(128)}, ...), condition=%wide.region_7.7_spmd, body=%wide.region_4.6_spmd.sunk | while | flops 637108736 | bytes 37845332 | solution.py:104
  167.5 36.8 reduce-scatter.18.cloned.1.call-done
  346.6 58.5 %all-gather.17.cloned.1.call-done = bf16[8,768,768]{2,1,0:T(8,128)(2,1)} async-done(((bf16[8,96,768]{2,1,0:T(8,128)(2,1)}), bf16[8,768,768]{2,1,0:T(8,128)(2,1)}) %all-gather.17.cloned.1.call-update) | async-done | bytes 9437200 | tf_op jit(solution)/shard_map/while/body/eval_jaxpr/all_gather | solution.py:185
  421.4 122.2 %all-gather.13.cloned.1.call-done = bf16[8,768,768]{1,2,0:T(8,128)(2,1)} async-done(((bf16[8,768,96]{1,2,0:T(8,128)(2,1)}), bf16[8,768,768]{1,2,0:T(8,128)(2,1)}) %all-gather.13.cloned.1.call-update) | async-done | bytes 9437200 | tf_op jit(solution)/shard_map/while/body/eval_jaxpr/all_gather | solution.py:246
  750.0 36.0 reduce_sum.320
  864.1 242.3 %while.93 = (s32[]{:T(128)}, f32[3072,3,64]{0,2,1:T(8,128)}, f32[3072,3,64]{0,2,1:T(8,128)}, bf16[4,512,3,64]{1,3,2,0:T(8,128)(2,1)}, s32[4]{0:T(128)S(1)}, /*in...) while((s32[]{:T(128)}, f32[3072,3,64]{0,2,1:T(8,128)}, ...), condition=%wide.region_29.29_spmd, body=%wide.region_27.28_spmd.sunk | while | flops 1536885248 | bytes 91103664 | solution.py:140
  1176.6 68.8 %reduce-scatter.24.cloned.1.call-done = f32[96,576]{1,0:T(8,128)} async-done(((f32[768,576]{1,0:T(8,128)}), f32[96,576]{1,0:T(8,128)}) %reduce-scatter.24.cloned.1.call-update) | async-done | bytes 221200 | tf_op jit(solution)/shard_map/while/body/eval_jaxpr/reduce_scatter | solution.py:339
  1246.4 38.4 reduce-scatter.32.cloned.1.call-done
  1287.4 38.0 reduce-scatter.34.cloned.1.call-done
  1329.7 313.3 %reduce-scatter.28.cloned.1.call-done = f32[8,96,768]{2,1,0:T(8,128)} async-done(((f32[8,768,768]{2,1,0:T(8,128)}), f32[8,96,768]{2,1,0:T(8,128)}) %reduce-scatter.28.cloned.1.call-update) | async-done | bytes 2359312 | tf_op jit(solution)/shard_map/while/body/eval_jaxpr/reduce_scatter | solution.py:341
  1646.4 313.2 %reduce-scatter.30.cloned.1.call-done = f32[8,768,96]{1,2,0:T(8,128)} async-done(((f32[8,768,768]{1,2,0:T(8,128)}), f32[8,768,96]{1,2,0:T(8,128)}) %reduce-scatter.30.cloned.1.call-update) | async-done | bytes 2359312 | tf_op jit(solution)/shard_map/while/body/eval_jaxpr/reduce_scatter | solution.py:342
  2039.3 71.7 %while.92 = (s32[]{:T(128)}, bf16[4,512,3,64]{1,3,2,0:T(8,128)(2,1)}, f32[4,3,512]{2,1,0:T(4,128)}, s32[4]{0:T(128)S(1)}, bf16[3072,3,64]{0,2,1:T(8,128)(2,1)}, ...) while((s32[]{:T(128)}, ...), condition=%wide.region_7.7_spmd, body=%wide.region_4.6_spmd.sunk | while | flops 637108736 | bytes 37845332 | solution.py:104
  2295.5 59.0 %all-gather.17.cloned.1.call-done = bf16[8,768,768]{2,1,0:T(8,128)(2,1)} async-done(((bf16[8,96,768]{2,1,0:T(8,128)(2,1)}), bf16[8,768,768]{2,1,0:T(8,128)(2,1)}) %all-gather.17.cloned.1.call-update) | async-done | bytes 9437200 | tf_op jit(solution)/shard_map/while/body/eval_jaxpr/all_gather | solution.py:185
  2371.0 122.4 %all-gather.13.cloned.1.call-done = bf16[8,768,768]{1,2,0:T(8,128)(2,1)} async-done(((bf16[8,768,96]{1,2,0:T(8,128)(2,1)}), bf16[8,768,768]{1,2,0:T(8,128)(2,1)}) %all-gather.13.cloned.1.call-update) | async-done | bytes 9437200 | tf_op jit(solution)/shard_map/while/body/eval_jaxpr/all_gather | solution.py:246
  2699.9 35.9 reduce_sum.320
  2737.2 34.9 reduce-scatter.22.cloned.1.call-done
  2813.9 242.1 %while.93 = (s32[]{:T(128)}, f32[3072,3,64]{0,2,1:T(8,128)}, f32[3072,3,64]{0,2,1:T(8,128)}, bf16[4,512,3,64]{1,3,2,0:T(8,128)(2,1)}, s32[4]{0:T(128)S(1)}, /*in...) while((s32[]{:T(128)}, f32[3072,3,64]{0,2,1:T(8,128)}, ...), condition=%wide.region_29.29_spmd, body=%wide.region_27.28_spmd.sunk | while | flops 1536885248 | bytes 91103664 | solution.py:140
  3126.3 68.3 %reduce-scatter.24.cloned.1.call-done = f32[96,576]{1,0:T(8,128)} async-done(((f32[768,576]{1,0:T(8,128)}), f32[96,576]{1,0:T(8,128)}) %reduce-scatter.24.cloned.1.call-update) | async-done | bytes 221200 | tf_op jit(solution)/shard_map/while/body/eval_jaxpr/reduce_scatter | solution.py:339
  3195.6 38.4 reduce-scatter.32.cloned.1.call-done
  3237.3 37.3 reduce-scatter.34.cloned.1.call-done
  3278.9 313.4 %reduce-scatter.28.cloned.1.call-done = f32[8,96,768]{2,1,0:T(8,128)} async-done(((f32[8,768,768]{2,1,0:T(8,128)}), f32[8,96,768]{2,1,0:T(8,128)}) %reduce-scatter.28.cloned.1.call-update) | async-done | bytes 2359312 | tf_op jit(solution)/shard_map/while/body/eval_jaxpr/reduce_scatter | solution.py:341
  3596.5 312.5 %reduce-scatter.30.cloned.1.call-done = f32[8,768,96]{1,2,0:T(8,128)} async-done(((f32[8,768,768]{1,2,0:T(8,128)}), f32[8,768,96]{1,2,0:T(8,128)}) %reduce-scatter.30.cloned.1.call-update) | async-done | bytes 2359312 | tf_op jit(solution)/shard_map/while/body/eval_jaxpr/reduce_scatter | solution.py:342
  3914.4 40.6 %all-reduce.7 = (f32[768]{0:T(1024)}, f32[768]{0:T(1024)}, f32[768,8]{0,1:T(8,128)}) all-reduce(f32[768]{0:T(1024)} %get-tuple-element.696, f32[768]{0:T(1024)} %get-tuple-element.697, f32[768,8]{0,1:T(8,128)} %get-tuple-element.700), channel_id=1, replica_groups=mesh['fsdp'=8,'tp'=4] {'fsdp','tp'}, use_global_device_ids=true, to_apply=%region_41.42 | all-reduce | flops 7680 | bytes 61440 | tf_op jit(solution)/shard_map/psum | solution.py:357
  (821 shorter events, 1770.8 us)
Async XLA Ops:
  15.0 189.4 %reduce-scatter.18.cloned.1.call-start = ((), (), s32[]{:S(2)}) async-start(), calls=%async_computation.10 | async-start | bytes 3932160 | tf_op jit(solution)/shard_map/while/body/eval_jaxpr/reduce_scatter | solution.py:199
  167.2 151.1 %all-gather.15.cloned.1.call-start = ((), (), s32[]{:S(2)}) async-start(), calls=%async_computation.12 | async-start | bytes 3932160 | tf_op jit(solution)/shard_map/while/body/eval_jaxpr/all_gather | solution.py:216
  208.3 196.8 %all-gather.17.cloned.1.call-start = ((), (), s32[]{:S(2)}) async-start(), calls=%async_computation.13 | async-start | bytes 10616832 | tf_op jit(solution)/shard_map/while/body/eval_jaxpr/all_gather | solution.py:185
  208.8 334.8 %all-gather.13.cloned.1.call-start = ((), (), s32[]{:S(2)}) async-start(), calls=%async_computation.11 | async-start | bytes 10616832 | tf_op jit(solution)/shard_map/while/body/eval_jaxpr/all_gather | solution.py:246
  209.4 576.7 %reduce-scatter.20.cloned.1.call-start = ((), (), s32[]{:S(2)}) async-start(), calls=%async_computation.15 | async-start | bytes 655360 | tf_op jit(solution)/shard_map/while
  649.1 173.2 %reduce-scatter.22.cloned.1.call-start = ((), (), s32[]{:S(2)}) async-start(), calls=%async_computation.16 | async-start | bytes 3932160 | tf_op jit(solution)/shard_map/while/body/eval_jaxpr/reduce_scatter | solution.py:275
  828.8 346.8 %reduce-scatter.26.cloned.1.call-start = ((), (), s32[]{:S(2)}) async-start(), calls=%async_computation.19 | async-start | bytes 884736 | tf_op jit(solution)/shard_map/while
  1112.9 132.5 %reduce-scatter.24.cloned.1.call-start = ((), (), s32[]{:S(2)}) async-start(), calls=%async_computation.18 | async-start | bytes 2211840 | tf_op jit(solution)/shard_map/while/body/eval_jaxpr/reduce_scatter | solution.py:339
  1121.4 163.5 %reduce-scatter.32.cloned.1.call-start = ((), (), s32[]{:S(2)}) async-start(), calls=%async_computation.22 | async-start | bytes 3932160 | tf_op jit(solution)/shard_map/while/body/eval_jaxpr/reduce_scatter | solution.py:327
  1125.7 199.7 %reduce-scatter.34.cloned.1.call-start = ((), (), s32[]{:S(2)}) async-start(), calls=%async_computation.23 | async-start | bytes 3932160 | tf_op jit(solution)/shard_map/while/body/eval_jaxpr/reduce_scatter | solution.py:238
  1126.4 516.5 %reduce-scatter.28.cloned.1.call-start = ((), (), s32[]{:S(2)}) async-start(), calls=%async_computation.20 | async-start | bytes 21233664 | tf_op jit(solution)/shard_map/while/body/eval_jaxpr/reduce_scatter | solution.py:341
  1143.0 816.7 %reduce-scatter.30.cloned.1.call-start = ((), (), s32[]{:S(2)}) async-start(), calls=%async_computation.21 | async-start | bytes 21233664 | tf_op jit(solution)/shard_map/while/body/eval_jaxpr/reduce_scatter | solution.py:342
  1968.8 185.0 %reduce-scatter.18.cloned.1.call-start = ((), (), s32[]{:S(2)}) async-start(), calls=%async_computation.10 | async-start | bytes 3932160 | tf_op jit(solution)/shard_map/while/body/eval_jaxpr/reduce_scatter | solution.py:199
  2119.6 147.6 %all-gather.15.cloned.1.call-start = ((), (), s32[]{:S(2)}) async-start(), calls=%async_computation.12 | async-start | bytes 3932160 | tf_op jit(solution)/shard_map/while/body/eval_jaxpr/all_gather | solution.py:216
  2157.7 196.9 %all-gather.17.cloned.1.call-start = ((), (), s32[]{:S(2)}) async-start(), calls=%async_computation.13 | async-start | bytes 10616832 | tf_op jit(solution)/shard_map/while/body/eval_jaxpr/all_gather | solution.py:185
  2158.3 335.0 %all-gather.13.cloned.1.call-start = ((), (), s32[]{:S(2)}) async-start(), calls=%async_computation.11 | async-start | bytes 10616832 | tf_op jit(solution)/shard_map/while/body/eval_jaxpr/all_gather | solution.py:246
  2159.0 576.9 %reduce-scatter.20.cloned.1.call-start = ((), (), s32[]{:S(2)}) async-start(), calls=%async_computation.15 | async-start | bytes 655360 | tf_op jit(solution)/shard_map/while
  2598.8 173.4 %reduce-scatter.22.cloned.1.call-start = ((), (), s32[]{:S(2)}) async-start(), calls=%async_computation.16 | async-start | bytes 3932160 | tf_op jit(solution)/shard_map/while/body/eval_jaxpr/reduce_scatter | solution.py:275
  2778.7 346.6 %reduce-scatter.26.cloned.1.call-start = ((), (), s32[]{:S(2)}) async-start(), calls=%async_computation.19 | async-start | bytes 884736 | tf_op jit(solution)/shard_map/while
  3062.6 132.0 %reduce-scatter.24.cloned.1.call-start = ((), (), s32[]{:S(2)}) async-start(), calls=%async_computation.18 | async-start | bytes 2211840 | tf_op jit(solution)/shard_map/while/body/eval_jaxpr/reduce_scatter | solution.py:339
  3071.1 162.9 %reduce-scatter.32.cloned.1.call-start = ((), (), s32[]{:S(2)}) async-start(), calls=%async_computation.22 | async-start | bytes 3932160 | tf_op jit(solution)/shard_map/while/body/eval_jaxpr/reduce_scatter | solution.py:327
  3075.4 199.2 %reduce-scatter.34.cloned.1.call-start = ((), (), s32[]{:S(2)}) async-start(), calls=%async_computation.23 | async-start | bytes 3932160 | tf_op jit(solution)/shard_map/while/body/eval_jaxpr/reduce_scatter | solution.py:238
  3076.2 516.1 %reduce-scatter.28.cloned.1.call-start = ((), (), s32[]{:S(2)}) async-start(), calls=%async_computation.20 | async-start | bytes 21233664 | tf_op jit(solution)/shard_map/while/body/eval_jaxpr/reduce_scatter | solution.py:341
  3092.8 816.2 %reduce-scatter.30.cloned.1.call-start = ((), (), s32[]{:S(2)}) async-start(), calls=%async_computation.21 | async-start | bytes 21233664 | tf_op jit(solution)/shard_map/while/body/eval_jaxpr/reduce_scatter | solution.py:342
  (162 other events, 6506.3 us)
Sparse Core Ops, SparseCore 0:
  15.1 31.2 all-gather.10
  164.8 39.4 reduce-scatter.17
  267.0 138.0 all-gather.16
  407.3 136.2 all-gather.12
  786.2 36.0 reduce-scatter.21
  828.9 28.5 all-gather.20
  1113.0 62.5 reduce-scatter.25
  1179.5 65.8 reduce-scatter.23
  1247.9 36.8 reduce-scatter.31
  1287.4 37.9 reduce-scatter.33
  1329.6 313.3 reduce-scatter.27
  1647.2 312.4 reduce-scatter.29
  2117.3 36.4 reduce-scatter.17
  2155.3 28.5 all-gather.18
  2185.6 28.5 all-gather.14
  2216.5 138.0 all-gather.16
  2357.0 136.2 all-gather.12
  2736.0 36.0 reduce-scatter.21
  3062.7 62.4 reduce-scatter.25
  3129.0 65.5 reduce-scatter.23
  3197.2 36.8 reduce-scatter.31
  3236.6 37.9 reduce-scatter.33
  3279.0 313.2 reduce-scatter.27
  3596.5 312.4 reduce-scatter.29
  (6 shorter events, 152.6 us)
where the time goes:
time: 3970 us; the launch traced here: 3960 us
  waiting for transfers between devices  2120 us (53%)
  local copies, waits for them, and re-layouts  660 us (17%)
  matrix products  566 us (14%)
  other arithmetic  329 us (8%)
  blocking collectives  181 us (5%)
  loops' own time  89 us (2%)
    reduce_scatter x2, waiting for transfers between devices, micro_step(): lax.psum_scatter(local_grads[2], 'fsdp', scatter_dimension=1, tiled=True)  627 us
    reduce_scatter x2, waiting for transfers between devices, micro_step(): lax.psum_scatter(local_grads[3], 'fsdp', scatter_dimension=2, tiled=True)  626 us
    all_gather x2, waiting for transfers between devices, micro_step(): lax.all_gather(w_out, 'fsdp', axis=2, tiled=True)  245 us
    reduce_scatter x2, waiting for transfers between devices, micro_step(): lax.psum_scatter(local_grads[0], 'fsdp', scatter_dimension=0, tiled=True)  137 us
    all_gather x2, waiting for transfers between devices, micro_step(): lax.all_gather(w_in, 'fsdp', axis=1, tiled=True)  118 us
    gather x4, local copies, waits for them, and re-layouts, micro_step(): cot_pad[token_of_slot]  105 us
    dot_general x16, matrix products, block_scores(): jnp.einsum('qhd,khd->hqk', q_blk, k_blk, preferred_element_type=jnp.float32)  85.5 us
    gather x4, local copies, waits for them, and re-layouts, micro_step(): picked = out_pad[slot]  83.7 us
  transfers between devices with their start and end apart: 30, of which 24 were waited for; matrix products, arithmetic and copies ran while one was open for 18% of the time, Pallas kernels for 0%

commit v1 on v0

v1 whole, which is shorter than its diff:
```python
import math

import jax
import jax.numpy as jnp
from jax import lax
from jax.experimental import pallas as pl
from jax.experimental.pallas import tpu as pltpu
from jax.sharding import PartitionSpec as P

HEAD_DIM = 64
WINDOW = 1024
CAP = 768
ROW_TILE = 16
QB = 256
CHUNK = 256
EPS = 1e-06
NEG = -1e30
F32 = jnp.float32
BF16 = jnp.bfloat16
I32 = jnp.int32
VMEM_LIMIT = 56 * 1024 * 1024
GELU_A = math.sqrt(2.0 / math.pi)
GELU_B = 0.044715
SIZES = (512, 256, 128, 64, 32, 16)


def dot_nn(a, b):
    return lax.dot_general(a, b, (((1,), (0,)), ((), ())), preferred_element_type=F32)


def dot_nt(a, b):
    return lax.dot_general(a, b, (((1,), (1,)), ((), ())), preferred_element_type=F32)


def dot_tn(a, b):
    return lax.dot_general(a, b, (((0,), (0,)), ((), ())), preferred_element_type=F32)


def params(*semantics):
    return pltpu.CompilerParams(dimension_semantics=semantics, vmem_limit_bytes=VMEM_LIMIT)


def whole(shape):
    zeros = (0,) * len(shape)
    return pl.BlockSpec(shape, lambda *_: zeros)


def attn_fwd_kernel(heads, me_ref, x0, x1, x2, x3, w_ref, lo_ref, proj_ref, mixed_ref, lse_ref,
                    send_ref, keep_ref, x_s, k_s, vt_s, q_s):
    me = me_ref[0]
    step = pl.program_id(0)
    part = x0.shape[0]
    seq = x_s.shape[0]
    nq = seq // QB
    per = part // QB

    @pl.when(step == 0)
    def _():
        for s, ref in enumerate((x0, x1, x2, x3)):
            x_s[pl.ds(pl.multiple_of((me ^ s) * part, part), part), :] = ref[...]

    @pl.when(step < nq)
    def _():
        rows = pl.ds(pl.multiple_of(step * QB, QB), QB)
        proj = dot_nn(x_s[rows, :], w_ref[:, : heads * 3 * HEAD_DIM]).astype(BF16)
        proj_ref[...] = proj
        for h in range(heads):
            base = h * 3 * HEAD_DIM
            q_s[h, rows, :] = proj[:, base : base + HEAD_DIM] * 0.125
            k_s[h, rows, :] = proj[:, base + HEAD_DIM : base + 2 * HEAD_DIM]
            vt_s[h, :, rows] = proj[:, base + 2 * HEAD_DIM : base + 3 * HEAD_DIM].T

    at = step - nq
    turn = at // per
    slot = jnp.where(turn == 0, 1, jnp.where(turn == 1, 3, jnp.where(turn == 2, 0, 2)))
    blk = (me ^ slot) * per + at % per

    def attend(nk):
        start = pl.multiple_of((blk - (nk - 1)) * QB, QB)
        rows = pl.ds(pl.multiple_of(blk * QB, QB), QB)
        keys = pl.ds(start, nk * QB)
        lo = lo_ref[:, rows]
        kpos = start + lax.broadcasted_iota(I32, (nk * QB, QB), 0)
        qpos = blk * QB + lax.broadcasted_iota(I32, (QB, QB), 1)
        outs = []
        for h in range(heads):
            s = dot_nt(k_s[h, keys, :], q_s[h, rows, :])
            s = jnp.where(kpos >= lo, s, NEG)
            last = jnp.where(kpos[(nk - 1) * QB :] <= qpos, s[(nk - 1) * QB :], NEG)
            s = last if nk == 1 else jnp.concatenate([s[: (nk - 1) * QB], last], axis=0)
            top = jnp.max(s, axis=0, keepdims=True)
            p = jnp.exp(s - top)
            total = jnp.sum(p, axis=0, keepdims=True)
            o = dot_nn(vt_s[h, :, keys], p.astype(BF16)) / total
            outs.append(o)
            lse_ref[h : h + 1, rows] = top + jnp.log(total)
        mixed_t = jnp.concatenate(outs, axis=0).astype(BF16)
        mixed_ref[:, rows] = mixed_t
        attn = dot_nt(mixed_t.T, w_ref[:, heads * 3 * HEAD_DIM :]).astype(BF16)

        @pl.when(at < nq // 2)
        def _():
            send_ref[...] = attn

        @pl.when(at >= nq // 2)
        def _():
            keep_ref[...] = attn

    most = WINDOW // QB + 1
    for nk in range(1, most + 1):
        cond = (blk == nk - 1) if nk < most else (blk >= most - 1)

        @pl.when((step >= nq) & cond)
        def _(nk=nk):
            attend(nk)


def attn_fwd(me, xs, w_cat, lo):
    part, width = xs[0].shape
    seq = part * 4
    heads = w_cat.shape[1] // (4 * HEAD_DIM)
    cols = heads * 3 * HEAD_DIM
    nq = seq // QB
    half = nq // 2
    spec = pltpu.PrefetchScalarGridSpec(
        num_scalar_prefetch=1,
        grid=(2 * nq,),
        in_specs=[whole((part, width))] * 4 + [
            whole(w_cat.shape), whole(lo.shape),
        ],
        out_specs=[
            pl.BlockSpec((QB, cols), lambda i, me: (jnp.minimum(i, nq - 1), 0)),
            whole((heads * HEAD_DIM, seq)),
            whole((8, seq)),
            pl.BlockSpec((QB, width), lambda i, me: (jnp.clip(i - nq, 0, half - 1), 0)),
            pl.BlockSpec((QB, width), lambda i, me: (jnp.clip(i - nq - half, 0, half - 1), 0)),
        ],
        scratch_shapes=[
            pltpu.VMEM((seq, width), BF16),
            pltpu.VMEM((heads, seq, HEAD_DIM), BF16),
            pltpu.VMEM((heads, HEAD_DIM, seq), BF16),
            pltpu.VMEM((heads, seq, HEAD_DIM), BF16),
        ],
    )
    return pl.pallas_call(
        lambda *refs: attn_fwd_kernel(heads, *refs),
        grid_spec=spec,
        out_shape=[
            jax.ShapeDtypeStruct((seq, cols), BF16),
            jax.ShapeDtypeStruct((heads * HEAD_DIM, seq), BF16),
            jax.ShapeDtypeStruct((8, seq), F32),
            jax.ShapeDtypeStruct((seq // 2, width), BF16),
            jax.ShapeDtypeStruct((seq // 2, width), BF16),
        ],
        compiler_params=params("arbitrary"),
        cost_estimate=pl.CostEstimate(flops=12_000_000_000, bytes_accessed=16_000_000, transcendentals=0),
        name="attn_fwd",
    )(me, *xs, w_cat, lo)


def attn_bwd_kernel(heads, me_ref, g0, g1, g2, g3, x0, x1, x2, x3, w_ref, lo_ref, proj_ref,
                    mixed_ref, lse_ref, dw_ref, send_ref, keep_ref, g_s, x_s, k_s, kt_s, v_s, dk_s, dv_s, dq_s,
                    dwo_s):
    me = me_ref[0]
    step = pl.program_id(0)
    part = x0.shape[0]
    seq = x_s.shape[0]
    nq = seq // QB
    per = part // QB
    cols = heads * 3 * HEAD_DIM

    @pl.when(step == 0)
    def _():
        for s, ref in enumerate((g0, g1, g2, g3)):
            g_s[pl.ds(pl.multiple_of((me ^ s) * part, part), part), :] = ref[...]
        for s, ref in enumerate((x0, x1, x2, x3)):
            x_s[pl.ds(pl.multiple_of((me ^ s) * part, part), part), :] = ref[...]
        dk_s[...] = jnp.zeros_like(dk_s)
        dv_s[...] = jnp.zeros_like(dv_s)
        dwo_s[...] = jnp.zeros_like(dwo_s)
        dw_ref[...] = jnp.zeros_like(dw_ref)

    def attend(nk):
        start = pl.multiple_of((step - (nk - 1)) * QB, QB)
        rows = pl.ds(pl.multiple_of(step * QB, QB), QB)
        keys = pl.ds(start, nk * QB)
        g = g_s[rows, :]
        gm_t = dot_nn(g, w_ref[:, cols:]).astype(BF16).T
        mixed_t = mixed_ref[:, rows]
        dwo_s[...] += dot_nn(mixed_t, g)
        prod = gm_t.astype(F32) * mixed_t.astype(F32)
        lo = lo_ref[:, rows]
        kpos = start + lax.broadcasted_iota(I32, (nk * QB, QB), 0)
        qpos = step * QB + lax.broadcasted_iota(I32, (QB, QB), 1)
        proj = proj_ref[...]
        for h in range(heads):
            base = h * 3 * HEAD_DIM
            here = slice(h * HEAD_DIM, (h + 1) * HEAD_DIM)
            q = proj[:, base : base + HEAD_DIM] * 0.125
            k_new = proj[:, base + HEAD_DIM : base + 2 * HEAD_DIM]
            k_s[h, rows, :] = k_new
            kt_s[h, :, rows] = k_new.T
            v_s[h, rows, :] = proj[:, base + 2 * HEAD_DIM : base + 3 * HEAD_DIM]
            drow = jnp.sum(prod[here], axis=0, keepdims=True)
            s = dot_nt(k_s[h, keys, :], q)
            s = jnp.where(kpos >= lo, s, NEG)
            last = jnp.where(kpos[(nk - 1) * QB :] <= qpos, s[(nk - 1) * QB :], NEG)
            s = last if nk == 1 else jnp.concatenate([s[: (nk - 1) * QB], last], axis=0)
            p = jnp.exp(s - lse_ref[h : h + 1, rows])
            dp = dot_nn(v_s[h, keys, :], gm_t[here])
            ds = (p * (dp - drow)).astype(BF16)
            dv_s[h, keys, :] += dot_nt(p.astype(BF16), gm_t[here])
            dk_s[h, keys, :] += dot_nn(ds, q)
            dq = dot_nn(kt_s[h, :, keys], ds) * 0.125
            dq_s[h, rows, :] = dq.astype(BF16).T

    most = WINDOW // QB + 1
    for nk in range(1, most + 1):
        cond = (step == nk - 1) if nk < most else ((step >= most - 1) & (step < nq))

        @pl.when(cond)
        def _(nk=nk):
            attend(nk)

    @pl.when(step >= nq)
    def _():
        at = step - nq
        turn = at // per
        slot = jnp.where(turn == 0, 1, jnp.where(turn == 1, 3, jnp.where(turn == 2, 0, 2)))
        blk = (me ^ slot) * per + at % per
        rows = pl.ds(pl.multiple_of(blk * QB, QB), QB)
        pieces = []
        for h in range(heads):
            pieces += [dq_s[h, rows, :], dk_s[h, rows, :].astype(BF16), dv_s[h, rows, :].astype(BF16)]
        dproj = jnp.concatenate(pieces, axis=1)
        dw_ref[:, :cols] += dot_tn(x_s[rows, :], dproj)
        gn = dot_nt(dproj, w_ref[:, :cols]).astype(BF16)

        @pl.when(at < nq // 2)
        def _():
            send_ref[...] = gn

        @pl.when(at >= nq // 2)
        def _():
            keep_ref[...] = gn

        @pl.when(at == nq - 1)
        def _():
            dw_ref[:, cols:] = dwo_s[...].T


def attn_bwd(me, gs, xs, w_cat, lo, proj, mixed_t, lse):
    part, width = xs[0].shape
    seq = part * 4
    heads = w_cat.shape[1] // (4 * HEAD_DIM)
    cols = heads * 3 * HEAD_DIM
    hc = heads * HEAD_DIM
    nq = seq // QB
    half = nq // 2
    spec = pltpu.PrefetchScalarGridSpec(
        num_scalar_prefetch=1,
        grid=(2 * nq,),
        in_specs=[whole((part, width))] * 8 + [
            whole(w_cat.shape), whole(lo.shape),
            pl.BlockSpec((QB, cols), lambda i, me: (jnp.minimum(i, nq - 1), 0)),
            whole((hc, seq)),
            whole((8, seq)),
        ],
        out_specs=[
            whole((width, cols + hc)),
            pl.BlockSpec((QB, width), lambda i, me: (jnp.clip(i - nq, 0, half - 1), 0)),
            pl.BlockSpec((QB, width), lambda i, me: (jnp.clip(i - nq - half, 0, half - 1), 0)),
        ],
        scratch_shapes=[
            pltpu.VMEM((seq, width), BF16),
            pltpu.VMEM((seq, width), BF16),
            pltpu.VMEM((heads, seq, HEAD_DIM), BF16),
            pltpu.VMEM((heads, HEAD_DIM, seq), BF16),
            pltpu.VMEM((heads, seq, HEAD_DIM), BF16),
            pltpu.VMEM((heads, seq, HEAD_DIM), F32),
            pltpu.VMEM((heads, seq, HEAD_DIM), F32),
            pltpu.VMEM((heads, seq, HEAD_DIM), BF16),
            pltpu.VMEM((hc, width), F32),
        ],
    )
    return pl.pallas_call(
        lambda *refs: attn_bwd_kernel(heads, *refs),
        grid_spec=spec,
        out_shape=[
            jax.ShapeDtypeStruct((width, cols + hc), F32),
            jax.ShapeDtypeStruct((seq // 2, width), BF16),
            jax.ShapeDtypeStruct((seq // 2, width), BF16),
        ],
        compiler_params=params("arbitrary"),
        cost_estimate=pl.CostEstimate(flops=40_000_000_000, bytes_accessed=20_000_000, transcendentals=0),
        name="attn_bwd",
    )(me, *gs, *xs, w_cat, lo, proj, mixed_t, lse)


def run_copies(n, src, src_at, dst, dst_at, sems, act):
    for i, size in enumerate(SIZES):
        done = n // (2 * size) * (2 * size)

        @pl.when((n // size) % 2 == 1)
        def _(i=i, size=size, done=done):
            copy = pltpu.make_async_copy(
                src.at[pl.ds(pl.multiple_of(src_at + done, ROW_TILE), size), :],
                dst.at[pl.ds(pl.multiple_of(dst_at + done, ROW_TILE), size), :],
                sems.at[i],
            )
            if act == "start":
                copy.start()
            else:
                copy.wait()


def dispatch_kernel(experts, n_ref, lo_ref, off_ref, x0, x1, x2, x3, c0, c1, c2, c3, rt_ref, pos_ref, *refs):
    xs_ref, gs_ref, meta_ref, x_s, c_s, xl, gl, in_sems, sems = refs[-9:]
    step = pl.program_id(0)
    slot = step % 2
    rows = xl.shape[1]
    part = x_s.shape[1]

    def load(s):
        for t, (x, c) in enumerate(((x0, c0), (x1, c1), (x2, c2), (x3, c3))):
            @pl.when(s == t)
            def _(x=x, c=c, t=t):
                pltpu.make_async_copy(x, x_s.at[t % 2], in_sems.at[t % 2, 0]).start()
                pltpu.make_async_copy(c, c_s.at[t % 2], in_sems.at[t % 2, 1]).start()

    def moves(at, slot, act):
        for e in range(experts):
            n, src, dst = n_ref[at, e], lo_ref[at, e], off_ref[at, e]
            run_copies(n, xl.at[slot], src, xs_ref.at[e], dst, sems.at[slot, 0, e], act)
            run_copies(n, gl.at[slot], src, gs_ref.at[e], dst, sems.at[slot, 1, e], act)

    @pl.when(step == 0)
    def _():
        load(0)

    @pl.when(step < 3)
    def _():
        load(step + 1)

    @pl.when(step >= 2)
    def _():
        moves(step - 2, slot, "wait")

    pltpu.make_async_copy(x0, x_s.at[slot], in_sems.at[slot, 0]).wait()
    pltpu.make_async_copy(c0, c_s.at[slot], in_sems.at[slot, 1]).wait()
    x = x_s[slot]
    logits = dot_nt(rt_ref[...], x)
    spots = pos_ref[0]
    p0, p1, r0, r1 = spots[0:1], spots[1:2], spots[2:3], spots[3:4]
    names = lax.broadcasted_iota(I32, logits.shape, 0)
    first = jnp.sum(jnp.where(names == r0, logits, 0.0), axis=0, keepdims=True)
    second = jnp.sum(jnp.where(names == r1, logits, 0.0), axis=0, keepdims=True)
    g0 = 1.0 / (1.0 + jnp.exp(second - first))
    g1 = 1.0 / (1.0 + jnp.exp(first - second))
    pick = lax.broadcasted_iota(I32, (8, part), 0)
    meta_ref[0] = jnp.where(
        pick == 0, p0.astype(F32), jnp.where(pick == 1, p1.astype(F32), jnp.where(pick == 2, g0, g1))
    )
    spot = lax.broadcasted_iota(I32, (rows, part), 0)
    is0 = spot == p0
    is1 = spot == p1
    plain = jnp.where(is0 | is1, 1.0, 0.0).astype(BF16)
    gated = jnp.where(is0, g0, jnp.where(is1, g1, 0.0)).astype(BF16)
    xl[slot] = dot_nn(plain, x).astype(BF16)
    gl[slot] = dot_nn(gated, c_s[slot]).astype(BF16)
    moves(step, slot, "start")

    @pl.when(step == 3)
    def _():
        moves(step - 1, 1 - slot, "wait")
        moves(step, slot, "wait")


def local_rows(part, experts):
    return -(-(2 * part + experts * (ROW_TILE - 1)) // 128) * 128


def dispatch(tables, xs, cs, router_t, spots, held, experts, most):
    part, width = xs[0].shape
    rows = local_rows(part, experts)
    anywhere = pl.BlockSpec(memory_space=pl.ANY)
    spec = pltpu.PrefetchScalarGridSpec(
        num_scalar_prefetch=3,
        grid=(4,),
        in_specs=[anywhere] * 8 + [
            whole(router_t.shape),
            pl.BlockSpec((1, 8, part), lambda i, *_: (i, 0, 0)),
        ] + [anywhere] * len(held),
        out_specs=[anywhere, anywhere, pl.BlockSpec((1, 8, part), lambda i, *_: (i, 0, 0))],
        scratch_shapes=[
            pltpu.VMEM((2, part, width), BF16),
            pltpu.VMEM((2, part, width), BF16),
            pltpu.VMEM((2, rows, width), BF16),
            pltpu.VMEM((2, rows, width), BF16),
            pltpu.SemaphoreType.DMA((2, 2)),
            pltpu.SemaphoreType.DMA((2, 2, experts, len(SIZES))),
        ],
    )
    return pl.pallas_call(
        lambda *refs: dispatch_kernel(experts, *refs),
        grid_spec=spec,
        out_shape=[
            jax.ShapeDtypeStruct((experts, most, width), BF16),
            jax.ShapeDtypeStruct((experts, most, width), BF16),
            jax.ShapeDtypeStruct((4, 8, part), F32),
        ],
        input_output_aliases={13: 0, 14: 1} if held else {},
        compiler_params=params("arbitrary"),
        cost_estimate=pl.CostEstimate(flops=10_000_000_000, bytes_accessed=20_000_000, transcendentals=0),
        name="dispatch",
    )(*tables, *xs, *cs, router_t, spots, *held)


def expert_kernel(first, tot_ref, xs_ref, gs_ref, w_ref, od_ref, dw_ref, din_s, dout_s):
    e = pl.program_id(0)
    c = pl.program_id(1)
    tot = tot_ref[first + e]
    width = xs_ref.shape[2]

    @pl.when(c == 0)
    def _():
        din_s[...] = jnp.zeros_like(din_s)
        dout_s[...] = jnp.zeros_like(dout_s)

    @pl.when(c * CHUNK < tot)
    def _():
        live = c * CHUNK + lax.broadcasted_iota(I32, (CHUNK, width), 0) < tot
        x = jnp.where(live, xs_ref[0], jnp.zeros((), BF16))
        g = jnp.where(live, gs_ref[0], jnp.zeros((), BF16))
        w_in = w_ref[0, 0]
        w_out_t = w_ref[0, 1]
        pre = dot_nn(x, w_in)
        dact = dot_nn(g, w_out_t)
        square = pre * pre
        t = jnp.tanh(GELU_A * pre * (1.0 + GELU_B * square))
        half = 0.5 * (1.0 + t)
        act = pre * half
        slope = half + (0.5 * GELU_A) * pre * (1.0 - t * t) * (1.0 + (3.0 * GELU_B) * square)
        act_low = act.astype(BF16)
        dpre = (slope * dact).astype(BF16)
        od_ref[0, :, :width] = dot_nt(act_low, w_out_t).astype(BF16)
        od_ref[0, :, width : 2 * width] = dot_nt(dpre, w_in).astype(BF16)
        dot_row = jnp.sum(act * dact, axis=1, keepdims=True)
        lane = lax.broadcasted_iota(I32, (CHUNK, 128), 1)
        od_ref[0, :, 2 * width :] = jnp.where(lane == first + e, dot_row, 0.0).astype(BF16)
        din_s[...] += dot_tn(x, dpre)
        dout_s[...] += dot_tn(g, act_low)

    @pl.when(c == pl.num_programs(1) - 1)
    def _():
        dw_ref[0, 0] = din_s[...].astype(BF16)
        dw_ref[0, 1] = dout_s[...].astype(BF16)


def run_experts(first, totals, xs, gs, weights):
    group, _, width, hidden = weights.shape
    most = xs.shape[1]
    chunks = most // CHUNK

    def rows_at(base):
        def index(e, c, tot):
            last = jnp.maximum((tot[first + e] + CHUNK - 1) // CHUNK - 1, 0)
            return (base + e, jnp.minimum(c, last), 0)

        return index

    spec = pltpu.PrefetchScalarGridSpec(
        num_scalar_prefetch=1,
        grid=(group, chunks),
        in_specs=[
            pl.BlockSpec((1, CHUNK, width), rows_at(first)),
            pl.BlockSpec((1, CHUNK, width), rows_at(first)),
            pl.BlockSpec((1, 2, width, hidden), lambda e, c, tot: (e, 0, 0, 0)),
        ],
        out_specs=[
            pl.BlockSpec((1, CHUNK, 2 * width + 128), rows_at(0)),
            pl.BlockSpec((1, 2, width, hidden), lambda e, c, tot: (e, 0, 0, 0)),
        ],
        scratch_shapes=[pltpu.VMEM((width, hidden), F32), pltpu.VMEM((width, hidden), F32)],
    )
    return pl.pallas_call(
        lambda *refs: expert_kernel(first, *refs),
        grid_spec=spec,
        out_shape=[
            jax.ShapeDtypeStruct((group, most, 2 * width + 128), BF16),
            jax.ShapeDtypeStruct((group, 2, width, hidden), BF16),
        ],
        compiler_params=params("arbitrary", "arbitrary"),
        cost_estimate=pl.CostEstimate(
            flops=group * 12 * 1024 * width * hidden, bytes_accessed=group * 20_000_000, transcendentals=0
        ),
        name="experts",
    )(totals, xs, gs, weights)


def combine_kernel(experts, groups, n_ref, lo_ref, off_ref, *refs):
    od_refs = refs[:groups]
    meta_ref, send_ref, keep_ref, od_l, sems = refs[groups:]
    step = pl.program_id(0)
    slot = step % 2
    rows = od_l.shape[1]
    each = experts // groups
    part = meta_ref.shape[2]
    width = (od_l.shape[2] - 128) // 2

    def moves(at, slot, act):
        for e in range(experts):
            n, dst, src = n_ref[at, e], lo_ref[at, e], off_ref[at, e]
            run_copies(n, od_refs[e // each].at[e % each], src, od_l.at[slot], dst, sems.at[slot, e], act)

    @pl.when(step == 0)
    def _():
        od_l[...] = jnp.zeros_like(od_l)
        moves(0, 0, "start")

    @pl.when(step < 3)
    def _():
        moves(step + 1, 1 - slot, "start")

    moves(step, slot, "wait")
    meta = meta_ref[0].T
    p0, p1, g0, g1 = (meta[:, i : i + 1] for i in range(4))
    spot = lax.broadcasted_iota(I32, (part, rows), 1).astype(F32)
    is0 = spot == p0
    is1 = spot == p1
    plain = jnp.where(is0 | is1, 1.0, 0.0).astype(BF16)
    gated = jnp.where(is0, g0, jnp.where(is1, g1, 0.0)).astype(BF16)
    out = dot_nn(gated, od_l[slot, :, :width]).astype(BF16)
    back = dot_nn(plain, od_l[slot, :, width:]).astype(BF16)

    @pl.when(step < 2)
    def _():
        send_ref[:, :width] = out
        send_ref[:, width:] = back

    @pl.when(step >= 2)
    def _():
        keep_ref[:, :width] = out
        keep_ref[:, width:] = back


def combine(tables, ods, meta):
    experts = sum(od.shape[0] for od in ods)
    groups = len(ods)
    wide = ods[0].shape[2]
    part = meta.shape[2]
    rows = local_rows(part, experts)
    anywhere = pl.BlockSpec(memory_space=pl.ANY)
    spec = pltpu.PrefetchScalarGridSpec(
        num_scalar_prefetch=3,
        grid=(4,),
        in_specs=[anywhere] * groups + [pl.BlockSpec((1, 8, part), lambda i, *_: (i, 0, 0))],
        out_specs=[
            pl.BlockSpec((part, wide), lambda i, *_: (jnp.minimum(i, 1), 0)),
            pl.BlockSpec((part, wide), lambda i, *_: (jnp.maximum(i - 2, 0), 0)),
        ],
        scratch_shapes=[
            pltpu.VMEM((2, rows, wide), BF16),
            pltpu.SemaphoreType.DMA((2, experts, len(SIZES))),
        ],
    )
    return pl.pallas_call(
        lambda *refs: combine_kernel(experts, groups, *refs),
        grid_spec=spec,
        out_shape=[jax.ShapeDtypeStruct((2 * part, wide), BF16)] * 2,
        compiler_params=params("arbitrary"),
        cost_estimate=pl.CostEstimate(flops=10_000_000_000, bytes_accessed=20_000_000, transcendentals=0),
        name="combine",
    )(*tables, *ods, meta)


def routing(routes, capacity, me, part):
    micro = routes.shape[0]
    experts = capacity.shape[0]
    picks = routes.reshape(micro, 4, part, 2).transpose(0, 1, 3, 2)
    names = jnp.arange(experts, dtype=I32)[:, None]
    named = picks[:, :, :, None, :] == names
    either = named[:, :, 0] | named[:, :, 1]
    earlier = jnp.arange(part)[:, None] < jnp.arange(part)[None, :]
    before = jnp.einsum("mbet,ts->mbes", either.astype(BF16), earlier.astype(BF16), preferred_element_type=F32)
    before = before.astype(I32)
    count = jnp.sum(either.astype(I32), axis=3)
    carry = jnp.cumsum(count, axis=1) - count
    kept = jnp.clip(capacity[None, None, :] - carry, 0, count)
    n = (kept + ROW_TILE - 1) // ROW_TILE * ROW_TILE
    lo = jnp.cumsum(n, axis=2) - n
    place = jnp.where(before < kept[..., None], lo[..., None] + before, -1)
    pos = jnp.max(jnp.where(named, place[:, :, None], -1), axis=3)
    order = me ^ jnp.array([1, 3, 0, 2], I32)
    spots = jnp.concatenate([pos, picks, jnp.zeros_like(pos), jnp.zeros_like(pos)], axis=2)
    spots = jnp.take(spots, order, axis=1)
    n = jnp.take(n, order, axis=1)
    lo = jnp.take(lo, order, axis=1)
    flat = n.reshape(micro * 4, experts)
    off = (jnp.cumsum(flat, axis=0) - flat).reshape(n.shape)
    return n, lo, off, jnp.sum(flat, axis=0), spots


def norm_scaled(values, gain):
    return values * lax.rsqrt(jnp.mean(values * values, axis=-1, keepdims=True) + EPS) * gain


def spread(rows):
    over = lax.ppermute(rows, "tp", [(i, i ^ 2) for i in range(4)])
    side = lax.ppermute(rows, "tp", [(i, i ^ 1) for i in range(4)])
    far = lax.ppermute(over, "tp", [(i, i ^ 1) for i in range(4)])
    return (side, far, rows, over)


def gather_sum(send, keep):
    part = keep.shape[0] // 2
    got = lax.ppermute(send, "tp", [(i, i ^ 1) for i in range(4)])
    both = keep.astype(F32) + got.astype(F32)
    away = lax.ppermute(both[part:].astype(BF16), "tp", [(i, i ^ 2) for i in range(4)])
    return both[:part] + away.astype(F32)


def local(tokens, cotangent, gain_attn, gain_moe, qkv_weight, out_weight, router, w_in, w_out, doc_lengths, routes,
          capacity):
    micro, part, width = tokens.shape
    seq = part * 4
    experts = w_in.shape[0]
    me = lax.axis_index("tp").astype(I32)
    me_arr = me.reshape(1)
    most = -(-micro * (CAP + 4 * ROW_TILE) // CHUNK) * CHUNK
    groups = 4
    each = experts // groups

    cat = jnp.concatenate([qkv_weight, out_weight.T], axis=1)
    w_cat = lax.all_gather(cat, "fsdp", axis=0, tiled=True)
    w_pair = jnp.stack([w_in, w_out.transpose(0, 2, 1)], axis=1)
    w_groups = [
        lax.all_gather(w_pair[g * each : (g + 1) * each], "fsdp", axis=2, tiled=True) for g in range(groups)
    ]

    n, lo_at, off, totals, spots = routing(routes, capacity, me, part)
    places = jnp.arange(seq, dtype=I32)
    ends = jnp.cumsum(doc_lengths.reshape(micro, -1), axis=1)
    begins = ends - doc_lengths.reshape(micro, -1)
    doc_start = jnp.max(jnp.where(places >= begins[:, :, None], begins[:, :, None], 0), axis=1)
    low = jnp.maximum(doc_start, places - (WINDOW - 1)).astype(I32)
    router_t = router.T
    router_float = router.astype(F32)

    x_float = [tokens[m].astype(F32) for m in range(micro)]
    normed_parts, cot_parts = [], []
    back_attn = []
    for m in range(micro):
        normed, back = jax.vjp(norm_scaled, x_float[m], gain_attn)
        back_attn.append(back)
        normed_parts.append(spread(normed.astype(BF16)))
    cot_parts = [spread(cotangent[m]) for m in range(micro)]

    fwd = []
    moe_rows, back_moe, hidden = [], [], []
    held = ()
    metas = []
    for m in range(micro):
        side, far, own, over = normed_parts[m]
        proj, mixed_t, lse, send, keep = attn_fwd(me_arr, (own, side, over, far), w_cat, low[m : m + 1])
        fwd.append((proj, mixed_t, lse))
        hid = x_float[m] + gather_sum(send, keep)
        hidden.append(hid)
        normed, back = jax.vjp(norm_scaled, hid, gain_moe)
        back_moe.append(back)
        moe_rows.append(normed.astype(BF16))
        xs, gs, meta = dispatch(
            (n[m], lo_at[m], off[m]), spread(moe_rows[m]), cot_parts[m], router_t, spots[m], held, experts, most
        )
        held = (xs, gs)
        metas.append(meta)

    ods, dws = [], []
    for g in range(groups):
        od, dw = run_experts(g * each, totals, xs, gs, w_groups[g])
        ods.append(od)
        dws.append(lax.psum_scatter(dw, "fsdp", scatter_dimension=2, tiled=True))

    outputs, grads_in = [], []
    grad_router = jnp.zeros(router.shape, F32)
    grad_gain_two = jnp.zeros(gain_moe.shape, F32)
    grad_gain_one = jnp.zeros(gain_attn.shape, F32)
    grad_cat = jnp.zeros((width, w_cat.shape[1]), F32)
    names = jnp.arange(experts, dtype=I32)
    for m in range(micro):
        send, keep = combine((n[m], lo_at[m], off[m]), ods, metas[m])
        summed = gather_sum(send, keep)
        outputs.append((hidden[m] + summed[:, :width]).astype(BF16))
        products = summed[:, 2 * width : 2 * width + experts]
        mine = lax.dynamic_slice_in_dim(routes[m], me * part, part, 0)
        gates = metas[m][2, 2:4].T
        full = jnp.sum(jnp.where(mine[:, :, None] == names, gates[:, :, None], 0.0), axis=1)
        grad_logits = products - full * jnp.sum(products, axis=1, keepdims=True)
        grad_router += jnp.einsum(
            "td,te->de", moe_rows[m].astype(F32), grad_logits, precision=lax.Precision.HIGHEST,
            preferred_element_type=F32,
        )
        grad_moe = summed[:, width : 2 * width] + jnp.einsum(
            "te,de->td", grad_logits, router_float, precision=lax.Precision.HIGHEST, preferred_element_type=F32
        )
        grad_norm, grad_gain = back_moe[m](grad_moe)
        grad_gain_two += grad_gain
        grad_hidden = cotangent[m].astype(F32) + grad_norm
        g_side, g_far, g_own, g_over = spread(grad_hidden.astype(BF16))
        side, far, own, over = normed_parts[m]
        proj, mixed_t, lse = fwd[m]
        dcat, send, keep = attn_bwd(
            me_arr, (g_own, g_side, g_over, g_far), (own, side, over, far), w_cat, low[m : m + 1], proj, mixed_t, lse
        )
        grad_cat += dcat
        grad_x, grad_gain = back_attn[m](gather_sum(send, keep))
        grad_gain_one += grad_gain
        grads_in.append((grad_hidden + grad_x).astype(BF16))

    grad_cat = lax.psum_scatter(grad_cat.astype(BF16), "fsdp", scatter_dimension=0, tiled=True).astype(F32)
    dw = jnp.concatenate(dws, axis=0).astype(F32)
    grad_router, grad_gain_one, grad_gain_two = lax.psum((grad_router, grad_gain_one, grad_gain_two), ("fsdp", "tp"))
    cols = qkv_weight.shape[1]
    return (
        jnp.stack(outputs),
        jnp.stack(grads_in),
        grad_gain_one,
        grad_gain_two,
        grad_cat[:, :cols],
        grad_cat[:, cols:].T,
        grad_router,
        dw[:, 0],
        dw[:, 1].transpose(0, 2, 1),
    )


def solution(mesh):
    rows = P(None, ("fsdp", "tp"), None)
    in_specs = (
        rows,
        rows,
        P(),
        P(),
        P("fsdp", "tp"),
        P("tp", "fsdp"),
        P(),
        P(None, "fsdp", "tp"),
        P(None, "tp", "fsdp"),
        P(None, "fsdp", None),
        P(None, "fsdp", None),
        P(),
    )
    out_specs = (
        rows,
        rows,
        P(),
        P(),
        P("fsdp", "tp"),
        P("tp", "fsdp"),
        P(),
        P(None, "fsdp", "tp"),
        P(None, "tp", "fsdp"),
    )
    return jax.shard_map(local, mesh=mesh, in_specs=in_specs, out_specs=out_specs, check_vma=False)
```

time: 3970 us -> 1140 us (0.29)
  waiting for transfers between devices: 2120 us -> 632 us
  local copies, waits for them, and re-layouts: 660 us -> 31.7 us
  matrix products: 566 us -> 9.27 us
  Pallas kernels: 0 us -> 326 us
  other arithmetic: 329 us -> 47.5 us
  blocking collectives: 181 us -> 43.4 us
  loops' own time: 89 us -> 0 us
    reduce_scatter x14 -> x5, waiting for transfers between devices: 1680 us -> 381 us  [the longest x4 334 us: local(): dws.append(lax.psum_scatter(dw, 'fsdp', scatter_dimension=2, tiled=True))]
    dot_general x84 -> x5, matrix products: 558 us -> 9.27 us  [the longest x2 6.07 us: local(): jnp.einsum('te,de->td', grad_logits, router_float, precision=lax.Precisio...]
    all_gather x12 -> x5, waiting for transfers between devices: 424 us -> 28.8 us  [the longest x4 27.4 us: local(): lax.all_gather(w_pair[g * each:(g + 1) * each], 'fsdp', axis=2, tiled=True)]
    pallas_call x0 -> x12, Pallas kernels: none -> 326 us  [the longest x4 112 us: run_experts(): pl.pallas_call(lambda *refs: expert_kernel(first, *refs), grid_spec=spec,...]
    gather x14 -> x3, local copies, waits for them, and re-layouts: 325 us -> 1.7 us  [the longest x1 0.57 us: routing(): n = jnp.take(n, order, axis=1)]
    ppermute x0 -> x36, waiting for transfers between devices: none -> 218 us  [the longest x6 119 us: gather_sum(): lax.ppermute(both[part:].astype(BF16), 'tp', [(i, i ^ 2) for i in range(4)])]
    reduce_sum x32 -> x9, other arithmetic: 169 us -> 8.35 us  [the longest x1 3.69 us: norm_scaled(): values * lax.rsqrt(jnp.mean(values * values, axis=-1, keepdims=True) + EPS)]
    all_gather x6 -> x0, blocking collectives: 140 us -> none  [the longest x2 65.2 us: micro_step(): lax.all_gather(qkv_weight, 'fsdp', axis=0, tiled=True)]
  transfers between devices with their start and end apart: 30 -> 46, of which waited for: 24 -> 19; matrix products, arithmetic and copies ran while one was open for 18% -> 5% of each run, Pallas kernels for 0% -> 21%
where the time goes in v1:
time: 1140 us; the launch traced here: 1130 us
  waiting for transfers between devices  632 us (55%)
  Pallas kernels  326 us (29%)
  other arithmetic  47.5 us (4%)
  blocking collectives  43.4 us (4%)
  local copies, waits for them, and re-layouts  31.7 us (3%)
  starting transfers between devices  20.5 us (2%)
  between operations  15.6 us (1%)
    reduce_scatter x4, waiting for transfers between devices, local(): dws.append(lax.psum_scatter(dw, 'fsdp', scatter_dimension=2, tiled=True))  334 us
    ppermute x6, waiting for transfers between devices, gather_sum(): lax.ppermute(both[part:].astype(BF16), 'tp', [(i, i ^ 2) for i in range(4)])  119 us
    pallas_call x4, Pallas kernels, run_experts(): pl.pallas_call(lambda *refs: expert_kernel(first, *refs), grid_spec=spec,...  112 us
    ppermute x8, waiting for transfers between devices, spread(): over = lax.ppermute(rows, 'tp', [(i, i ^ 2) for i in range(4)])  94.4 us
    pallas_call x2, Pallas kernels, attn_bwd(): pl.pallas_call(lambda *refs: attn_bwd_kernel(heads, *refs), grid_spec=spe...  72.6 us
    pallas_call x2, Pallas kernels, attn_fwd(): pl.pallas_call(lambda *refs: attn_fwd_kernel(heads, *refs), grid_spec=spe...  59.5 us
    reduce_scatter x1, waiting for transfers between devices, local(): lax.psum_scatter(grad_cat.astype(BF16), 'fsdp', scatter_dimension=0, tile...  47 us
    pallas_call x2, Pallas kernels, combine(): pl.pallas_call(lambda *refs: combine_kernel(experts, groups, *refs), grid...  43.7 us
  transfers between devices with their start and end apart: 46, of which 19 were waited for; matrix products, arithmetic and copies ran while one was open for 5% of the time, Pallas kernels for 21%

profile of v1, /device:TPU:0, one launch (start us, length us, event | category | flops | bytes accessed | tf_op | source)
XLA Modules:
  0.0 1125.7 jit_solution(6273977953408885184)
XLA Ops:
  19.7 17.6 %collective-permute-done.6.refs_3_.refs_7_ = bf16[512,768]{1,0:T(8,128)(2,1)} collective-permute-done((bf16[512,768]{1,0:T(8,128)(2,1)S(1)}, bf16[512,768]{1,0:T(8,128)(2,1)}, u32[]{:S(2)}, u32[]{:S(2)}) %collective-permute-start.6) | collective-permute-done | bytes 786464 | tf_op jit(solution)/shard_map/ppermute | solution.py:609
  54.7 29.5 %attn_fwd.3 = (bf16[2048,576]{1,0:T(8,128)(2,1)}, bf16[192,2048]{1,0:T(8,128)(2,1)}, f32[8,2048]{1,0:T(8,128)}, bf16[1024,768]{1,0:T(8,128)(2,1)}, bf16[1024,768]{1,0:T(8,128)(2,1)}) custom-call(s32[1]{0:T(128)} %bitcast.1.refs_0_, bf16[512,768]{1,0:T(8,128)(2,1)} %copy-done.33, bf16[512,768]{1,0:T(8,128)(2,1)} %collective-permute-done.5.refs_2_.refs_6_, ...), custom_call_target="tpu_custom_call" | custom-call | flops 12000000000 | bytes 16000000 | tf_op jit(solution)/shard_map/attn_fwd/pallas_call | solution.py:145
  84.3 30.0 %attn_fwd.2 = (bf16[2048,576]{1,0:T(8,128)(2,1)}, bf16[192,2048]{1,0:T(8,128)(2,1)}, f32[8,2048]{1,0:T(8,128)}, bf16[1024,768]{1,0:T(8,128)(2,1)}, bf16[1024,768]{1,0:T(8,128)(2,1)}) custom-call(s32[1]{0:T(128)} %bitcast.1.refs_0_, bf16[512,768]{1,0:T(8,128)(2,1)} %copy-done.32, bf16[512,768]{1,0:T(8,128)(2,1)} %collective-permute-done.refs_2_.refs_6_, ...), custom_call_target="tpu_custom_call" | custom-call | flops 12000000000 | bytes 16000000 | tf_op jit(solution)/shard_map/attn_fwd/pallas_call | solution.py:145
  131.6 38.9 %collective-permute-done.9 = bf16[512,768]{1,0:T(8,128)(2,1)} collective-permute-done((bf16[512,768]{1,0:T(8,128)(2,1)}, bf16[512,768]{1,0:T(8,128)(2,1)}, u32[]{:S(2)}, u32[]{:S(2)}) %collective-permute-start.9) | collective-permute-done | bytes 786464 | tf_op jit(solution)/shard_map/ppermute | solution.py:619
  226.3 18.8 %dispatch.2 = (bf16[8,1792,768]{2,1,0:T(8,128)(2,1)}, bf16[8,1792,768]{2,1,0:T(8,128)(2,1)}, f32[4,8,512]{2,1,0:T(8,128)}) custom-call(s32[4,8]{1,0:T(4,128)} %bitcast.118, s32[4,8]{1,0:T(4,128)} %bitcast.120, s32[4,8]{1,0:T(4,128)} %get-tuple-element.173.refs_2_, bf16[512,768]{1,0:T(8,128)(2,1)} %collective-permute-done.16.refs_3_, ...), custom_call_target="tpu_custom_call" | custom-call | flops 10000000000 | bytes 20000000 | tf_op jit(solution)/shard_map/dispatch/pallas_call | solution.py:404
  246.8 19.0 %dispatch.3 = (bf16[8,1792,768]{2,1,0:T(8,128)(2,1)}, bf16[8,1792,768]{2,1,0:T(8,128)(2,1)}, f32[4,8,512]{2,1,0:T(8,128)}) custom-call(s32[4,8]{1,0:T(4,128)} %bitcast.114, s32[4,8]{1,0:T(4,128)} %bitcast.116, s32[4,8]{1,0:T(4,128)} %get-tuple-element.174.refs_2_, bf16[512,768]{1,0:T(8,128)(2,1)} %copy-done.36, ...), custom_call_target="tpu_custom_call", output_to_operand_aliasing={{0}: (13, {}), {1}: (14, {})} | custom-call | flops 10000000000 | bytes 20000000 | tf_op jit(solution)/shard_map/dispatch/pallas_call | solution.py:404
  265.8 29.7 %experts.7 = (bf16[2,1792,1664]{2,1,0:T(8,128)(2,1)}, bf16[2,2,768,768]{3,2,1,0:T(8,128)(2,1)}) custom-call(s32[8]{0:T(128)} %get-tuple-element.142.refs_0_, bf16[8,1792,768]{2,1,0:T(8,128)(2,1)} %get-tuple-element.50.refs_1_, bf16[8,1792,768]{2,1,0:T(8,128)(2,1)} %get-tuple-element.51.refs_2_, bf16[2,2,768,768]{3,2,1,0:T(8,128)(2,1)} %all-gather.14.cloned.1.call-done.refs_3_), custom_call_target="tpu_custom_call" | custom-call | flops 14495514624 | bytes 40000000 | tf_op jit(solution)/shard_map/experts/pallas_call | solution.py:486
  295.5 27.5 %experts.6 = (bf16[2,1792,1664]{2,1,0:T(8,128)(2,1)}, bf16[2,2,768,768]{3,2,1,0:T(8,128)(2,1)}) custom-call(s32[8]{0:T(128)} %get-tuple-element.142.refs_0_, bf16[8,1792,768]{2,1,0:T(8,128)(2,1)} %get-tuple-element.50.refs_1_, bf16[8,1792,768]{2,1,0:T(8,128)(2,1)} %get-tuple-element.51.refs_2_, bf16[2,2,768,768]{3,2,1,0:T(8,128)(2,1)} %all-gather.12.cloned.1.call-done.refs_3_), custom_call_target="tpu_custom_call" | custom-call | flops 14495514624 | bytes 40000000 | tf_op jit(solution)/shard_map/experts/pallas_call | solution.py:486
  323.0 25.6 %experts.5 = (bf16[2,1792,1664]{2,1,0:T(8,128)(2,1)}, bf16[2,2,768,768]{3,2,1,0:T(8,128)(2,1)}) custom-call(s32[8]{0:T(128)} %get-tuple-element.142.refs_0_, bf16[8,1792,768]{2,1,0:T(8,128)(2,1)} %get-tuple-element.50.refs_1_, bf16[8,1792,768]{2,1,0:T(8,128)(2,1)} %get-tuple-element.51.refs_2_, bf16[2,2,768,768]{3,2,1,0:T(8,128)(2,1)} %all-gather.10.cloned.1.call-done.refs_3_), custom_call_target="tpu_custom_call" | custom-call | flops 14495514624 | bytes 40000000 | tf_op jit(solution)/shard_map/experts/pallas_call | solution.py:486
  348.6 27.4 %all-gather.8.cloned.1.call-done.refs_3_ = bf16[2,2,768,768]{3,2,1,0:T(8,128)(2,1)} async-done(((bf16[2,2,96,768]{3,2,1,0:T(8,128)(2,1)}), bf16[2,2,768,768]{3,2,1,0:T(8,128)(2,1)}) %all-gather.8.cloned.1.call-update) | async-done | bytes 4718608 | tf_op jit(solution)/shard_map/all_gather | solution.py:638
  376.0 29.6 %experts.4 = (bf16[2,1792,1664]{2,1,0:T(8,128)(2,1)}, bf16[2,2,768,768]{3,2,1,0:T(8,128)(2,1)}) custom-call(s32[8]{0:T(128)} %get-tuple-element.142.refs_0_, bf16[8,1792,768]{2,1,0:T(8,128)(2,1)} %get-tuple-element.50.refs_1_, bf16[8,1792,768]{2,1,0:T(8,128)(2,1)} %get-tuple-element.51.refs_2_, bf16[2,2,768,768]{3,2,1,0:T(8,128)(2,1)} %all-gather.8.cloned.1.call-done.refs_3_), custom_call_target="tpu_custom_call" | custom-call | flops 14495514624 | bytes 40000000 | tf_op jit(solution)/shard_map/experts/pallas_call | solution.py:486
  405.6 21.6 %combine.3 = (bf16[1024,1664]{1,0:T(8,128)(2,1)}, bf16[1024,1664]{1,0:T(8,128)(2,1)}) custom-call(s32[4,8]{1,0:T(4,128)} %bitcast.115, s32[4,8]{1,0:T(4,128)} %bitcast.117, s32[4,8]{1,0:T(4,128)} %get-tuple-element.174.refs_2_, bf16[2,1792,1664]{2,1,0:T(8,128)(2,1)} %get-tuple-element.52.refs_3_, bf16[2,1792,1664]{2,1,0:T(8,128)(2,1)} %get-tuple-element.53.refs_4_, ...), custom_call_target="tpu_custom_call" | custom-call | flops 10000000000 | bytes 20000000 | tf_op jit(solution)/shard_map/combine/pallas_call | solution.py:567
  427.3 22.1 %combine.2 = (bf16[1024,1664]{1,0:T(8,128)(2,1)}, bf16[1024,1664]{1,0:T(8,128)(2,1)}) custom-call(s32[4,8]{1,0:T(4,128)} %bitcast.119, s32[4,8]{1,0:T(4,128)} %bitcast.121, s32[4,8]{1,0:T(4,128)} %get-tuple-element.173.refs_2_, bf16[2,1792,1664]{2,1,0:T(8,128)(2,1)} %get-tuple-element.52.refs_3_, bf16[2,1792,1664]{2,1,0:T(8,128)(2,1)} %get-tuple-element.53.refs_4_, ...), custom_call_target="tpu_custom_call" | custom-call | flops 10000000000 | bytes 20000000 | tf_op jit(solution)/shard_map/combine/pallas_call | solution.py:567
  462.5 31.5 %collective-permute-done.25 = bf16[512,1664]{1,0:T(8,128)(2,1)S(1)} collective-permute-done((bf16[512,1664]{1,0:T(8,128)(2,1)S(1)}, bf16[512,1664]{1,0:T(8,128)(2,1)S(1)}, u32[]{:S(2)}, u32[]{:S(2)}) %collective-permute-start.25) | collective-permute-done | bytes 1703968 | tf_op jit(solution)/shard_map/ppermute | solution.py:619
  496.9 32.6 %collective-permute-done.23 = bf16[512,1664]{1,0:T(8,128)(2,1)S(1)} collective-permute-done((bf16[512,1664]{1,0:T(8,128)(2,1)}, bf16[512,1664]{1,0:T(8,128)(2,1)S(1)}, u32[]{:S(2)}, u32[]{:S(2)}) %collective-permute-start.23) | collective-permute-done | bytes 1703968 | tf_op jit(solution)/shard_map/ppermute | solution.py:619
  545.6 18.4 %collective-permute-done.32.refs_3_ = bf16[512,768]{1,0:T(8,128)(2,1)S(1)} collective-permute-done((bf16[512,768]{1,0:T(8,128)(2,1)S(1)}, bf16[512,768]{1,0:T(8,128)(2,1)S(1)}, u32[]{:S(2)}, u32[]{:S(2)}) %collective-permute-start.32) | collective-permute-done | bytes 786464 | tf_op jit(solution)/shard_map/ppermute | solution.py:609
  580.3 36.1 %attn_bwd.3 = (f32[768,768]{1,0:T(8,128)}, bf16[1024,768]{1,0:T(8,128)(2,1)}, bf16[1024,768]{1,0:T(8,128)(2,1)}) custom-call(s32[1]{0:T(128)} %bitcast.1.refs_0_, bf16[512,768]{1,0:T(8,128)(2,1)} %copy-done.31, bf16[512,768]{1,0:T(8,128)(2,1)} %copy-done.58, bf16[512,768]{1,0:T(8,128)(2,1)} %copy-done.57, bf16[512,768]{1,0:T(8,128)(2,1)} %copy-done.59, ...), custom_call_target="tpu_custom_call" | custom-call | flops 40000000000 | bytes 20000000 | tf_op jit(solution)/shard_map/attn_bwd/pallas_call | solution.py:286
  617.6 36.5 %attn_bwd.2 = (f32[768,768]{1,0:T(8,128)}, bf16[1024,768]{1,0:T(8,128)(2,1)}, bf16[1024,768]{1,0:T(8,128)(2,1)}) custom-call(s32[1]{0:T(128)} %bitcast.1.refs_0_, bf16[512,768]{1,0:T(8,128)(2,1)} %copy-done.30, bf16[512,768]{1,0:T(8,128)(2,1)} %copy-done.55, bf16[512,768]{1,0:T(8,128)(2,1)} %copy-done.54, bf16[512,768]{1,0:T(8,128)(2,1)} %copy-done.56, ...), custom_call_target="tpu_custom_call" | custom-call | flops 40000000000 | bytes 20000000 | tf_op jit(solution)/shard_map/attn_bwd/pallas_call | solution.py:286
  672.0 47.0 %reduce-scatter.6.cloned.1.call-done = bf16[96,768]{1,0:T(8,128)(2,1)} async-done(((bf16[768,768]{1,0:T(8,128)(2,1)}), bf16[96,768]{1,0:T(8,128)(2,1)}) %reduce-scatter.6.cloned.1.call-update) | async-done | bytes 147472 | tf_op jit(solution)/shard_map/reduce_scatter | solution.py:720
  726.1 43.4 %all-reduce = (f32[768]{0:T(1024)}, f32[768]{0:T(1024)}, f32[768,8]{0,1:T(8,128)}) all-reduce(f32[768]{0:T(1024)S(1)} %add.204, f32[768]{0:T(1024)S(1)} %add.205, f32[768,8]{0,1:T(8,128)S(1)} %convolution_add_fusion), channel_id=1, replica_groups=mesh['fsdp'=8,'tp'=4] {'fsdp','tp'}, use_global_device_ids=true, to_apply=%region_22.24 | all-reduce | flops 7680 | bytes 61440 | tf_op jit(solution)/shard_map/psum | solution.py:722
  779.6 38.5 %reduce-scatter.14.cloned.1.call-done = bf16[2,2,96,768]{3,2,1,0:T(8,128)(2,1)} async-done(((bf16[2,2,768,768]{3,2,1,0:T(8,128)(2,1)}), bf16[2,2,96,768]{3,2,1,0:T(8,128)(2,1)}) %reduce-scatter.14.cloned.1.call-update) | async-done | bytes 589840 | tf_op jit(solution)/shard_map/reduce_scatter | solution.py:682
  818.1 98.7 %reduce-scatter.12.cloned.1.call-done = bf16[2,2,96,768]{3,2,1,0:T(8,128)(2,1)} async-done(((bf16[2,2,768,768]{3,2,1,0:T(8,128)(2,1)}), bf16[2,2,96,768]{3,2,1,0:T(8,128)(2,1)}) %reduce-scatter.12.cloned.1.call-update) | async-done | bytes 589840 | tf_op jit(solution)/shard_map/reduce_scatter | solution.py:682
  916.8 98.7 %reduce-scatter.10.cloned.1.call-done = bf16[2,2,96,768]{3,2,1,0:T(8,128)(2,1)} async-done(((bf16[2,2,768,768]{3,2,1,0:T(8,128)(2,1)}), bf16[2,2,96,768]{3,2,1,0:T(8,128)(2,1)}) %reduce-scatter.10.cloned.1.call-update) | async-done | bytes 589840 | tf_op jit(solution)/shard_map/reduce_scatter | solution.py:682
  1015.5 98.5 %reduce-scatter.8.cloned.1.call-done = bf16[2,2,96,768]{3,2,1,0:T(8,128)(2,1)} async-done(((bf16[2,2,768,768]{3,2,1,0:T(8,128)(2,1)}), bf16[2,2,96,768]{3,2,1,0:T(8,128)(2,1)}) %reduce-scatter.8.cloned.1.call-update) | async-done | bytes 589840 | tf_op jit(solution)/shard_map/reduce_scatter | solution.py:682
  (307 shorter events, 192.9 us)
Async XLA Ops:
  7.2 47.5 %all-gather.6.cloned.1.call-start = ((), (), s32[]{:S(2)}) async-start(), calls=%async_computation.5 | async-start | bytes 1327104 | tf_op jit(solution)/shard_map/all_gather | solution.py:635
  9.8 256.0 %all-gather.14.cloned.1.call-start = ((), (), s32[]{:S(2)}) async-start(), calls=%async_computation.9 | async-start | bytes 5308416 | tf_op jit(solution)/shard_map/all_gather | solution.py:638
  12.9 282.6 %all-gather.12.cloned.1.call-start = ((), (), s32[]{:S(2)}) async-start(), calls=%async_computation.8 | async-start | bytes 5308416 | tf_op jit(solution)/shard_map/all_gather | solution.py:638
  13.7 309.4 %all-gather.10.cloned.1.call-start = ((), (), s32[]{:S(2)}) async-start(), calls=%async_computation.7 | async-start | bytes 5308416 | tf_op jit(solution)/shard_map/all_gather | solution.py:638
  14.2 361.8 %all-gather.8.cloned.1.call-start = ((), (), s32[]{:S(2)}) async-start(), calls=%async_computation.6 | async-start | bytes 5308416 | tf_op jit(solution)/shard_map/all_gather | solution.py:638
  18.9 65.3 %collective-permute-start = (bf16[512,768]{1,0:T(8,128)(2,1)S(1)}, bf16[512,768]{1,0:T(8,128)(2,1)}, u32[]{:S(2)}, u32[]{:S(2)}) collective-permute-start(bf16[512,768]{1,0:T(8,128)(2,1)S(1)} %get-tuple-element.154.refs_1_.refs_5_), channel_id=1, source_target_pairs={{0,1},{1,0},{2,3},{3,2},{4,5},{5,4},{6,7},{7,6},{8,9},{9,8},{10,11... | collective-permute-start | bytes 2359304 | tf_op jit(solution)/shard_map/ppermute | solution.py:610
  84.2 35.5 %collective-permute-start.8 = (bf16[1024,768]{1,0:T(8,128)(2,1)}, bf16[1024,768]{1,0:T(8,128)(2,1)}, u32[]{:S(2)}, u32[]{:S(2)}) collective-permute-start(bf16[1024,768]{1,0:T(8,128)(2,1)} %get-tuple-element.47), channel_id=1, source_target_pairs={{0,1},{1,0},{2,3},{3,2},{4,5},{5,4},{6,7},{7,6},{8,9},{9,8},{10,11... | collective-permute-start | bytes 4718600 | tf_op jit(solution)/shard_map/ppermute | solution.py:617
  116.1 77.1 %collective-permute-start.20 = (bf16[512,768]{1,0:T(8,128)(2,1)}, bf16[512,768]{1,0:T(8,128)(2,1)}, u32[]{:S(2)}, u32[]{:S(2)}) collective-permute-start(bf16[512,768]{1,0:T(8,128)(2,1)} %get-tuple-element.159.refs_9_), channel_id=1, source_target_pairs={{0,2},{1,3},{2,0},{3,1},{4,6},{5,7},{6,4},{7,5},{8,10},{9,11},{10,... | collective-permute-start | bytes 2359304 | tf_op jit(solution)/shard_map/ppermute | solution.py:609
  117.6 76.2 %collective-permute-start.19 = (bf16[512,768]{1,0:T(8,128)(2,1)}, bf16[512,768]{1,0:T(8,128)(2,1)}, u32[]{:S(2)}, u32[]{:S(2)}) collective-permute-start(bf16[512,768]{1,0:T(8,128)(2,1)} %get-tuple-element.159.refs_9_), channel_id=1, source_target_pairs={{0,1},{1,0},{2,3},{3,2},{4,5},{5,4},{6,7},{7,6},{8,9},{9,8},{10,11... | collective-permute-start | bytes 2359304 | tf_op jit(solution)/shard_map/ppermute | solution.py:610
  117.6 96.2 %collective-permute-start.14 = (bf16[512,768]{1,0:T(8,128)(2,1)}, bf16[512,768]{1,0:T(8,128)(2,1)}, u32[]{:S(2)}, u32[]{:S(2)}) collective-permute-start(bf16[512,768]{1,0:T(8,128)(2,1)} %get-tuple-element.160.refs_9_), channel_id=1, source_target_pairs={{0,2},{1,3},{2,0},{3,1},{4,6},{5,7},{6,4},{7,5},{8,10},{9,11},{10,... | collective-permute-start | bytes 2359304 | tf_op jit(solution)/shard_map/ppermute | solution.py:609
  118.1 600.9 %reduce-scatter.6.cloned.1.call-start = ((), (), s32[]{:S(2)}) async-start(), calls=%async_computation.10 | async-start | bytes 1327104 | tf_op jit(solution)/shard_map/reduce_scatter | solution.py:720
  123.0 47.5 %collective-permute-start.9 = (bf16[512,768]{1,0:T(8,128)(2,1)}, bf16[512,768]{1,0:T(8,128)(2,1)}, u32[]{:S(2)}, u32[]{:S(2)}) collective-permute-start(bf16[512,768]{1,0:T(8,128)(2,1)} %slice.363), channel_id=1, source_target_pairs={{0,2},{1,3},{2,0},{3,1},{4,6},{5,7},{6,4},{7,5},{8,10},{9,11},{10,... | collective-permute-start | bytes 2359304 | tf_op jit(solution)/shard_map/ppermute | solution.py:619
  128.0 58.5 %collective-permute-start.4 = (bf16[512,768]{1,0:T(8,128)(2,1)S(1)}, bf16[512,768]{1,0:T(8,128)(2,1)}, u32[]{:S(2)}, u32[]{:S(2)}) collective-permute-start(bf16[512,768]{1,0:T(8,128)(2,1)S(1)} %slice.364), channel_id=1, source_target_pairs={{0,2},{1,3},{2,0},{3,1},{4,6},{5,7},{6,4},{7,5},{8,10},{9,11},{10,... | collective-permute-start | bytes 2359304 | tf_op jit(solution)/shard_map/ppermute | solution.py:619
  453.8 40.1 %collective-permute-start.25 = (bf16[512,1664]{1,0:T(8,128)(2,1)S(1)}, bf16[512,1664]{1,0:T(8,128)(2,1)S(1)}, u32[]{:S(2)}, u32[]{:S(2)}) collective-permute-start(bf16[512,1664]{1,0:T(8,128)(2,1)S(1)} %slice.359), channel_id=1, source_target_pairs={{0,2},{1,3},{2,0},{3,1},{4,6},{5,7},{6,4},{7,5},{8,10},{9,11},{10,... | collective-permute-start | bytes 5111816 | tf_op jit(solution)/shard_map/ppermute | solution.py:619
  460.1 69.4 %collective-permute-start.23 = (bf16[512,1664]{1,0:T(8,128)(2,1)}, bf16[512,1664]{1,0:T(8,128)(2,1)S(1)}, u32[]{:S(2)}, u32[]{:S(2)}) collective-permute-start(bf16[512,1664]{1,0:T(8,128)(2,1)} %slice.360), channel_id=1, source_target_pairs={{0,2},{1,3},{2,0},{3,1},{4,6},{5,7},{6,4},{7,5},{8,10},{9,11},{10,... | collective-permute-start | bytes 5111816 | tf_op jit(solution)/shard_map/ppermute | solution.py:619
  544.5 34.6 %collective-permute-start.27 = (bf16[512,768]{1,0:T(8,128)(2,1)S(1)}, bf16[512,768]{1,0:T(8,128)(2,1)S(1)}, u32[]{:S(2)}, u32[]{:S(2)}) collective-permute-start(bf16[512,768]{1,0:T(8,128)(2,1)S(1)} %get-tuple-element.153.refs_1_), channel_id=1, source_target_pairs={{0,2},{1,3},{2,0},{3,1},{4,6},{5,7},{6,4},{7,5},{8,10},{9,11},{10,... | collective-permute-start | bytes 2359304 | tf_op jit(solution)/shard_map/ppermute | solution.py:609
  564.1 52.3 %collective-permute-start.26 = (bf16[512,768]{1,0:T(8,128)(2,1)S(1)}, bf16[512,768]{1,0:T(8,128)(2,1)S(1)}, u32[]{:S(2)}, u32[]{:S(2)}) collective-permute-start(bf16[512,768]{1,0:T(8,128)(2,1)S(1)} %get-tuple-element.153.refs_1_), channel_id=1, source_target_pairs={{0,1},{1,0},{2,3},{3,2},{4,5},{5,4},{6,7},{7,6},{8,9},{9,8},{10,11... | collective-permute-start | bytes 2359304 | tf_op jit(solution)/shard_map/ppermute | solution.py:610
  579.1 37.3 %collective-permute-start.28 = (bf16[512,768]{1,0:T(8,128)(2,1)S(1)}, bf16[512,768]{1,0:T(8,128)(2,1)S(1)}, u32[]{:S(2)}, u32[]{:S(2)}) collective-permute-start(bf16[512,768]{1,0:T(8,128)(2,1)S(1)} %collective-permute-done.27.refs_3_), channel_id=1, source_target_pairs={{0,1},{1,0},{2,3},{3,2},{4,5},{5,4},{6,7},{7,6},{8,9},{9,8},{10,11... | collective-permute-start | bytes 2359304 | tf_op jit(solution)/shard_map/ppermute | solution.py:611
  657.0 161.1 %reduce-scatter.14.cloned.1.call-start = ((), (), s32[]{:S(2)}) async-start(), calls=%async_computation.14 | async-start | bytes 5308416 | tf_op jit(solution)/shard_map/reduce_scatter | solution.py:682
  657.8 259.0 %reduce-scatter.12.cloned.1.call-start = ((), (), s32[]{:S(2)}) async-start(), calls=%async_computation.13 | async-start | bytes 5308416 | tf_op jit(solution)/shard_map/reduce_scatter | solution.py:682
  658.5 357.0 %reduce-scatter.10.cloned.1.call-start = ((), (), s32[]{:S(2)}) async-start(), calls=%async_computation.12 | async-start | bytes 5308416 | tf_op jit(solution)/shard_map/reduce_scatter | solution.py:682
  659.3 454.7 %reduce-scatter.8.cloned.1.call-start = ((), (), s32[]{:S(2)}) async-start(), calls=%async_computation.11 | async-start | bytes 5308416 | tf_op jit(solution)/shard_map/reduce_scatter | solution.py:682
  665.0 57.4 %collective-permute-start.35 = (bf16[512,768]{1,0:T(8,128)(2,1)}, bf16[512,768]{1,0:T(8,128)(2,1)}, u32[]{:S(2)}, u32[]{:S(2)}) collective-permute-start(bf16[512,768]{1,0:T(8,128)(2,1)} %slice.361), channel_id=1, source_target_pairs={{0,2},{1,3},{2,0},{3,1},{4,6},{5,7},{6,4},{7,5},{8,10},{9,11},{10,... | collective-permute-start | bytes 2359304 | tf_op jit(solution)/shard_map/ppermute | solution.py:619
  668.0 54.4 %collective-permute-start.30 = (bf16[512,768]{1,0:T(8,128)(2,1)}, bf16[512,768]{1,0:T(8,128)(2,1)}, u32[]{:S(2)}, u32[]{:S(2)}) collective-permute-start(bf16[512,768]{1,0:T(8,128)(2,1)} %slice.362), channel_id=1, source_target_pairs={{0,2},{1,3},{2,0},{3,1},{4,6},{5,7},{6,4},{7,5},{8,10},{9,11},{10,... | collective-permute-start | bytes 2359304 | tf_op jit(solution)/shard_map/ppermute | solution.py:619
  (82 other events, 1432.1 us)
Sparse Core Ops, SparseCore 0:
  10.8 43.8 all-gather.5
  56.9 78.6 all-gather.13
  137.7 78.0 all-gather.11
  217.9 78.0 all-gather.9
  298.0 78.0 all-gather.7
  657.1 61.8 reduce-scatter.5
  722.6 95.4 reduce-scatter.13
  821.8 94.9 reduce-scatter.11
  920.5 94.9 reduce-scatter.9
  1019.0 94.9 reduce-scatter.7

commit v2 on v1

--- a/solution.py
+++ b/solution.py
@@ -45,37 +45,36 @@
     return pl.BlockSpec(shape, lambda *_: zeros)
 
 
-def attn_fwd_kernel(heads, me_ref, x0, x1, x2, x3, w_ref, lo_ref, proj_ref, mixed_ref, lse_ref,
-                    send_ref, keep_ref, x_s, k_s, vt_s, q_s):
-    me = me_ref[0]
-    step = pl.program_id(0)
-    part = x0.shape[0]
-    seq = x_s.shape[0]
-    nq = seq // QB
-    per = part // QB
-
-    @pl.when(step == 0)
-    def _():
-        for s, ref in enumerate((x0, x1, x2, x3)):
-            x_s[pl.ds(pl.multiple_of((me ^ s) * part, part), part), :] = ref[...]
-
-    @pl.when(step < nq)
-    def _():
-        rows = pl.ds(pl.multiple_of(step * QB, QB), QB)
-        proj = dot_nn(x_s[rows, :], w_ref[:, : heads * 3 * HEAD_DIM]).astype(BF16)
-        proj_ref[...] = proj
-        for h in range(heads):
-            base = h * 3 * HEAD_DIM
-            q_s[h, rows, :] = proj[:, base : base + HEAD_DIM] * 0.125
-            k_s[h, rows, :] = proj[:, base + HEAD_DIM : base + 2 * HEAD_DIM]
-            vt_s[h, :, rows] = proj[:, base + 2 * HEAD_DIM : base + 3 * HEAD_DIM].T
-
-    at = step - nq
-    turn = at // per
-    slot = jnp.where(turn == 0, 1, jnp.where(turn == 1, 3, jnp.where(turn == 2, 0, 2)))
-    blk = (me ^ slot) * per + at % per
-
-    def attend(nk):
+def next_on_cycle(i):
+    y, z = i % 2, i // 2
+    return jnp.where(y == 0, jnp.where(z < 3, i + 2, i + 1), jnp.where(z > 0, i - 2, i - 1))
+
+
+def before_on_cycle(i):
+    y, z = i % 2, i // 2
+    return jnp.where(y == 0, jnp.where(z > 0, i - 2, i + 1), jnp.where(z < 3, i + 2, i - 1))
+
+
+def remote(src, dst, sems, k, peer):
+    send, recv = sems
+    return pltpu.make_async_remote_copy(
+        src_ref=src, dst_ref=dst, send_sem=send.at[k], recv_sem=recv.at[k], device_id=peer,
+        device_id_type=pl.DeviceIdType.MESH,
+    )
+
+
+def greet(peers):
+    barrier = pltpu.get_barrier_semaphore()
+    for peer in peers:
+        pl.semaphore_signal(barrier, inc=1, device_id=peer, device_id_type=pl.DeviceIdType.MESH)
+    pl.semaphore_wait(barrier, len(peers))
+
+
+def attend_rows(blk, lo_ref, q_s, k_s, vt_s, mixed_ref, lse_ref, finish):
+    heads = q_s.shape[0]
+    most = WINDOW // QB + 1
+
+    def window(nk):
         start = pl.multiple_of((blk - (nk - 1)) * QB, QB)
         rows = pl.ds(pl.multiple_of(blk * QB, QB), QB)
         keys = pl.ds(start, nk * QB)
@@ -91,79 +90,297 @@
             top = jnp.max(s, axis=0, keepdims=True)
             p = jnp.exp(s - top)
             total = jnp.sum(p, axis=0, keepdims=True)
-            o = dot_nn(vt_s[h, :, keys], p.astype(BF16)) / total
-            outs.append(o)
+            outs.append(dot_nn(vt_s[h, :, keys], p.astype(BF16)) / total)
             lse_ref[h : h + 1, rows] = top + jnp.log(total)
         mixed_t = jnp.concatenate(outs, axis=0).astype(BF16)
         mixed_ref[:, rows] = mixed_t
-        attn = dot_nt(mixed_t.T, w_ref[:, heads * 3 * HEAD_DIM :]).astype(BF16)
-
-        @pl.when(at < nq // 2)
-        def _():
-            send_ref[...] = attn
-
-        @pl.when(at >= nq // 2)
-        def _():
-            keep_ref[...] = attn
-
-    most = WINDOW // QB + 1
+        finish(mixed_t)
+
     for nk in range(1, most + 1):
         cond = (blk == nk - 1) if nk < most else (blk >= most - 1)
 
-        @pl.when((step >= nq) & cond)
+        @pl.when(cond)
         def _(nk=nk):
-            attend(nk)
-
-
-def attn_fwd(me, xs, w_cat, lo):
-    part, width = xs[0].shape
+            window(nk)
+
+
+SLOT_ORDER = (3, 2, 1, 0)
+STEPS = 9
+NAMES = (
+    "n_over", "n_side", "n_far", "c_over", "c_side", "c_far", "m_over", "m_side", "m_far", "a_far", "a_own", "b_over"
+)
+
+
+def forward_kernel(heads, ring, tok_ref, cot_ref, gain1_ref, gain2_ref, cat_ref, lo_ref, xn_out, moe_out, cot_out,
+                   mixed_ref, lse_ref, hid_ref, wcat_out, xn_s, q_s, k_s, vt_s, part_s, side_s, over_s, moe_s, wcat_ref, send_sem,
+                   recv_sem, local_sem):
+    micro, part, width = tok_ref.shape
     seq = part * 4
-    heads = w_cat.shape[1] // (4 * HEAD_DIM)
     cols = heads * 3 * HEAD_DIM
+    per = part // QB
     nq = seq // QB
-    half = nq // 2
-    spec = pltpu.PrefetchScalarGridSpec(
-        num_scalar_prefetch=1,
-        grid=(2 * nq,),
-        in_specs=[whole((part, width))] * 4 + [
-            whole(w_cat.shape), whole(lo.shape),
-        ],
-        out_specs=[
-            pl.BlockSpec((QB, cols), lambda i, me: (jnp.minimum(i, nq - 1), 0)),
-            whole((heads * HEAD_DIM, seq)),
-            whole((8, seq)),
-            pl.BlockSpec((QB, width), lambda i, me: (jnp.clip(i - nq, 0, half - 1), 0)),
-            pl.BlockSpec((QB, width), lambda i, me: (jnp.clip(i - nq - half, 0, half - 1), 0)),
+    step = pl.program_id(0)
+    m = step // STEPS
+    t = step % STEPS
+    me = lax.axis_index("tp").astype(I32)
+    side = {"tp": me ^ 1}
+    over = {"tp": me ^ 2}
+    sems = (send_sem, recv_sem)
+    mine = pl.ds(pl.multiple_of(me * part, part), part)
+    theirs = pl.ds(pl.multiple_of((me ^ 2) * part, part), part)
+
+    def copy(name, k):
+        table = {
+            "n_over": (0, xn_s.at[k, mine], xn_s.at[k, mine], over),
+            "n_side": (1, xn_s.at[k, mine], xn_s.at[k, mine], side),
+            "n_far": (2, xn_s.at[k, theirs], xn_s.at[k, theirs], side),
+            "c_over": (3, cot_ref.at[k], cot_out.at[k, 3], over),
+            "c_side": (4, cot_ref.at[k], cot_out.at[k, 0], side),
+            "c_far": (5, cot_out.at[k, 3], cot_out.at[k, 1], side),
+            "m_over": (6, moe_s.at[k], moe_out.at[k, 3], over),
+            "m_side": (7, moe_s.at[k], moe_out.at[k, 0], side),
+            "m_far": (8, moe_out.at[k, 3], moe_out.at[k, 1], side),
+            "a_far": (9, part_s.at[k, 3], side_s.at[k, 0], side),
+            "a_own": (10, part_s.at[k, 1], side_s.at[k, 1], side),
+            "b_over": (11, part_s.at[k, 2], over_s.at[k], over),
+        }
+        at, source, target, peer = table[name]
+        return remote(source, target, sems, 12 * k + at, peer)
+
+    def keep(at, k):
+        source, target = ((cot_ref.at[k], cot_out.at[k, 2]), (moe_s.at[k], moe_out.at[k, 2]), (xn_s.at[k], xn_out.at[k]))[at]
+        return pltpu.make_async_copy(source, target, local_sem.at[3 * k + at])
+
+    if ring:
+        here = lax.axis_index("fsdp").astype(I32)
+        ahead, behind = next_on_cycle(here), before_on_cycle(here)
+        rows = cat_ref.shape[0]
+
+        def hop(k, source, peer):
+            at = pl.ds(pl.multiple_of(source * rows, rows), rows)
+            return remote(wcat_ref.at[at], wcat_ref.at[at], sems, 24 + k, peer)
+
+    tiles = part // 128
+
+    @pl.when(step == 0)
+    def _():
+        peers = [side, over]
+        if ring:
+            peers += [{"fsdp": ahead}, {"fsdp": behind}]
+        greet(peers)
+        if ring:
+            wcat_ref[pl.ds(pl.multiple_of(here * rows, rows), rows), :] = cat_ref[...]
+            hop(0, here, {"fsdp": ahead}).start()
+            hop(1, here, {"fsdp": behind}).start()
+        else:
+            wcat_ref[...] = cat_ref[...]
+        for k in range(micro):
+            def body(i, _, k=k):
+                at = pl.ds(pl.multiple_of(i * 128, 128), 128)
+                x = tok_ref[k, at, :].astype(F32)
+                r = lax.rsqrt(jnp.mean(x * x, axis=1, keepdims=True) + EPS)
+                xn_s[k, pl.ds(pl.multiple_of(me * part + i * 128, 128), 128), :] = (x * r * gain1_ref[...]).astype(BF16)
+                return 0
+
+            lax.fori_loop(0, tiles, body, 0)
+            if k == 0:
+                c = 0
+                copy("n_over", c).start()
+                copy("n_side", c).start()
+        if ring:
+            one, two = here, here
+            for k in range(1, 4):
+                one, two = before_on_cycle(one), next_on_cycle(two)
+                hop(2 * k - 2, one, {"fsdp": ahead}).wait_recv()
+                hop(2 * k, one, {"fsdp": ahead}).start()
+                hop(2 * k - 1, two, {"fsdp": behind}).wait_recv()
+                if k < 3:
+                    hop(2 * k + 1, two, {"fsdp": behind}).start()
+            hop(6, before_on_cycle(one), {"fsdp": ahead}).wait_recv()
+        c = 0
+        copy("n_over", c).wait_recv()
+        copy("n_far", c).start()
+        copy("n_side", c).wait_recv()
+        copy("n_far", c).wait_recv()
+        c = 1
+        copy("n_over", c).start()
+        copy("n_side", c).start()
+
+    @pl.when(step == STEPS)
+    def _():
+        c = 1
+        copy("n_side", c).wait_recv()
+        copy("n_far", c).wait_recv()
+
+    @pl.when((t == 0) & (m < micro))
+    def _():
+        def body(i, _):
+            at = pl.ds(pl.multiple_of(i * QB, QB), QB)
+            proj = dot_nn(xn_s[m, at, :], wcat_ref[:, :cols]).astype(BF16)
+            for h in range(heads):
+                base = h * 3 * HEAD_DIM
+                q_s[h, at, :] = proj[:, base : base + HEAD_DIM] * 0.125
+                k_s[h, at, :] = proj[:, base + HEAD_DIM : base + 2 * HEAD_DIM]
+                vt_s[h, :, at] = proj[:, base + 2 * HEAD_DIM : base + 3 * HEAD_DIM].T
+            return 0
+
+        lax.fori_loop(0, nq, body, 0)
+
+    @pl.when((t > 0) & (m < micro))
+    def _():
+        at = t - 1
+        slot = 3 - at // per
+        blk = (me ^ slot) * per + at % per
+
+        def finish(mixed_t):
+            rows = pl.ds(pl.multiple_of(at % per * QB, QB), QB)
+            part_s[m, slot, rows, :] = dot_nt(mixed_t.T, wcat_ref[:, cols:]).astype(BF16)
+
+        attend_rows(blk, lo_ref.at[m], q_s, k_s, vt_s, mixed_ref.at[m], lse_ref.at[m], finish)
+
+    for k in range(micro):
+        first = k * STEPS
+        c = k
+
+        @pl.when(step == first + per)
+        def _(c=c):
+            copy("a_far", c).start()
+
+        @pl.when(step == first + 2 * per)
+        def _(c=c, k=k):
+            copy("a_far", c).wait_recv()
+            part_s[k, 2] = (part_s[k, 2].astype(F32) + side_s[k, 0].astype(F32)).astype(BF16)
+            copy("b_over", c).start()
+            if k == 0:
+                d = 1
+                copy("n_over", d).wait_recv()
+                copy("n_far", d).start()
+                keep(0, c).start()
+                copy("c_side", c).start()
+                copy("c_over", c).start()
+            else:
+                d = 0
+                copy("m_over", d).wait_recv()
+                copy("m_far", d).start()
+                keep(0, c).start()
+                copy("c_side", c).start()
+                copy("c_over", c).start()
+
+        @pl.when(step == first + 3 * per)
+        def _(c=c, k=k):
+            copy("a_own", c).start()
+            if k == 1:
+                d = 0
+                copy("c_over", d).wait_recv()
+                copy("c_far", d).start()
+
+        @pl.when(step == first + 4 * per)
+        def _(c=c, k=k):
+            copy("a_own", c).wait_recv()
+            copy("b_over", c).wait_recv()
+
+            def body(i, _):
+                at = pl.ds(pl.multiple_of(i * 128, 128), 128)
+                hid = (
+                    tok_ref[k, at, :].astype(F32) + part_s[k, 0, at, :].astype(F32)
+                    + side_s[k, 1, at, :].astype(F32) + over_s[k, at, :].astype(F32)
+                )
+                hid_ref[k, at, :] = hid
+                r = lax.rsqrt(jnp.mean(hid * hid, axis=1, keepdims=True) + EPS)
+                moe_s[k, at, :] = (hid * r * gain2_ref[...]).astype(BF16)
+                return 0
+
+            lax.fori_loop(0, tiles, body, 0)
+            copy("m_over", c).start()
+            copy("m_side", c).start()
+            keep(1, c).start()
+            keep(2, c).start()
+
+    def keep_w():
+        return pltpu.make_async_copy(wcat_ref, wcat_out, local_sem.at[6])
+
+    @pl.when(step == STEPS)
+    def _():
+        keep_w().start()
+
+    @pl.when(step == 2 * STEPS)
+    def _():
+        c, d = 0, 1
+        keep_w().wait()
+        copy("m_over", d).wait_recv()
+        copy("m_far", d).start()
+        copy("c_over", d).wait_recv()
+        copy("c_far", d).start()
+        for e in (c, d):
+            copy("c_side", e).wait_recv()
+            copy("c_far", e).wait_recv()
+            copy("m_side", e).wait_recv()
+            copy("m_far", e).wait_recv()
+            for name in NAMES:
+                copy(name, e).wait_send()
+            for at in range(3):
+                keep(at, e).wait()
+        if ring:
+            one, two = here, here
+            for k in range(4):
+                hop(2 * k, one, {"fsdp": ahead}).wait_send()
+                if k < 3:
+                    hop(2 * k + 1, two, {"fsdp": behind}).wait_send()
+                one, two = before_on_cycle(one), next_on_cycle(two)
+
+
+def forward_half(tokens, cotangent, gain1, gain2, cat, low, ring):
+    micro, part, width = tokens.shape
+    seq = part * 4
+    wide = cat.shape[1]
+    heads = wide // (4 * HEAD_DIM)
+    hc = heads * HEAD_DIM
+    anywhere = pl.BlockSpec(memory_space=pl.ANY)
+    return pl.pallas_call(
+        lambda *refs: forward_kernel(heads, ring, *refs),
+        grid=(2 * STEPS + 1,),
+        in_specs=[whole(tokens.shape), anywhere, whole((1, width)), whole((1, width)), whole(cat.shape), whole(low.shape)],
+        out_specs=[anywhere, anywhere, anywhere, whole((micro, hc, seq)), whole((micro, 8, seq)),
+                   whole((micro, part, width)), anywhere],
+        out_shape=[
+            jax.ShapeDtypeStruct((micro, seq, width), BF16),
+            jax.ShapeDtypeStruct((micro, 4, part, width), BF16),
+            jax.ShapeDtypeStruct((micro, 4, part, width), BF16),
+            jax.ShapeDtypeStruct((micro, hc, seq), BF16),
+            jax.ShapeDtypeStruct((micro, 8, seq), F32),
+            jax.ShapeDtypeStruct((micro, part, width), F32),
+            jax.ShapeDtypeStruct((width, wide), BF16),
         ],
         scratch_shapes=[
-            pltpu.VMEM((seq, width), BF16),
+            pltpu.VMEM((micro, seq, width), BF16),
+            pltpu.VMEM((heads, seq, HEAD_DIM), BF16),
             pltpu.VMEM((heads, seq, HEAD_DIM), BF16),
             pltpu.VMEM((heads, HEAD_DIM, seq), BF16),
-            pltpu.VMEM((heads, seq, HEAD_DIM), BF16),
+            pltpu.VMEM((micro, 4, part, width), BF16),
+            pltpu.VMEM((micro, 2, part, width), BF16),
+            pltpu.VMEM((micro, part, width), BF16),
+            pltpu.VMEM((micro, part, width), BF16),
+            pltpu.VMEM((width, wide), BF16),
+            pltpu.SemaphoreType.DMA((31,)),
+            pltpu.SemaphoreType.DMA((31,)),
+            pltpu.SemaphoreType.DMA((7,)),
         ],
-    )
-    return pl.pallas_call(
-        lambda *refs: attn_fwd_kernel(heads, *refs),
-        grid_spec=spec,
-        out_shape=[
-            jax.ShapeDtypeStruct((seq, cols), BF16),
-            jax.ShapeDtypeStruct((heads * HEAD_DIM, seq), BF16),
-            jax.ShapeDtypeStruct((8, seq), F32),
-            jax.ShapeDtypeStruct((seq // 2, width), BF16),
-            jax.ShapeDtypeStruct((seq // 2, width), BF16),
-        ],
-        compiler_params=params("arbitrary"),
-        cost_estimate=pl.CostEstimate(flops=12_000_000_000, bytes_accessed=16_000_000, transcendentals=0),
-        name="attn_fwd",
-    )(me, *xs, w_cat, lo)
-
-
-def attn_bwd_kernel(heads, me_ref, g0, g1, g2, g3, x0, x1, x2, x3, w_ref, lo_ref, proj_ref,
-                    mixed_ref, lse_ref, dw_ref, send_ref, keep_ref, g_s, x_s, k_s, kt_s, v_s, dk_s, dv_s, dq_s,
-                    dwo_s):
+        compiler_params=pltpu.CompilerParams(
+            dimension_semantics=("arbitrary",), vmem_limit_bytes=VMEM_LIMIT, collective_id=1, has_side_effects=True
+        ),
+        cost_estimate=pl.CostEstimate(flops=100_000_000_000, bytes_accessed=100_000_000, transcendentals=0),
+        name="forward_half",
+    )(tokens, cotangent, gain1, gain2, cat, low)
+
+
+def attn_bwd_kernel(heads, held, me_ref, g0, g1, g2, g3, x_ref, w_ref, lo_ref, mixed_ref,
+                    lse_ref, *refs):
+    before = refs[:2] if held else ()
+    (dw_ref, gain_ref, send_ref, keep_ref, g_s, k_s, kt_s, v_s, dk_s, dv_s, dq_s, dwo_s) = refs[-12:]
+    x_s, mixed_ref, lse_ref, lo_ref = x_ref.at[0], mixed_ref.at[0], lse_ref.at[0], lo_ref.at[0]
     me = me_ref[0]
     step = pl.program_id(0)
-    part = x0.shape[0]
+    part = g0.shape[0]
     seq = x_s.shape[0]
     nq = seq // QB
     per = part // QB
@@ -173,12 +390,15 @@
     def _():
         for s, ref in enumerate((g0, g1, g2, g3)):
             g_s[pl.ds(pl.multiple_of((me ^ s) * part, part), part), :] = ref[...]
-        for s, ref in enumerate((x0, x1, x2, x3)):
-            x_s[pl.ds(pl.multiple_of((me ^ s) * part, part), part), :] = ref[...]
         dk_s[...] = jnp.zeros_like(dk_s)
         dv_s[...] = jnp.zeros_like(dv_s)
         dwo_s[...] = jnp.zeros_like(dwo_s)
-        dw_ref[...] = jnp.zeros_like(dw_ref)
+        if before:
+            dw_ref[...] = before[0][...]
+            gain_ref[...] = before[1][...]
+        else:
+            dw_ref[...] = jnp.zeros_like(dw_ref)
+            gain_ref[...] = jnp.zeros_like(gain_ref)
 
     def attend(nk):
         start = pl.multiple_of((step - (nk - 1)) * QB, QB)
@@ -192,7 +412,7 @@
         lo = lo_ref[:, rows]
         kpos = start + lax.broadcasted_iota(I32, (nk * QB, QB), 0)
         qpos = step * QB + lax.broadcasted_iota(I32, (QB, QB), 1)
-        proj = proj_ref[...]
+        proj = dot_nn(x_s[rows, :], w_ref[:, :cols]).astype(BF16)
         for h in range(heads):
             base = h * 3 * HEAD_DIM
             here = slice(h * HEAD_DIM, (h + 1) * HEAD_DIM)
@@ -234,7 +454,9 @@
             pieces += [dq_s[h, rows, :], dk_s[h, rows, :].astype(BF16), dv_s[h, rows, :].astype(BF16)]
         dproj = jnp.concatenate(pieces, axis=1)
         dw_ref[:, :cols] += dot_tn(x_s[rows, :], dproj)
-        gn = dot_nt(dproj, w_ref[:, :cols]).astype(BF16)
+        gn = dot_nt(dproj, w_ref[:, :cols])
+        gain_ref[...] += jnp.sum((gn * x_s[rows, :].astype(F32)).reshape(QB // 8, 8, gn.shape[1]), axis=0)
+        gn = gn.astype(BF16)
 
         @pl.when(at < nq // 2)
         def _():
@@ -246,11 +468,11 @@
 
         @pl.when(at == nq - 1)
         def _():
-            dw_ref[:, cols:] = dwo_s[...].T
-
-
-def attn_bwd(me, gs, xs, w_cat, lo, proj, mixed_t, lse):
-    part, width = xs[0].shape
+            dw_ref[:, cols:] += dwo_s[...].T
+
+
+def attn_bwd(m, me, gs, xn, w_cat, lo, mixed_t, lse, before, deps=()):
+    part, width = gs[0].shape
     seq = part * 4
     heads = w_cat.shape[1] // (4 * HEAD_DIM)
     cols = heads * 3 * HEAD_DIM
@@ -260,19 +482,21 @@
     spec = pltpu.PrefetchScalarGridSpec(
         num_scalar_prefetch=1,
         grid=(2 * nq,),
-        in_specs=[whole((part, width))] * 8 + [
-            whole(w_cat.shape), whole(lo.shape),
-            pl.BlockSpec((QB, cols), lambda i, me: (jnp.minimum(i, nq - 1), 0)),
-            whole((hc, seq)),
-            whole((8, seq)),
-        ],
+        in_specs=[whole((part, width))] * 4 + [
+            pl.BlockSpec((1, seq, width), lambda i, me: (m, 0, 0)),
+            whole(w_cat.shape),
+            pl.BlockSpec((1, 1, seq), lambda i, me: (m, 0, 0)),
+            pl.BlockSpec((1, hc, seq), lambda i, me: (m, 0, 0)),
+            pl.BlockSpec((1, 8, seq), lambda i, me: (m, 0, 0)),
+        ] + ([whole((width, cols + hc)), whole((8, width))] if before else [])
+        + [pl.BlockSpec(memory_space=pl.ANY)] * len(deps),
         out_specs=[
             whole((width, cols + hc)),
+            whole((8, width)),
             pl.BlockSpec((QB, width), lambda i, me: (jnp.clip(i - nq, 0, half - 1), 0)),
             pl.BlockSpec((QB, width), lambda i, me: (jnp.clip(i - nq - half, 0, half - 1), 0)),
         ],
         scratch_shapes=[
-            pltpu.VMEM((seq, width), BF16),
             pltpu.VMEM((seq, width), BF16),
             pltpu.VMEM((heads, seq, HEAD_DIM), BF16),
             pltpu.VMEM((heads, HEAD_DIM, seq), BF16),
@@ -284,17 +508,18 @@
         ],
     )
     return pl.pallas_call(
-        lambda *refs: attn_bwd_kernel(heads, *refs),
+        lambda *refs: attn_bwd_kernel(heads, bool(before), *refs),
         grid_spec=spec,
         out_shape=[
             jax.ShapeDtypeStruct((width, cols + hc), F32),
+            jax.ShapeDtypeStruct((8, width), F32),
             jax.ShapeDtypeStruct((seq // 2, width), BF16),
             jax.ShapeDtypeStruct((seq // 2, width), BF16),
         ],
         compiler_params=params("arbitrary"),
         cost_estimate=pl.CostEstimate(flops=40_000_000_000, bytes_accessed=20_000_000, transcendentals=0),
         name="attn_bwd",
-    )(me, *gs, *xs, w_cat, lo, proj, mixed_t, lse)
+    )(me, *gs, xn, w_cat, lo, mixed_t, lse, *before, *deps)
 
 
 def run_copies(n, src, src_at, dst, dst_at, sems, act):
@@ -314,19 +539,19 @@
                 copy.wait()
 
 
-def dispatch_kernel(experts, n_ref, lo_ref, off_ref, x0, x1, x2, x3, c0, c1, c2, c3, rt_ref, pos_ref, *refs):
+def dispatch_kernel(m, experts, n_ref, lo_ref, off_ref, x_all, c_all, rt_ref, pos_ref, *refs):
     xs_ref, gs_ref, meta_ref, x_s, c_s, xl, gl, in_sems, sems = refs[-9:]
     step = pl.program_id(0)
     slot = step % 2
     rows = xl.shape[1]
     part = x_s.shape[1]
 
-    def load(s):
-        for t, (x, c) in enumerate(((x0, c0), (x1, c1), (x2, c2), (x3, c3))):
-            @pl.when(s == t)
-            def _(x=x, c=c, t=t):
-                pltpu.make_async_copy(x, x_s.at[t % 2], in_sems.at[t % 2, 0]).start()
-                pltpu.make_async_copy(c, c_s.at[t % 2], in_sems.at[t % 2, 1]).start()
+    def loads(s):
+        at = s % 2
+        return (
+            pltpu.make_async_copy(x_all.at[m, s], x_s.at[at], in_sems.at[at, 0]),
+            pltpu.make_async_copy(c_all.at[m, s], c_s.at[at], in_sems.at[at, 1]),
+        )
 
     def moves(at, slot, act):
         for e in range(experts):
@@ -336,18 +561,20 @@
 
     @pl.when(step == 0)
     def _():
-        load(0)
+        for copy in loads(0):
+            copy.start()
 
     @pl.when(step < 3)
     def _():
-        load(step + 1)
+        for copy in loads(step + 1):
+            copy.start()
 
     @pl.when(step >= 2)
     def _():
         moves(step - 2, slot, "wait")
 
-    pltpu.make_async_copy(x0, x_s.at[slot], in_sems.at[slot, 0]).wait()
-    pltpu.make_async_copy(c0, c_s.at[slot], in_sems.at[slot, 1]).wait()
+    for copy in loads(step):
+        copy.wait()
     x = x_s[slot]
     logits = dot_nt(rt_ref[...], x)
     spots = pos_ref[0]
@@ -380,14 +607,14 @@
     return -(-(2 * part + experts * (ROW_TILE - 1)) // 128) * 128
 
 
-def dispatch(tables, xs, cs, router_t, spots, held, experts, most):
-    part, width = xs[0].shape
+def dispatch(m, tables, xs, cs, router_t, spots, held, experts, most):
+    part, width = xs.shape[2:]
     rows = local_rows(part, experts)
     anywhere = pl.BlockSpec(memory_space=pl.ANY)
     spec = pltpu.PrefetchScalarGridSpec(
         num_scalar_prefetch=3,
         grid=(4,),
-        in_specs=[anywhere] * 8 + [
+        in_specs=[anywhere] * 2 + [
             whole(router_t.shape),
             pl.BlockSpec((1, 8, part), lambda i, *_: (i, 0, 0)),
         ] + [anywhere] * len(held),
@@ -402,21 +629,25 @@
         ],
     )
     return pl.pallas_call(
-        lambda *refs: dispatch_kernel(experts, *refs),
+        lambda *refs: dispatch_kernel(m, experts, *refs),
         grid_spec=spec,
         out_shape=[
             jax.ShapeDtypeStruct((experts, most, width), BF16),
             jax.ShapeDtypeStruct((experts, most, width), BF16),
             jax.ShapeDtypeStruct((4, 8, part), F32),
         ],
-        input_output_aliases={13: 0, 14: 1} if held else {},
+        input_output_aliases={7: 0, 8: 1} if held else {},
         compiler_params=params("arbitrary"),
         cost_estimate=pl.CostEstimate(flops=10_000_000_000, bytes_accessed=20_000_000, transcendentals=0),
         name="dispatch",
-    )(*tables, *xs, *cs, router_t, spots, *held)
-
-
-def expert_kernel(first, tot_ref, xs_ref, gs_ref, w_ref, od_ref, dw_ref, din_s, dout_s):
+    )(*tables, xs, cs, router_t, spots, *held)
+
+
+def expert_kernel(first, shards, deps, split, tot_ref, src_ref, out_ref, xs_ref, gs_ref, *refs):
+    w_refs = refs[:shards]
+    refs = refs[shards + deps :]
+    od_ref, dw_refs = refs[0], refs[1 : 3 if split else 2]
+    w_s, din_s, dout_s = refs[-3:]
     e = pl.program_id(0)
     c = pl.program_id(1)
     tot = tot_ref[first + e]
@@ -426,14 +657,19 @@
     def _():
         din_s[...] = jnp.zeros_like(din_s)
         dout_s[...] = jnp.zeros_like(dout_s)
+        for s, ref in enumerate(w_refs):
+            rows = ref.shape[2]
+            at = pl.ds(pl.multiple_of(src_ref[s] * rows, rows), rows)
+            w_s[0, at, :] = ref[0, 0]
+            w_s[1, at, :] = ref[0, 1]
 
     @pl.when(c * CHUNK < tot)
     def _():
         live = c * CHUNK + lax.broadcasted_iota(I32, (CHUNK, width), 0) < tot
         x = jnp.where(live, xs_ref[0], jnp.zeros((), BF16))
         g = jnp.where(live, gs_ref[0], jnp.zeros((), BF16))
-        w_in = w_ref[0, 0]
-        w_out_t = w_ref[0, 1]
+        w_in = w_s[0]
+        w_out_t = w_s[1]
         pre = dot_nn(x, w_in)
         dact = dot_nn(g, w_out_t)
         square = pre * pre
@@ -453,54 +689,75 @@
 
     @pl.when(c == pl.num_programs(1) - 1)
     def _():
-        dw_ref[0, 0] = din_s[...].astype(BF16)
-        dw_ref[0, 1] = dout_s[...].astype(BF16)
-
-
-def run_experts(first, totals, xs, gs, weights):
-    group, _, width, hidden = weights.shape
+        if not split:
+            dw_refs[0][0, 0] = din_s[...].astype(BF16)
+            dw_refs[0][0, 1] = dout_s[...].astype(BF16)
+        else:
+            count, rows = dw_refs[0].shape[2:4]
+            for which, ref in enumerate(dw_refs):
+                for k in range(count):
+                    at = pl.ds(pl.multiple_of(out_ref[which * count + k] * rows, rows), rows)
+                    ref[0, 0, k] = din_s[at, :].astype(BF16)
+                    ref[0, 1, k] = dout_s[at, :].astype(BF16)
+
+
+def run_experts(first, group, totals, xs, gs, w_shards, src, out_order, split, deps=()):
+    arrays = [array for array, _ in w_shards]
+    shards = len(arrays)
+    rows, hidden = arrays[0].shape[2:]
+    width = xs.shape[2]
     most = xs.shape[1]
     chunks = most // CHUNK
 
     def rows_at(base):
-        def index(e, c, tot):
+        def index(e, c, tot, *_):
             last = jnp.maximum((tot[first + e] + CHUNK - 1) // CHUNK - 1, 0)
             return (base + e, jnp.minimum(c, last), 0)
 
         return index
 
+    def shard_at(base):
+        return lambda e, c, *_: (first - base + e, 0, 0, 0)
+
+    if split:
+        half = (group, 2, out_order.shape[0] // 2, width // out_order.shape[0], hidden)
+        dw_shapes = [half, half]
+        dw_specs = [pl.BlockSpec((1,) + half[1:], lambda e, c, *_: (e, 0, 0, 0, 0))] * 2
+    else:
+        dw_shapes = [(group, 2, width, hidden)]
+        dw_specs = [pl.BlockSpec((1, 2, width, hidden), lambda e, c, *_: (e, 0, 0, 0))]
     spec = pltpu.PrefetchScalarGridSpec(
-        num_scalar_prefetch=1,
+        num_scalar_prefetch=3,
         grid=(group, chunks),
         in_specs=[
             pl.BlockSpec((1, CHUNK, width), rows_at(first)),
             pl.BlockSpec((1, CHUNK, width), rows_at(first)),
-            pl.BlockSpec((1, 2, width, hidden), lambda e, c, tot: (e, 0, 0, 0)),
+        ] + [pl.BlockSpec((1, 2, rows, hidden), shard_at(base)) for _, base in w_shards]
+        + [pl.BlockSpec(memory_space=pl.ANY)] * len(deps),
+        out_specs=[pl.BlockSpec((1, CHUNK, 2 * width + 128), rows_at(0))] + dw_specs,
+        scratch_shapes=[
+            pltpu.VMEM((2, width, hidden), BF16),
+            pltpu.VMEM((width, hidden), F32),
+            pltpu.VMEM((width, hidden), F32),
         ],
-        out_specs=[
-            pl.BlockSpec((1, CHUNK, 2 * width + 128), rows_at(0)),
-            pl.BlockSpec((1, 2, width, hidden), lambda e, c, tot: (e, 0, 0, 0)),
-        ],
-        scratch_shapes=[pltpu.VMEM((width, hidden), F32), pltpu.VMEM((width, hidden), F32)],
     )
     return pl.pallas_call(
-        lambda *refs: expert_kernel(first, *refs),
+        lambda *refs: expert_kernel(first, shards, len(deps), split, *refs),
         grid_spec=spec,
-        out_shape=[
-            jax.ShapeDtypeStruct((group, most, 2 * width + 128), BF16),
-            jax.ShapeDtypeStruct((group, 2, width, hidden), BF16),
-        ],
+        out_shape=[jax.ShapeDtypeStruct((group, most, 2 * width + 128), BF16)]
+        + [jax.ShapeDtypeStruct(shape, BF16) for shape in dw_shapes],
         compiler_params=params("arbitrary", "arbitrary"),
         cost_estimate=pl.CostEstimate(
-            flops=group * 12 * 1024 * width * hidden, bytes_accessed=group * 20_000_000, transcendentals=0
+            flops=group * 24 * 1024 * width * hidden, bytes_accessed=group * 20_000_000, transcendentals=0
         ),
         name="experts",
-    )(totals, xs, gs, weights)
+    )(totals, src, out_order, xs, gs, *arrays, *deps)
 
 
 def combine_kernel(experts, groups, n_ref, lo_ref, off_ref, *refs):
     od_refs = refs[:groups]
-    meta_ref, send_ref, keep_ref, od_l, sems = refs[groups:]
+    meta_ref = refs[groups]
+    osend_ref, okeep_ref, bsend_ref, bkeep_ref, od_l, sems = refs[-6:]
     step = pl.program_id(0)
     slot = step % 2
     rows = od_l.shape[1]
@@ -535,29 +792,32 @@
 
     @pl.when(step < 2)
     def _():
-        send_ref[:, :width] = out
-        send_ref[:, width:] = back
+        osend_ref[...] = out
+        bsend_ref[...] = back
 
     @pl.when(step >= 2)
     def _():
-        keep_ref[:, :width] = out
-        keep_ref[:, width:] = back
-
-
-def combine(tables, ods, meta):
+        okeep_ref[...] = out
+        bkeep_ref[...] = back
+
+
+def combine(tables, ods, meta, deps=()):
     experts = sum(od.shape[0] for od in ods)
     groups = len(ods)
     wide = ods[0].shape[2]
+    width = (wide - 128) // 2
     part = meta.shape[2]
     rows = local_rows(part, experts)
     anywhere = pl.BlockSpec(memory_space=pl.ANY)
     spec = pltpu.PrefetchScalarGridSpec(
         num_scalar_prefetch=3,
         grid=(4,),
-        in_specs=[anywhere] * groups + [pl.BlockSpec((1, 8, part), lambda i, *_: (i, 0, 0))],
+        in_specs=[anywhere] * groups + [pl.BlockSpec((1, 8, part), lambda i, *_: (i, 0, 0))]
+        + [anywhere] * len(deps),
         out_specs=[
-            pl.BlockSpec((part, wide), lambda i, *_: (jnp.minimum(i, 1), 0)),
-            pl.BlockSpec((part, wide), lambda i, *_: (jnp.maximum(i - 2, 0), 0)),
+            pl.BlockSpec((part, cols), index)
+            for cols in (width, wide - width)
+            for index in (lambda i, *_: (jnp.minimum(i, 1), 0), lambda i, *_: (jnp.maximum(i - 2, 0), 0))
         ],
         scratch_shapes=[
             pltpu.VMEM((2, rows, wide), BF16),
@@ -567,11 +827,11 @@
     return pl.pallas_call(
         lambda *refs: combine_kernel(experts, groups, *refs),
         grid_spec=spec,
-        out_shape=[jax.ShapeDtypeStruct((2 * part, wide), BF16)] * 2,
+        out_shape=[jax.ShapeDtypeStruct((2 * part, cols), BF16) for cols in (width, width, wide - width, wide - width)],
         compiler_params=params("arbitrary"),
         cost_estimate=pl.CostEstimate(flops=10_000_000_000, bytes_accessed=20_000_000, transcendentals=0),
         name="combine",
-    )(*tables, *ods, meta)
+    )(*tables, *ods, meta, *deps)
 
 
 def routing(routes, capacity, me, part):
@@ -612,12 +872,40 @@
     return (side, far, rows, over)
 
 
-def gather_sum(send, keep):
-    part = keep.shape[0] // 2
+def pair_sum(send, keep):
     got = lax.ppermute(send, "tp", [(i, i ^ 1) for i in range(4)])
-    both = keep.astype(F32) + got.astype(F32)
+    return keep.astype(F32) + got.astype(F32)
+
+
+def chip_sum(both):
+    part = both.shape[0] // 2
     away = lax.ppermute(both[part:].astype(BF16), "tp", [(i, i ^ 2) for i in range(4)])
     return both[:part] + away.astype(F32)
+
+
+def line_sum(send, keep):
+    return line_finish(line_start(send, keep))
+
+
+def line_start(send, keep):
+    got = lax.ppermute(send, "fsdp", [(i, i ^ 1) for i in range(8)])
+    return keep.astype(F32) + got.astype(F32)
+
+
+def line_finish(both):
+    total = both[..., 0, :, :]
+    for k in range(1, 4):
+        piece = both[..., k, :, :].astype(BF16)
+        total += lax.ppermute(piece, "fsdp", [(i, i ^ (2 * k)) for i in range(8)]).astype(F32)
+    return total
+
+
+def sum_everywhere(values, axis, count):
+    step = 1
+    while step < count:
+        values += lax.ppermute(values, axis, [(i, i ^ step) for i in range(count)])
+        step *= 2
+    return values
 
 
 def local(tokens, cotangent, gain_attn, gain_moe, qkv_weight, out_weight, router, w_in, w_out, doc_lengths, routes,
@@ -625,6 +913,8 @@
     micro, part, width = tokens.shape
     seq = part * 4
     experts = w_in.shape[0]
+    n_fsdp = lax.axis_size("fsdp")
+    ring = n_fsdp == 8
     me = lax.axis_index("tp").astype(I32)
     me_arr = me.reshape(1)
     most = -(-micro * (CAP + 4 * ROW_TILE) // CHUNK) * CHUNK
@@ -632,8 +922,14 @@
     each = experts // groups
 
     cat = jnp.concatenate([qkv_weight, out_weight.T], axis=1)
-    w_cat = lax.all_gather(cat, "fsdp", axis=0, tiled=True)
     w_pair = jnp.stack([w_in, w_out.transpose(0, 2, 1)], axis=1)
+    if ring:
+        row_index = lax.axis_index("fsdp").astype(I32)
+        near = 2 * ((row_index // 2) ^ jnp.arange(4, dtype=I32))
+        out_order = jnp.concatenate([near + row_index % 2, near + (1 - row_index % 2)])
+    else:
+        cat = lax.all_gather(cat, "fsdp", axis=0, tiled=True)
+        out_order = jnp.zeros((1,), I32)
     w_groups = [
         lax.all_gather(w_pair[g * each : (g + 1) * each], "fsdp", axis=2, tiled=True) for g in range(groups)
     ]
@@ -647,51 +943,49 @@
     router_t = router.T
     router_float = router.astype(F32)
 
-    x_float = [tokens[m].astype(F32) for m in range(micro)]
-    normed_parts, cot_parts = [], []
-    back_attn = []
+    low = low[:, None, :]
+    xn, moe, cot, mixed_t, lse, hidden, w_cat = forward_half(
+        tokens, cotangent, gain_attn[None], gain_moe[None], cat, low, ring
+    )
+    metas, held = [], ()
     for m in range(micro):
-        normed, back = jax.vjp(norm_scaled, x_float[m], gain_attn)
-        back_attn.append(back)
-        normed_parts.append(spread(normed.astype(BF16)))
-    cot_parts = [spread(cotangent[m]) for m in range(micro)]
-
-    fwd = []
-    moe_rows, back_moe, hidden = [], [], []
-    held = ()
-    metas = []
-    for m in range(micro):
-        side, far, own, over = normed_parts[m]
-        proj, mixed_t, lse, send, keep = attn_fwd(me_arr, (own, side, over, far), w_cat, low[m : m + 1])
-        fwd.append((proj, mixed_t, lse))
-        hid = x_float[m] + gather_sum(send, keep)
-        hidden.append(hid)
-        normed, back = jax.vjp(norm_scaled, hid, gain_moe)
-        back_moe.append(back)
-        moe_rows.append(normed.astype(BF16))
         xs, gs, meta = dispatch(
-            (n[m], lo_at[m], off[m]), spread(moe_rows[m]), cot_parts[m], router_t, spots[m], held, experts, most
+            m, (n[m], lo_at[m], off[m]), moe, cot, router_t, spots[m], held, experts, most
         )
         held = (xs, gs)
         metas.append(meta)
-
-    ods, dws = [], []
+    back_attn = [jax.vjp(norm_scaled, tokens[m].astype(F32), gain_attn)[1] for m in range(micro)]
+    back_moe = [jax.vjp(norm_scaled, hidden[m], gain_moe)[1] for m in range(micro)]
+    moe_rows = [moe[m, 2] for m in range(micro)]
+
+    ods, dws, halves, deps = [], [], [], ()
     for g in range(groups):
-        od, dw = run_experts(g * each, totals, xs, gs, w_groups[g])
+        first = g * each
+        split = ring and g < groups // 2
+        od, *dw = run_experts(
+            first, each, totals, xs, gs, [(w_groups[g], first)], jnp.zeros((1,), I32), out_order, split, deps
+        )
+        deps = (od,)
         ods.append(od)
-        dws.append(lax.psum_scatter(dw, "fsdp", scatter_dimension=2, tiled=True))
+        if split:
+            halves.append(line_start(dw[1], dw[0]))
+        else:
+            dws.append(lax.psum_scatter(dw[0], "fsdp", scatter_dimension=2, tiled=True).astype(F32))
 
     outputs, grads_in = [], []
     grad_router = jnp.zeros(router.shape, F32)
     grad_gain_two = jnp.zeros(gain_moe.shape, F32)
-    grad_gain_one = jnp.zeros(gain_attn.shape, F32)
-    grad_cat = jnp.zeros((width, w_cat.shape[1]), F32)
     names = jnp.arange(experts, dtype=I32)
+    before, deps = (), ()
+    ready = [tuple(halves[m : m + 1]) for m in range(micro)]
     for m in range(micro):
-        send, keep = combine((n[m], lo_at[m], off[m]), ods, metas[m])
-        summed = gather_sum(send, keep)
-        outputs.append((hidden[m] + summed[:, :width]).astype(BF16))
-        products = summed[:, 2 * width : 2 * width + experts]
+        out_send, out_keep, send, keep = combine((n[m], lo_at[m], off[m]), ods, metas[m], deps + ready[m])
+        both = pair_sum(send, keep)
+        deps = (both,)
+        summed = chip_sum(both)
+        out_both = pair_sum(out_send, out_keep)
+        outputs.append((hidden[m] + chip_sum(out_both)).astype(BF16))
+        products = summed[:, width : width + experts]
         mine = lax.dynamic_slice_in_dim(routes[m], me * part, part, 0)
         gates = metas[m][2, 2:4].T
         full = jnp.sum(jnp.where(mine[:, :, None] == names, gates[:, :, None], 0.0), axis=1)
@@ -700,35 +994,41 @@
             "td,te->de", moe_rows[m].astype(F32), grad_logits, precision=lax.Precision.HIGHEST,
             preferred_element_type=F32,
         )
-        grad_moe = summed[:, width : 2 * width] + jnp.einsum(
+        grad_moe = summed[:, :width] + jnp.einsum(
             "te,de->td", grad_logits, router_float, precision=lax.Precision.HIGHEST, preferred_element_type=F32
         )
         grad_norm, grad_gain = back_moe[m](grad_moe)
         grad_gain_two += grad_gain
         grad_hidden = cotangent[m].astype(F32) + grad_norm
         g_side, g_far, g_own, g_over = spread(grad_hidden.astype(BF16))
-        side, far, own, over = normed_parts[m]
-        proj, mixed_t, lse = fwd[m]
-        dcat, send, keep = attn_bwd(
-            me_arr, (g_own, g_side, g_over, g_far), (own, side, over, far), w_cat, low[m : m + 1], proj, mixed_t, lse
+        done = [line_finish(half) for half in halves[m : m + 1]]
+        dws[m:m] = done
+        done += [outputs[0]] if m == 1 else []
+        dcat, gain_rows, send, keep = attn_bwd(
+            m, me_arr, (g_own, g_side, g_over, g_far), xn, w_cat, low, mixed_t, lse, before, tuple(done)
         )
-        grad_cat += dcat
-        grad_x, grad_gain = back_attn[m](gather_sum(send, keep))
-        grad_gain_one += grad_gain
+        before = (dcat, gain_rows)
+        grad_x, _ = back_attn[m](chip_sum(pair_sum(send, keep)))
         grads_in.append((grad_hidden + grad_x).astype(BF16))
 
-    grad_cat = lax.psum_scatter(grad_cat.astype(BF16), "fsdp", scatter_dimension=0, tiled=True).astype(F32)
-    dw = jnp.concatenate(dws, axis=0).astype(F32)
-    grad_router, grad_gain_one, grad_gain_two = lax.psum((grad_router, grad_gain_one, grad_gain_two), ("fsdp", "tp"))
     cols = qkv_weight.shape[1]
+    if ring:
+        blocks = dcat.reshape(n_fsdp, width // n_fsdp, -1).astype(BF16)
+        grad_cat = line_sum(jnp.take(blocks, out_order[4:], axis=0), jnp.take(blocks, out_order[:4], axis=0))
+    else:
+        grad_cat = lax.psum_scatter(dcat.astype(BF16), "fsdp", scatter_dimension=0, tiled=True).astype(F32)
+    grad_gain_one = jnp.sum(gain_rows, axis=0) / gain_attn
+    small = jnp.concatenate([grad_router.T, grad_gain_one[None], grad_gain_two[None]], axis=0)
+    small = sum_everywhere(sum_everywhere(small, "tp", 4), "fsdp", n_fsdp)
+    dw = jnp.concatenate(dws, axis=0)
     return (
         jnp.stack(outputs),
         jnp.stack(grads_in),
-        grad_gain_one,
-        grad_gain_two,
+        small[experts],
+        small[experts + 1],
         grad_cat[:, :cols],
         grad_cat[:, cols:].T,
-        grad_router,
+        small[:experts].T,
         dw[:, 0],
         dw[:, 1].transpose(0, 2, 1),
     )

time: 1140 us -> 832 us (0.73)
  waiting for transfers between devices: 632 us -> 219 us
  Pallas kernels: 326 us -> 433 us
  blocking collectives: 43.4 us -> 0 us
  local copies, waits for them, and re-layouts: 31.7 us -> 48.5 us
  other arithmetic: 47.5 us -> 62.2 us
    reduce_scatter x5 -> x2, waiting for transfers between devices: 381 us -> 0.01 us  [local(): lax.psum_scatter(dw[0], 'fsdp', scatter_dimension=2, tiled=True).astype(F32)]
    pallas_call x10 -> x9, Pallas kernels: 282 us -> 388 us  [the longest x1 163 us: forward_half(): pl.pallas_call(lambda *refs: forward_kernel(heads, ring, *refs), grid=(2...]
    ppermute x8 -> x2, waiting for transfers between devices: 94.4 us -> 0.01 us  [spread(): over = lax.ppermute(rows, 'tp', [(i, i ^ 2) for i in range(4)])]
    psum x1 -> x0, blocking collectives: 43.4 us -> none  [local(): lax.psum((grad_router, grad_gain_one, grad_gain_two), ('fsdp', 'tp'))]
    ppermute x12 -> x29, waiting for transfers between devices: 123 us -> 160 us  [the longest x9 82.5 us: line_finish(): lax.ppermute(piece, 'fsdp', [(i, i ^ 2 * k) for i in range(8)]).astype(F32)]
    all_gather x4, waiting for transfers between devices: 27.4 us -> 57.7 us  [local(): lax.all_gather(w_pair[g * each:(g + 1) * each], 'fsdp', axis=2, tiled=True)]
    ppermute x12 -> x29, starting transfers between devices: 8.43 us -> 25.9 us  [the longest x9 10.5 us: line_finish(): lax.ppermute(piece, 'fsdp', [(i, i ^ 2 * k) for i in range(8)]).astype(F32)]
  transfers between devices with their start and end apart: 46 -> 41, of which waited for: 19 -> 14; matrix products, arithmetic and copies ran while one was open for 5% -> 12% of each run, Pallas kernels for 21% -> 53%
where the time goes in v2:
time: 832 us; the launch traced here: 817 us
  Pallas kernels  433 us (52%)
  waiting for transfers between devices  219 us (26%)
  other arithmetic  62.2 us (7%)
  local copies, waits for them, and re-layouts  48.5 us (6%)
  starting transfers between devices  28.8 us (3%)
  between operations  15.6 us (2%)
  matrix products  9.65 us (1%)
    pallas_call x1, Pallas kernels, forward_half(): pl.pallas_call(lambda *refs: forward_kernel(heads, ring, *refs), grid=(2...  163 us
    pallas_call x4, Pallas kernels, run_experts(): pl.pallas_call(lambda *refs: expert_kernel(first, shards, len(deps), spli...  109 us
    ppermute x9, waiting for transfers between devices, line_finish(): lax.ppermute(piece, 'fsdp', [(i, i ^ 2 * k) for i in range(8)]).astype(F32)  82.5 us
    pallas_call x2, Pallas kernels, attn_bwd(): pl.pallas_call(lambda *refs: attn_bwd_kernel(heads, bool(before), *refs),...  78.4 us
    ppermute x6, waiting for transfers between devices, chip_sum(): lax.ppermute(both[part:].astype(BF16), 'tp', [(i, i ^ 2) for i in range(4)])  59 us
    all_gather x4, waiting for transfers between devices, local(): lax.all_gather(w_pair[g * each:(g + 1) * each], 'fsdp', axis=2, tiled=True)  57.7 us
    pallas_call x2, Pallas kernels, combine(): pl.pallas_call(lambda *refs: combine_kernel(experts, groups, *refs), grid...  44.9 us
    pallas_call x2, Pallas kernels, dispatch(): pl.pallas_call(lambda *refs: dispatch_kernel(m, experts, *refs), grid_spe...  37.9 us
  transfers between devices with their start and end apart: 41, of which 14 were waited for; matrix products, arithmetic and copies ran while one was open for 12% of the time, Pallas kernels for 53%

profile of v2, /device:TPU:0, one launch (start us, length us, event | category | flops | bytes accessed | tf_op | source)
XLA Modules:
  0.0 817.1 jit_solution(8732974443343129171)
XLA Ops:
  23.3 162.7 %forward_half.1 = (bf16[2,2048,768]{2,1,0:T(8,128)(2,1)}, bf16[2,4,512,768]{3,2,1,0:T(8,128)(2,1)}, bf16[2,4,512,768]{3,2,1,0:T(8,128)(2,1)}, bf16[2,192,2048]{2...) custom-call(bf16[2,512,768]{2,1,0:T(8,128)(2,1)} %refs_0_.1, ...), custom_call_target="tpu_custom_call" | custom-call | flops 99999997952 | bytes 100000000 | tf_op jit(solution)/shard_map/forward_half/pallas_call | solution.py:339
  186.0 19.1 %dispatch.2 = (bf16[8,1792,768]{2,1,0:T(8,128)(2,1)}, bf16[8,1792,768]{2,1,0:T(8,128)(2,1)}, f32[4,8,512]{2,1,0:T(8,128)}) custom-call(s32[4,8]{1,0:T(4,128)} %bitcast.201, s32[4,8]{1,0:T(4,128)} %bitcast.203, s32[4,8]{1,0:T(4,128)} %get-tuple-element.186.refs_2_, bf16[2,4,512,768]{3,2,1,0:T(8,128)(2,1)} %get-tuple-element.51.refs_3_, ...), custom_call_target="tpu_custom_call" | custom-call | flops 10000000000 | bytes 20000000 | tf_op jit(solution)/shard_map/dispatch/pallas_call | solution.py:631
  205.1 18.8 %dispatch.3 = (bf16[8,1792,768]{2,1,0:T(8,128)(2,1)}, bf16[8,1792,768]{2,1,0:T(8,128)(2,1)}, f32[4,8,512]{2,1,0:T(8,128)}) custom-call(s32[4,8]{1,0:T(4,128)} %bitcast.197, s32[4,8]{1,0:T(4,128)} %bitcast.199, s32[4,8]{1,0:T(4,128)} %get-tuple-element.187.refs_2_, ...), custom_call_target="tpu_custom_call", output_to_operand_aliasing={{0}: (7, {}), {1}: (8, {})} | custom-call | flops 10000000000 | bytes 20000000 | tf_op jit(solution)/shard_map/dispatch/pallas_call | solution.py:631
  224.5 30.0 %experts.4 = (bf16[2,1792,1664]{2,1,0:T(8,128)(2,1)}, bf16[2,2,4,96,768]{4,3,2,1,0:T(8,128)(2,1)}, bf16[2,2,4,96,768]{4,3,2,1,0:T(8,128)(2,1)}) custom-call(s32[8]{0:T(128)} %get-tuple-element.154.refs_0_, s32[1]{0:T(128)} %constant.124.clone.1.refs_1_, s32[8]{0:T(128)} %pad_add_fusion.refs_2_, bf16[8,1792,768]{2,1,0:T(8,128)(2,1)} %get-tuple-element.55.refs_3_, ...), custom_call_target="tpu_custom_call" | custom-call | flops 28991029248 | bytes 40000000 | tf_op jit(solution)/shard_map/experts/pallas_call | solution.py:744
  258.9 25.8 %experts.5 = (bf16[2,1792,1664]{2,1,0:T(8,128)(2,1)}, bf16[2,2,4,96,768]{4,3,2,1,0:T(8,128)(2,1)}, bf16[2,2,4,96,768]{4,3,2,1,0:T(8,128)(2,1)}) custom-call(s32[8]{0:T(128)} %get-tuple-element.154.refs_0_, s32[1]{0:T(128)} %constant.124.clone.1.refs_1_, s32[8]{0:T(128)} %pad_add_fusion.refs_2_, bf16[8,1792,768]{2,1,0:T(8,128)(2,1)} %get-tuple-element.55.refs_3_, ...), custom_call_target="tpu_custom_call" | custom-call | flops 28991029248 | bytes 40000000 | tf_op jit(solution)/shard_map/experts/pallas_call | solution.py:744
  289.7 25.7 %experts.6 = (bf16[2,1792,1664]{2,1,0:T(8,128)(2,1)}, bf16[2,2,768,768]{3,2,1,0:T(8,128)(2,1)}) custom-call(s32[8]{0:T(128)} %get-tuple-element.154.refs_0_, s32[1]{0:T(128)} %constant.124.clone.1.refs_1_, s32[8]{0:T(128)} %pad_add_fusion.refs_2_, bf16[8,1792,768]{2,1,0:T(8,128)(2,1)} %get-tuple-element.55.refs_3_, ...), custom_call_target="tpu_custom_call" | custom-call | flops 28991029248 | bytes 40000000 | tf_op jit(solution)/shard_map/experts/pallas_call | solution.py:744
  315.3 57.7 %all-gather.11.cloned.1.call-done.refs_5_ = bf16[2,2,768,768]{3,2,1,0:T(8,128)(2,1)} async-done(((bf16[2,2,96,768]{3,2,1,0:T(8,128)(2,1)}), bf16[2,2,768,768]{3,2,1,0:T(8,128)(2,1)}) %all-gather.11.cloned.1.call-update) | async-done | bytes 4718608 | tf_op jit(solution)/shard_map/all_gather | solution.py:934
  373.0 27.8 %experts.7 = (bf16[2,1792,1664]{2,1,0:T(8,128)(2,1)}, bf16[2,2,768,768]{3,2,1,0:T(8,128)(2,1)}) custom-call(s32[8]{0:T(128)} %get-tuple-element.154.refs_0_, s32[1]{0:T(128)} %constant.124.clone.1.refs_1_, s32[8]{0:T(128)} %pad_add_fusion.refs_2_, bf16[8,1792,768]{2,1,0:T(8,128)(2,1)} %get-tuple-element.55.refs_3_, ...), custom_call_target="tpu_custom_call" | custom-call | flops 28991029248 | bytes 40000000 | tf_op jit(solution)/shard_map/experts/pallas_call | solution.py:744
  401.2 4.6 fusion.65
  409.5 21.9 %combine.2 = (bf16[1024,768]{1,0:T(8,128)(2,1)}, bf16[1024,768]{1,0:T(8,128)(2,1)}, bf16[1024,896]{1,0:T(8,128)(2,1)}, bf16[1024,896]{1,0:T(8,128)(2,1)}) custom-call(s32[4,8]{1,0:T(4,128)} %bitcast.202, s32[4,8]{1,0:T(4,128)} %bitcast.204, s32[4,8]{1,0:T(4,128)} %get-tuple-element.186.refs_2_, bf16[2,1792,1664]{2,1,0:T(8,128)(2,1)} %get-tuple-element.57.refs_6_.refs_3_, ...), custom_call_target="tpu_custom_call" | custom-call | flops 10000000000 | bytes 20000000 | tf_op jit(solution)/shard_map/combine/pallas_call | solution.py:827
  431.6 4.6 fusion.66
  443.7 23.0 %combine.3 = (bf16[1024,768]{1,0:T(8,128)(2,1)}, bf16[1024,768]{1,0:T(8,128)(2,1)}, bf16[1024,896]{1,0:T(8,128)(2,1)}, bf16[1024,896]{1,0:T(8,128)(2,1)}) custom-call(s32[4,8]{1,0:T(4,128)} %bitcast.198, s32[4,8]{1,0:T(4,128)} %bitcast.200, s32[4,8]{1,0:T(4,128)} %get-tuple-element.187.refs_2_, bf16[2,1792,1664]{2,1,0:T(8,128)(2,1)} %get-tuple-element.57.refs_6_.refs_3_, ...), custom_call_target="tpu_custom_call" | custom-call | flops 10000000000 | bytes 20000000 | tf_op jit(solution)/shard_map/combine/pallas_call | solution.py:827
  480.4 12.0 %collective-permute-done.7 = bf16[512,896]{1,0:T(8,128)(2,1)S(1)} collective-permute-done((bf16[512,896]{1,0:T(8,128)(2,1)S(1)}, bf16[512,896]{1,0:T(8,128)(2,1)S(1)}, u32[]{:S(2)}, u32[]{:S(2)}) %collective-permute-start.7) | collective-permute-done | bytes 917536 | tf_op jit(solution)/shard_map/ppermute | solution.py:882
  495.2 17.0 %collective-permute-done.17 = bf16[512,896]{1,0:T(8,128)(2,1)} collective-permute-done((bf16[512,896]{1,0:T(8,128)(2,1)}, bf16[512,896]{1,0:T(8,128)(2,1)}, u32[]{:S(2)}, u32[]{:S(2)}) %collective-permute-start.17) | collective-permute-done | bytes 917536 | tf_op jit(solution)/shard_map/ppermute | solution.py:882
  521.7 6.7 collective-permute-done.2
  535.3 34.4 %collective-permute-done.12 = bf16[2,2,96,768]{3,2,1,0:T(8,128)(2,1)} collective-permute-done((bf16[2,2,96,768]{3,2,1,0:T(8,128)(2,1)}, bf16[2,2,96,768]{3,2,1,0:T(8,128)(2,1)}, u32[]{:S(2)}, u32[]{:S(2)}) %collective-permute-start.12) | collective-permute-done | bytes 589856 | tf_op jit(solution)/shard_map/ppermute | solution.py:899
  574.1 39.7 %collective-permute-done.22 = bf16[2,2,96,768]{3,2,1,0:T(8,128)(2,1)} collective-permute-done((bf16[2,2,96,768]{3,2,1,0:T(8,128)(2,1)}, bf16[2,2,96,768]{3,2,1,0:T(8,128)(2,1)}, u32[]{:S(2)}, u32[]{:S(2)}) %collective-permute-start.22) | collective-permute-done | bytes 589856 | tf_op jit(solution)/shard_map/ppermute | solution.py:899
  623.4 38.9 %attn_bwd.2 = (f32[768,768]{1,0:T(8,128)}, f32[8,768]{1,0:T(8,128)}, bf16[1024,768]{1,0:T(8,128)(2,1)}, bf16[1024,768]{1,0:T(8,128)(2,1)}) custom-call(s32[1]{0:T(128)} %bitcast.30.refs_0_, bf16[512,768]{1,0:T(8,128)(2,1)} %get-tuple-element.158.refs_1_, bf16[512,768]{1,0:T(8,128)(2,1)} %copy-done.54, bf16[512,768]{1,0:T(8,128)(2,1)} %collective-permute-done.9.refs_3_, ...), custom_call_target="tpu_custom_call" | custom-call | flops 40000000000 | bytes 20000000 | tf_op jit(solution)/shard_map/attn_bwd/pallas_call | solution.py:510
  663.5 39.4 %attn_bwd.3 = (f32[768,768]{1,0:T(8,128)}, f32[8,768]{1,0:T(8,128)}, bf16[1024,768]{1,0:T(8,128)(2,1)}, bf16[1024,768]{1,0:T(8,128)(2,1)}) custom-call(s32[1]{0:T(128)} %bitcast.30.refs_0_, bf16[512,768]{1,0:T(8,128)(2,1)} %get-tuple-element.159.refs_1_, bf16[512,768]{1,0:T(8,128)(2,1)} %copy-done.56, bf16[512,768]{1,0:T(8,128)(2,1)} %copy-done.53, ...), custom_call_target="tpu_custom_call" | custom-call | flops 40000000000 | bytes 20000000 | tf_op jit(solution)/shard_map/attn_bwd/pallas_call | solution.py:510
  718.0 10.3 %collective-permute-done.28 = f32[10,768]{1,0:T(8,128)S(1)} collective-permute-done((f32[10,768]{1,0:T(8,128)S(1)}, f32[10,768]{1,0:T(8,128)S(1)}, u32[]{:S(2)}, u32[]{:S(2)}) %collective-permute-start.28) | collective-permute-done | bytes 30752 | tf_op jit(solution)/shard_map/ppermute | solution.py:906
  728.6 4.0 collective-permute-done.29
  752.1 4.3 collective-permute-done.33
  776.3 9.8 %collective-permute-done.15 = bf16[512,768]{1,0:T(8,128)(2,1)} collective-permute-done((bf16[512,768]{1,0:T(8,128)(2,1)}, bf16[512,768]{1,0:T(8,128)(2,1)}, u32[]{:S(2)}, u32[]{:S(2)}) %collective-permute-start.15) | collective-permute-done | bytes 786464 | tf_op jit(solution)/shard_map/ppermute | solution.py:882
  786.1 13.4 %collective-permute-done.25 = bf16[512,768]{1,0:T(8,128)(2,1)} collective-permute-done((bf16[512,768]{1,0:T(8,128)(2,1)}, bf16[512,768]{1,0:T(8,128)(2,1)}, u32[]{:S(2)}, u32[]{:S(2)}) %collective-permute-start.25) | collective-permute-done | bytes 786464 | tf_op jit(solution)/shard_map/ppermute | solution.py:882
  (316 shorter events, 149.6 us)
Async XLA Ops:
  7.2 217.3 %all-gather.5.cloned.1.call-start = ((), (), s32[]{:S(2)}) async-start(), calls=%async_computation.2 | async-start | bytes 5308416 | tf_op jit(solution)/shard_map/all_gather | solution.py:934
  10.4 248.5 %all-gather.7.cloned.1.call-start = ((), (), s32[]{:S(2)}) async-start(), calls=%async_computation.3 | async-start | bytes 5308416 | tf_op jit(solution)/shard_map/all_gather | solution.py:934
  11.1 278.5 %all-gather.9.cloned.1.call-start = ((), (), s32[]{:S(2)}) async-start(), calls=%async_computation.4 | async-start | bytes 5308416 | tf_op jit(solution)/shard_map/all_gather | solution.py:934
  11.9 361.2 %all-gather.11.cloned.1.call-start = ((), (), s32[]{:S(2)}) async-start(), calls=%async_computation.5 | async-start | bytes 5308416 | tf_op jit(solution)/shard_map/all_gather | solution.py:934
  12.4 755.5 %reduce-scatter.5.cloned.1.call-start = ((), (), s32[]{:S(2)}) async-start(), calls=%async_computation.7 | async-start | bytes 5308416 | tf_op jit(solution)/shard_map/reduce_scatter | solution.py:973
  257.8 143.4 %collective-permute-start = (bf16[2,2,4,96,768]{4,3,1,0,2:T(8,128)(2,1)}, bf16[2,2,4,96,768]{4,3,1,0,2:T(8,128)(2,1)}, u32[]{:S(2)}, u32[]{:S(2)}) collective-permute-start(bf16[2,2,4,96,768]{4,3,1,0,2:T(8,128)(2,1)} %copy.106), channel_id=1, source_target_pairs={{0,4},{4,0},{8,12},{12,8},{16,20},{20,16},{24,28},{28,24},{1,5},{5... | collective-permute-start | bytes 7077896 | tf_op jit(solution)/shard_map/ppermute | solution.py:891
  286.5 145.1 %collective-permute-start.4 = (bf16[2,2,4,96,768]{4,3,1,0,2:T(8,128)(2,1)S(1)}, bf16[2,2,4,96,768]{4,3,1,0,2:T(8,128)(2,1)}, u32[]{:S(2)}, u32[]{:S(2)}) collective-permute-start(bf16[2,2,4,96,768]{4,3,1,0,2:T(8,128)(2,1)S(1)} %copy.109), channel_id=1, source_target_pairs={{0,4},{4,0},{8,12},{12,8},{16,20},{20,16},{24,28},{28,24},{1,5},{5... | collective-permute-start | bytes 7077896 | tf_op jit(solution)/shard_map/ppermute | solution.py:891
  400.9 369.2 %reduce-scatter.3.cloned.1.call-start = ((), (), s32[]{:S(2)}) async-start(), calls=%async_computation.6 | async-start | bytes 5308416 | tf_op jit(solution)/shard_map/reduce_scatter | solution.py:973
  471.6 63.5 %collective-permute-start.13 = (bf16[2,2,96,768]{3,2,1,0:T(8,128)(2,1)}, bf16[2,2,96,768]{3,2,1,0:T(8,128)(2,1)}, u32[]{:S(2)}, u32[]{:S(2)}) collective-permute-start(bf16[2,2,96,768]{3,2,1,0:T(8,128)(2,1)} %get-tuple-element.173), channel_id=1, source_target_pairs={{0,24},{4,28},{8,16},{12,20},{16,8},{20,12},{24,0},{28,4},{1,25},{... | collective-permute-start | bytes 1769480 | tf_op jit(solution)/shard_map/ppermute | solution.py:899
  472.9 96.7 %collective-permute-start.12 = (bf16[2,2,96,768]{3,2,1,0:T(8,128)(2,1)}, bf16[2,2,96,768]{3,2,1,0:T(8,128)(2,1)}, u32[]{:S(2)}, u32[]{:S(2)}) collective-permute-start(bf16[2,2,96,768]{3,2,1,0:T(8,128)(2,1)} %get-tuple-element.174), channel_id=1, source_target_pairs={{0,16},{4,20},{8,24},{12,28},{16,0},{20,4},{24,8},{28,12},{1,17},{... | collective-permute-start | bytes 1769480 | tf_op jit(solution)/shard_map/ppermute | solution.py:899
  473.1 96.6 %collective-permute-start.11 = (bf16[2,2,96,768]{3,2,1,0:T(8,128)(2,1)}, bf16[2,2,96,768]{3,2,1,0:T(8,128)(2,1)}, u32[]{:S(2)}, u32[]{:S(2)}) collective-permute-start(bf16[2,2,96,768]{3,2,1,0:T(8,128)(2,1)} %get-tuple-element.172), channel_id=1, source_target_pairs={{0,8},{4,12},{8,0},{12,4},{16,24},{20,28},{24,16},{28,20},{1,9},{5... | collective-permute-start | bytes 1769480 | tf_op jit(solution)/shard_map/ppermute | solution.py:899
  492.4 36.0 %collective-permute-start.2 = (bf16[512,768]{1,0:T(8,128)(2,1)}, bf16[512,768]{1,0:T(8,128)(2,1)}, u32[]{:S(2)}, u32[]{:S(2)}) collective-permute-start(bf16[512,768]{1,0:T(8,128)(2,1)} %slice.497), channel_id=1, source_target_pairs={{0,2},{1,3},{2,0},{3,1},{4,6},{5,7},{6,4},{7,5},{8,10},{9,11},{10,... | collective-permute-start | bytes 2359304 | tf_op jit(solution)/shard_map/ppermute | solution.py:882
  531.8 42.1 %collective-permute-start.9 = (bf16[512,768]{1,0:T(8,128)(2,1)}, bf16[512,768]{1,0:T(8,128)(2,1)}, u32[]{:S(2)}, u32[]{:S(2)}) collective-permute-start(bf16[512,768]{1,0:T(8,128)(2,1)} %get-tuple-element.158.refs_1_), channel_id=1, source_target_pairs={{0,2},{1,3},{2,0},{3,1},{4,6},{5,7},{6,4},{7,5},{8,10},{9,11},{10,... | collective-permute-start | bytes 2359304 | tf_op jit(solution)/shard_map/ppermute | solution.py:869
  533.6 39.3 %collective-permute-start.23 = (bf16[2,2,96,768]{3,2,1,0:T(8,128)(2,1)}, bf16[2,2,96,768]{3,2,1,0:T(8,128)(2,1)}, u32[]{:S(2)}, u32[]{:S(2)}) collective-permute-start(bf16[2,2,96,768]{3,2,1,0:T(8,128)(2,1)} %get-tuple-element.170), channel_id=1, source_target_pairs={{0,24},{4,28},{8,16},{12,20},{16,8},{20,12},{24,0},{28,4},{1,25},{... | collective-permute-start | bytes 1769480 | tf_op jit(solution)/shard_map/ppermute | solution.py:899
  535.1 78.6 %collective-permute-start.22 = (bf16[2,2,96,768]{3,2,1,0:T(8,128)(2,1)}, bf16[2,2,96,768]{3,2,1,0:T(8,128)(2,1)}, u32[]{:S(2)}, u32[]{:S(2)}) collective-permute-start(bf16[2,2,96,768]{3,2,1,0:T(8,128)(2,1)} %get-tuple-element.171), channel_id=1, source_target_pairs={{0,16},{4,20},{8,24},{12,28},{16,0},{20,4},{24,8},{28,12},{1,17},{... | collective-permute-start | bytes 1769480 | tf_op jit(solution)/shard_map/ppermute | solution.py:899
  569.7 45.2 %collective-permute-start.21 = (bf16[2,2,96,768]{3,2,1,0:T(8,128)(2,1)}, bf16[2,2,96,768]{3,2,1,0:T(8,128)(2,1)}, u32[]{:S(2)}, u32[]{:S(2)}) collective-permute-start(bf16[2,2,96,768]{3,2,1,0:T(8,128)(2,1)} %get-tuple-element.169), channel_id=1, source_target_pairs={{0,8},{4,12},{8,0},{12,4},{16,24},{20,28},{24,16},{28,20},{1,9},{5... | collective-permute-start | bytes 1769480 | tf_op jit(solution)/shard_map/ppermute | solution.py:899
  572.9 49.2 %collective-permute-start.8 = (bf16[512,768]{1,0:T(8,128)(2,1)}, bf16[512,768]{1,0:T(8,128)(2,1)S(1)}, u32[]{:S(2)}, u32[]{:S(2)}) collective-permute-start(bf16[512,768]{1,0:T(8,128)(2,1)} %get-tuple-element.158.refs_1_), channel_id=1, source_target_pairs={{0,1},{1,0},{2,3},{3,2},{4,5},{5,4},{6,7},{7,6},{8,9},{9,8},{10,11... | collective-permute-start | bytes 2359304 | tf_op jit(solution)/shard_map/ppermute | solution.py:870
  572.9 49.0 %collective-permute-start.19 = (bf16[512,768]{1,0:T(8,128)(2,1)S(1)}, bf16[512,768]{1,0:T(8,128)(2,1)S(1)}, u32[]{:S(2)}, u32[]{:S(2)}) collective-permute-start(bf16[512,768]{1,0:T(8,128)(2,1)S(1)} %copy-done.34), channel_id=1, source_target_pairs={{0,2},{1,3},{2,0},{3,1},{4,6},{5,7},{6,4},{7,5},{8,10},{9,11},{10,... | collective-permute-start | bytes 2359304 | tf_op jit(solution)/shard_map/ppermute | solution.py:869
  573.9 48.2 %collective-permute-start.10 = (bf16[512,768]{1,0:T(8,128)(2,1)}, bf16[512,768]{1,0:T(8,128)(2,1)S(1)}, u32[]{:S(2)}, u32[]{:S(2)}) collective-permute-start(bf16[512,768]{1,0:T(8,128)(2,1)} %collective-permute-done.9.refs_3_), channel_id=1, source_target_pairs={{0,1},{1,0},{2,3},{3,2},{4,5},{5,4},{6,7},{7,6},{8,9},{9,8},{10,11... | collective-permute-start | bytes 2359304 | tf_op jit(solution)/shard_map/ppermute | solution.py:871
  618.0 115.1 %collective-permute-start.5 = (bf16[1024,768]{1,0:T(8,128)(2,1)}, bf16[1024,768]{1,0:T(8,128)(2,1)}, u32[]{:S(2)}, u32[]{:S(2)}) collective-permute-start(bf16[1024,768]{1,0:T(8,128)(2,1)} %get-tuple-element.72), channel_id=1, source_target_pairs={{0,1},{1,0},{2,3},{3,2},{4,5},{5,4},{6,7},{7,6},{8,9},{9,8},{10,11... | collective-permute-start | bytes 4718600 | tf_op jit(solution)/shard_map/ppermute | solution.py:876
  618.0 44.3 %collective-permute-start.18 = (bf16[512,768]{1,0:T(8,128)(2,1)S(1)}, bf16[512,768]{1,0:T(8,128)(2,1)S(1)}, u32[]{:S(2)}, u32[]{:S(2)}) collective-permute-start(bf16[512,768]{1,0:T(8,128)(2,1)S(1)} %copy-done.34), channel_id=1, source_target_pairs={{0,1},{1,0},{2,3},{3,2},{4,5},{5,4},{6,7},{7,6},{8,9},{9,8},{10,11... | collective-permute-start | bytes 2359304 | tf_op jit(solution)/shard_map/ppermute | solution.py:870
  622.0 40.3 %collective-permute-start.20 = (bf16[512,768]{1,0:T(8,128)(2,1)S(1)}, bf16[512,768]{1,0:T(8,128)(2,1)S(1)}, u32[]{:S(2)}, u32[]{:S(2)}) collective-permute-start(bf16[512,768]{1,0:T(8,128)(2,1)S(1)} %collective-permute-done.19.refs_3_), channel_id=1, source_target_pairs={{0,1},{1,0},{2,3},{3,2},{4,5},{5,4},{6,7},{7,6},{8,9},{9,8},{10,11... | collective-permute-start | bytes 2359304 | tf_op jit(solution)/shard_map/ppermute | solution.py:871
  718.0 39.2 %collective-permute-start.14 = (bf16[1024,768]{1,0:T(8,128)(2,1)}, bf16[1024,768]{1,0:T(8,128)(2,1)}, u32[]{:S(2)}, u32[]{:S(2)}) collective-permute-start(bf16[1024,768]{1,0:T(8,128)(2,1)} %get-tuple-element.78), channel_id=1, source_target_pairs={{0,1},{1,0},{2,3},{3,2},{4,5},{5,4},{6,7},{7,6},{8,9},{9,8},{10,11... | collective-permute-start | bytes 4718600 | tf_op jit(solution)/shard_map/ppermute | solution.py:876
  750.4 51.4 %collective-permute-start.6 = (bf16[512,768]{1,0:T(8,128)(2,1)}, bf16[512,768]{1,0:T(8,128)(2,1)}, u32[]{:S(2)}, u32[]{:S(2)}) collective-permute-start(bf16[512,768]{1,0:T(8,128)(2,1)} %slice.496), channel_id=1, source_target_pairs={{0,2},{1,3},{2,0},{3,1},{4,6},{5,7},{6,4},{7,5},{8,10},{9,11},{10,... | collective-permute-start | bytes 2359304 | tf_op jit(solution)/shard_map/ppermute | solution.py:882
  (75 other events, 1336.6 us)
Sparse Core Ops, SparseCore 0:
  10.8 92.0 all-gather.4
  105.1 78.0 all-gather.6
  185.4 78.0 all-gather.8
  266.1 106.9 all-gather.10
  401.0 128.7 reduce-scatter.4
  569.9 113.6 reduce-scatter.2

commit v3 on v2

v3 whole, which is shorter than its diff:
```python
import math

import jax
import jax.numpy as jnp
from jax import lax
from jax.experimental import pallas as pl
from jax.experimental.pallas import tpu as pltpu
from jax.sharding import PartitionSpec as P

HEAD_DIM = 64
WINDOW = 1024
CAP = 768
ROW_TILE = 16
QB = 256
CHUNK = 256
EPS = 1e-06
NEG = -1e30
F32 = jnp.float32
BF16 = jnp.bfloat16
I32 = jnp.int32
VMEM_LIMIT = 56 * 1024 * 1024
GELU_A = math.sqrt(2.0 / math.pi)
GELU_B = 0.044715
NEAR = 2


def dot_nn(a, b):
    return lax.dot_general(a, b, (((1,), (0,)), ((), ())), preferred_element_type=F32)


def dot_nt(a, b):
    return lax.dot_general(a, b, (((1,), (1,)), ((), ())), preferred_element_type=F32)


def dot_tn(a, b):
    return lax.dot_general(a, b, (((0,), (0,)), ((), ())), preferred_element_type=F32)


def params(*semantics):
    return pltpu.CompilerParams(dimension_semantics=semantics, vmem_limit_bytes=VMEM_LIMIT)


def whole(shape):
    zeros = (0,) * len(shape)
    return pl.BlockSpec(shape, lambda *_: zeros)


def next_on_cycle(i):
    y, z = i % 2, i // 2
    return jnp.where(y == 0, jnp.where(z < 3, i + 2, i + 1), jnp.where(z > 0, i - 2, i - 1))


def before_on_cycle(i):
    y, z = i % 2, i // 2
    return jnp.where(y == 0, jnp.where(z > 0, i - 2, i + 1), jnp.where(z < 3, i + 2, i - 1))


def remote(src, dst, sems, k, peer):
    send, recv = sems
    return pltpu.make_async_remote_copy(
        src_ref=src, dst_ref=dst, send_sem=send.at[k], recv_sem=recv.at[k], device_id=peer,
        device_id_type=pl.DeviceIdType.MESH,
    )


def greet(peers):
    barrier = pltpu.get_barrier_semaphore()
    for peer in peers:
        pl.semaphore_signal(barrier, inc=1, device_id=peer, device_id_type=pl.DeviceIdType.MESH)
    pl.semaphore_wait(barrier, len(peers))


def attend_rows(blk, lo_ref, q_s, k_s, vt_s, mixed_ref, lse_ref, finish):
    heads = q_s.shape[0]
    most = WINDOW // QB + 1

    def window(nk):
        start = pl.multiple_of((blk - (nk - 1)) * QB, QB)
        rows = pl.ds(pl.multiple_of(blk * QB, QB), QB)
        keys = pl.ds(start, nk * QB)
        lo = lo_ref[:, rows]
        kpos = start + lax.broadcasted_iota(I32, (nk * QB, QB), 0)
        qpos = blk * QB + lax.broadcasted_iota(I32, (QB, QB), 1)
        outs = []
        for h in range(heads):
            s = dot_nt(k_s[h, keys, :], q_s[h, rows, :])
            s = jnp.where(kpos >= lo, s, NEG)
            last = jnp.where(kpos[(nk - 1) * QB :] <= qpos, s[(nk - 1) * QB :], NEG)
            s = last if nk == 1 else jnp.concatenate([s[: (nk - 1) * QB], last], axis=0)
            top = jnp.max(s, axis=0, keepdims=True)
            p = jnp.exp(s - top)
            total = jnp.sum(p, axis=0, keepdims=True)
            outs.append(dot_nn(vt_s[h, :, keys], p.astype(BF16)) / total)
            lse_ref[h : h + 1, rows] = top + jnp.log(total)
        mixed_t = jnp.concatenate(outs, axis=0).astype(BF16)
        mixed_ref[:, rows] = mixed_t
        finish(mixed_t)

    for nk in range(1, most + 1):
        cond = (blk == nk - 1) if nk < most else (blk >= most - 1)

        @pl.when(cond)
        def _(nk=nk):
            window(nk)


SLOT_ORDER = (3, 2, 1, 0)
STEPS = 9
NAMES = (
    "n_over", "n_side", "n_far", "m_over", "m_side", "m_far", "a_far", "a_own", "b_over"
)


def forward_kernel(heads, ring, tok_ref, cot_ref, gain1_ref, gain2_ref, cat_ref, lo_ref, far_ref, near_ref, xn_out, moe_out, cot_out,
                   mixed_ref, lse_ref, hid_ref, wcat_out, far_out, near_out, xn_s, q_s, k_s, vt_s, part_s, side_s, over_s, moe_s, wcat_ref, send_sem,
                   recv_sem, local_sem):
    micro, part, width = tok_ref.shape
    seq = part * 4
    cols = heads * 3 * HEAD_DIM
    per = part // QB
    nq = seq // QB
    step = pl.program_id(0)
    m = step // STEPS
    t = step % STEPS
    me = lax.axis_index("tp").astype(I32)
    side = {"tp": me ^ 1}
    over = {"tp": me ^ 2}
    sems = (send_sem, recv_sem)
    mine = pl.ds(pl.multiple_of(me * part, part), part)
    theirs = pl.ds(pl.multiple_of((me ^ 2) * part, part), part)

    def copy(name, k):
        table = {
            "n_over": (0, xn_s.at[k, mine], xn_s.at[k, mine], over),
            "n_side": (1, xn_s.at[k, mine], xn_s.at[k, mine], side),
            "n_far": (2, xn_s.at[k, theirs], xn_s.at[k, theirs], side),
            "m_over": (6, moe_s.at[k], moe_out.at[k, 3], over),
            "m_side": (7, moe_s.at[k], moe_out.at[k, 0], side),
            "m_far": (8, moe_out.at[k, 3], moe_out.at[k, 1], side),
            "a_far": (9, part_s.at[k, 3], side_s.at[k, 0], side),
            "a_own": (10, part_s.at[k, 1], side_s.at[k, 1], side),
            "b_over": (11, part_s.at[k, 2], over_s.at[k], over),
        }
        at, source, target, peer = table[name]
        return remote(source, target, sems, 12 * k + at, peer)

    def keep(at, k):
        source, target = ((cot_ref.at[k], cot_out.at[k]), (moe_s.at[k], moe_out.at[k, 2]), (xn_s.at[k], xn_out.at[k]))[at]
        return pltpu.make_async_copy(source, target, local_sem.at[3 * k + at])

    if ring:
        here = lax.axis_index("fsdp").astype(I32)
        ahead, behind = next_on_cycle(here), before_on_cycle(here)
        rows = cat_ref.shape[0]

        def hop(k, source, peer):
            at = pl.ds(pl.multiple_of(source * rows, rows), rows)
            return remote(wcat_ref.at[at], wcat_ref.at[at], sems, 24 + k, peer)

        far_rows = far_ref.shape[2]

        chains = far_ref.shape[0]
        onward = (chains + 1) // 2

        def far_hop(c, k, source, peer):
            at = pl.ds(pl.multiple_of(source * far_rows, far_rows), far_rows)
            held = far_ref.at[c] if k < 2 else far_out.at[c, :, at]
            return remote(held, far_out.at[c, :, at], sems, 31 + 7 * c + k, peer)

        def far_last(c, one, two):
            return far_hop(c, 6, one, {"fsdp": ahead}) if c < onward else far_hop(c, 6, two, {"fsdp": behind})

        def far_own():
            at = pl.ds(pl.multiple_of(here * far_rows, far_rows), far_rows)
            return pltpu.make_async_copy(far_ref, far_out.at[:, :, at], local_sem.at[7])

        def along(k):
            one, two = here, here
            for _ in range(k):
                one, two = before_on_cycle(one), next_on_cycle(two)
            return one, two

    tiles = part // 128

    @pl.when(step == 0)
    def _():
        peers = [side, over]
        if ring:
            peers += [{"fsdp": ahead}, {"fsdp": behind}]
        greet(peers)
        if ring:
            wcat_ref[pl.ds(pl.multiple_of(here * rows, rows), rows), :] = cat_ref[...]
            hop(0, here, {"fsdp": ahead}).start()
            hop(1, here, {"fsdp": behind}).start()
            far_own().start()
            for c in range(chains):
                far_hop(c, 0, here, {"fsdp": ahead}).start()
                far_hop(c, 1, here, {"fsdp": behind}).start()
        else:
            wcat_ref[...] = cat_ref[...]
        for k in range(micro):
            def body(i, _, k=k):
                at = pl.ds(pl.multiple_of(i * 128, 128), 128)
                x = tok_ref[k, at, :].astype(F32)
                r = lax.rsqrt(jnp.mean(x * x, axis=1, keepdims=True) + EPS)
                xn_s[k, pl.ds(pl.multiple_of(me * part + i * 128, 128), 128), :] = (x * r * gain1_ref[...]).astype(BF16)
                return 0

            lax.fori_loop(0, tiles, body, 0)
            if k == 0:
                c = 0
                copy("n_over", c).start()
                copy("n_side", c).start()
        if ring:
            one, two = here, here
            for k in range(1, 4):
                one, two = before_on_cycle(one), next_on_cycle(two)
                hop(2 * k - 2, one, {"fsdp": ahead}).wait_recv()
                hop(2 * k, one, {"fsdp": ahead}).start()
                hop(2 * k - 1, two, {"fsdp": behind}).wait_recv()
                if k < 3:
                    hop(2 * k + 1, two, {"fsdp": behind}).start()
        copy("n_over", 0).wait_recv()
        copy("n_far", 0).start()
        copy("n_over", 1).start()
        copy("n_side", 1).start()
        if ring:
            hop(6, before_on_cycle(one), {"fsdp": ahead}).wait_recv()
        copy("n_side", 0).wait_recv()
        copy("n_far", 0).wait_recv()
        for k in range(micro):
            keep(0, k).start()

    if ring:
        for turn in range(3 * chains):
            k, c = turn // chains + 1, turn % chains

            @pl.when(step == 2 + turn * 16 // (3 * chains))
            def _(k=k, c=c):
                one, two = along(k)
                far_hop(c, 2 * k - 2, one, {"fsdp": ahead}).wait_recv()
                far_hop(c, 2 * k - 1, two, {"fsdp": behind}).wait_recv()
                if k < 3:
                    far_hop(c, 2 * k, one, {"fsdp": ahead}).start()
                    far_hop(c, 2 * k + 1, two, {"fsdp": behind}).start()
                else:
                    far_last(c, one, two).start()

    @pl.when(step == STEPS)
    def _():
        c = 1
        copy("n_side", c).wait_recv()
        copy("n_far", c).wait_recv()

    @pl.when((t == 0) & (m < micro))
    def _():
        def body(i, _):
            at = pl.ds(pl.multiple_of(i * QB, QB), QB)
            proj = dot_nn(xn_s[m, at, :], wcat_ref[:, :cols]).astype(BF16)
            for h in range(heads):
                base = h * 3 * HEAD_DIM
                q_s[h, at, :] = proj[:, base : base + HEAD_DIM] * 0.125
                k_s[h, at, :] = proj[:, base + HEAD_DIM : base + 2 * HEAD_DIM]
                vt_s[h, :, at] = proj[:, base + 2 * HEAD_DIM : base + 3 * HEAD_DIM].T
            return 0

        lax.fori_loop(0, nq, body, 0)

    @pl.when((t > 0) & (m < micro))
    def _():
        at = t - 1
        slot = 3 - at // per
        blk = (me ^ slot) * per + at % per

        def finish(mixed_t):
            rows = pl.ds(pl.multiple_of(at % per * QB, QB), QB)
            part_s[m, slot, rows, :] = dot_nt(mixed_t.T, wcat_ref[:, cols:]).astype(BF16)

        attend_rows(blk, lo_ref.at[m], q_s, k_s, vt_s, mixed_ref.at[m], lse_ref.at[m], finish)

    for k in range(micro):
        first = k * STEPS
        c = k

        @pl.when(step == first + per)
        def _(c=c):
            copy("a_far", c).start()

        @pl.when(step == first + 2 * per)
        def _(c=c, k=k):
            copy("a_far", c).wait_recv()
            part_s[k, 2] = (part_s[k, 2].astype(F32) + side_s[k, 0].astype(F32)).astype(BF16)
            copy("b_over", c).start()
            if k == 0:
                copy("n_over", 1).wait_recv()
                copy("n_far", 1).start()
            else:
                copy("m_over", 0).wait_recv()
                copy("m_far", 0).start()

        @pl.when(step == first + 3 * per)
        def _(c=c, k=k):
            copy("a_own", c).start()
        @pl.when(step == first + 4 * per)
        def _(c=c, k=k):
            copy("a_own", c).wait_recv()
            copy("b_over", c).wait_recv()

            def body(i, _):
                at = pl.ds(pl.multiple_of(i * 128, 128), 128)
                hid = (
                    tok_ref[k, at, :].astype(F32) + part_s[k, 0, at, :].astype(F32)
                    + side_s[k, 1, at, :].astype(F32) + over_s[k, at, :].astype(F32)
                )
                hid_ref[k, at, :] = hid
                r = lax.rsqrt(jnp.mean(hid * hid, axis=1, keepdims=True) + EPS)
                moe_s[k, at, :] = (hid * r * gain2_ref[...]).astype(BF16)
                return 0

            lax.fori_loop(0, tiles, body, 0)
            copy("m_over", c).start()
            copy("m_side", c).start()
            keep(1, c).start()
            keep(2, c).start()

    def keep_near():
        return pltpu.make_async_copy(near_ref, near_out, local_sem.at[8])

    def keep_w():
        return pltpu.make_async_copy(wcat_ref, wcat_out, local_sem.at[6])

    @pl.when(step == STEPS)
    def _():
        keep_w().start()
        keep_near().start()

    @pl.when(step == 2 * STEPS)
    def _():
        c, d = 0, 1
        keep_w().wait()
        keep_near().wait()
        copy("m_over", d).wait_recv()
        copy("m_far", d).start()
        for e in (c, d):
            copy("m_side", e).wait_recv()
            copy("m_far", e).wait_recv()
            for name in NAMES:
                copy(name, e).wait_send()
            for at in range(3):
                keep(at, e).wait()
        if ring:
            one, two = here, here
            for k in range(4):
                hop(2 * k, one, {"fsdp": ahead}).wait_send()
                for c in range(chains):
                    if k < 3:
                        far_hop(c, 2 * k, one, {"fsdp": ahead}).wait_send()
                        far_hop(c, 2 * k + 1, two, {"fsdp": behind}).wait_send()
                    else:
                        far_last(c, one, two).wait_send()
                if k < 3:
                    hop(2 * k + 1, two, {"fsdp": behind}).wait_send()
                one, two = before_on_cycle(one), next_on_cycle(two)
            far_own().wait()
            for c in range(chains):
                far_last(c, one, two).wait_recv()


def forward_half(tokens, cotangent, gain1, gain2, cat, low, far, near, ring):
    micro, part, width = tokens.shape
    seq = part * 4
    wide = cat.shape[1]
    heads = wide // (4 * HEAD_DIM)
    hc = heads * HEAD_DIM
    anywhere = pl.BlockSpec(memory_space=pl.ANY)
    return pl.pallas_call(
        lambda *refs: forward_kernel(heads, ring, *refs),
        grid=(2 * STEPS + 1,),
        in_specs=[whole(tokens.shape), anywhere, whole((1, width)), whole((1, width)), whole(cat.shape), whole(low.shape), anywhere, anywhere],
        out_specs=[anywhere, anywhere, anywhere, whole((micro, hc, seq)), whole((micro, 8, seq)),
                   whole((micro, part, width)), anywhere, anywhere, anywhere],
        out_shape=[
            jax.ShapeDtypeStruct((micro, seq, width), BF16),
            jax.ShapeDtypeStruct((micro, 4, part, width), BF16),
            jax.ShapeDtypeStruct((micro, part, width), BF16),
            jax.ShapeDtypeStruct((micro, hc, seq), BF16),
            jax.ShapeDtypeStruct((micro, 8, seq), F32),
            jax.ShapeDtypeStruct((micro, part, width), F32),
            jax.ShapeDtypeStruct((width, wide), BF16),
            jax.ShapeDtypeStruct(far.shape[:2] + (width, far.shape[3]) if ring else (8, 128), BF16),
            jax.ShapeDtypeStruct(near.shape, BF16),
        ],
        scratch_shapes=[
            pltpu.VMEM((micro, seq, width), BF16),
            pltpu.VMEM((heads, seq, HEAD_DIM), BF16),
            pltpu.VMEM((heads, seq, HEAD_DIM), BF16),
            pltpu.VMEM((heads, HEAD_DIM, seq), BF16),
            pltpu.VMEM((micro, 4, part, width), BF16),
            pltpu.VMEM((micro, 2, part, width), BF16),
            pltpu.VMEM((micro, part, width), BF16),
            pltpu.VMEM((micro, part, width), BF16),
            pltpu.VMEM((width, wide), BF16),
            pltpu.SemaphoreType.DMA((31 + 7 * far.shape[0],)),
            pltpu.SemaphoreType.DMA((31 + 7 * far.shape[0],)),
            pltpu.SemaphoreType.DMA((9,)),
        ],
        compiler_params=pltpu.CompilerParams(
            dimension_semantics=("arbitrary",), vmem_limit_bytes=VMEM_LIMIT, collective_id=1, has_side_effects=True
        ),
        cost_estimate=pl.CostEstimate(flops=100_000_000_000, bytes_accessed=100_000_000, transcendentals=0),
        name="forward_half",
    )(tokens, cotangent, gain1, gain2, cat, low, far, near)


def run_copy(n, src, src_at, dst, dst_at, sem, act):
    n = pl.multiple_of(n, ROW_TILE)

    @pl.when(n > 0)
    def _():
        copy = pltpu.make_async_copy(
            src.at[pl.ds(pl.multiple_of(src_at, ROW_TILE), n), :],
            dst.at[pl.ds(pl.multiple_of(dst_at, ROW_TILE), n), :],
            sem,
        )
        if act == "start":
            copy.start()
        else:
            copy.wait()


def sort_rows(experts, tables, xs_ref, xl, sems, values):
    n_ref, lo_ref, off_ref = tables
    step = pl.program_id(0)
    slot = step % 2

    def moves(at, slot, act):
        for e in range(experts):
            run_copy(n_ref[at, e], xl.at[slot], lo_ref[at, e], xs_ref.at[e], off_ref[at, e], sems.at[slot, e], act)

    @pl.when(step >= 2)
    def _():
        moves(step - 2, slot, "wait")

    xl[slot] = values()
    moves(step, slot, "start")

    @pl.when(step == pl.num_programs(0) - 1)
    def _():
        moves(step - 1, 1 - slot, "wait")
        moves(step, slot, "wait")


def dispatch_kernel(experts, n_ref, lo_ref, off_ref, x_ref, rt_ref, pos_ref, xs_ref, meta_ref, xl, sems):
    rows = xl.shape[1]
    part = x_ref.shape[1]
    x = x_ref[0]
    logits = dot_nt(rt_ref[...], x)
    spots = pos_ref[0]
    p0, p1, r0, r1 = spots[0:1], spots[1:2], spots[2:3], spots[3:4]
    names = lax.broadcasted_iota(I32, logits.shape, 0)
    first = jnp.sum(jnp.where(names == r0, logits, 0.0), axis=0, keepdims=True)
    second = jnp.sum(jnp.where(names == r1, logits, 0.0), axis=0, keepdims=True)
    g0 = 1.0 / (1.0 + jnp.exp(second - first))
    g1 = 1.0 / (1.0 + jnp.exp(first - second))
    pick = lax.broadcasted_iota(I32, (8, part), 0)
    meta_ref[0] = jnp.where(
        pick == 0, p0.astype(F32), jnp.where(pick == 1, p1.astype(F32), jnp.where(pick == 2, g0, g1))
    )
    spot = lax.broadcasted_iota(I32, (rows, part), 0)
    plain = jnp.where((spot == p0) | (spot == p1), 1.0, 0.0).astype(BF16)
    sort_rows(experts, (n_ref, lo_ref, off_ref), xs_ref, xl, sems, lambda: dot_nn(plain, x).astype(BF16))


def gated_kernel(experts, n_ref, lo_ref, off_ref, side_ref, far_ref, own_ref, over_ref, meta_ref, gs_ref, c_s, xl, in_sems,
                 sems):
    step = pl.program_id(0)
    slot = step % 2
    rows = xl.shape[1]
    part = c_s.shape[1]

    def load(s):
        for t, ref in enumerate((side_ref, far_ref, own_ref, over_ref)):
            @pl.when(s % 4 == t)
            def _(ref=ref):
                pltpu.make_async_copy(ref.at[s // 4], c_s.at[s % 2], in_sems.at[s % 2]).start()

    @pl.when(step == 0)
    def _():
        load(step)

    @pl.when(step < pl.num_programs(0) - 1)
    def _():
        load(step + 1)

    meta = meta_ref[0]
    spot = lax.broadcasted_iota(I32, (rows, part), 0).astype(F32)
    gated = jnp.where(
        spot == meta[0:1], meta[2:3], jnp.where(spot == meta[1:2], meta[3:4], 0.0)
    ).astype(BF16)
    pltpu.make_async_copy(own_ref.at[0], c_s.at[slot], in_sems.at[slot]).wait()
    sort_rows(experts, (n_ref, lo_ref, off_ref), gs_ref, xl, sems, lambda: dot_nn(gated, c_s[slot]).astype(BF16))


def local_rows(part, experts):
    return -(-(2 * part + experts * (ROW_TILE - 1)) // 128) * 128


def dispatch(tables, xs, router_t, spots, most):
    count, part, width = xs.shape
    experts = router_t.shape[0]
    rows = local_rows(part, experts)
    spec = pltpu.PrefetchScalarGridSpec(
        num_scalar_prefetch=3,
        grid=(count,),
        in_specs=[
            pl.BlockSpec((1, part, width), lambda i, *_: (i, 0, 0)),
            whole(router_t.shape),
            pl.BlockSpec((1, 8, part), lambda i, *_: (i, 0, 0)),
        ],
        out_specs=[pl.BlockSpec(memory_space=pl.ANY), pl.BlockSpec((1, 8, part), lambda i, *_: (i, 0, 0))],
        scratch_shapes=[pltpu.VMEM((2, rows, width), BF16), pltpu.SemaphoreType.DMA((2, experts))],
    )
    return pl.pallas_call(
        lambda *refs: dispatch_kernel(experts, *refs),
        grid_spec=spec,
        out_shape=[
            jax.ShapeDtypeStruct((experts, most, width), BF16),
            jax.ShapeDtypeStruct((count, 8, part), F32),
        ],
        compiler_params=params("arbitrary"),
        cost_estimate=pl.CostEstimate(flops=20_000_000_000, bytes_accessed=20_000_000, transcendentals=0),
        name="dispatch",
    )(*tables, xs, router_t, spots)


def dispatch_gated(tables, parts, meta, experts, most, deps):
    _, part, width = parts[0].shape
    count = meta.shape[0]
    rows = local_rows(part, experts)
    anywhere = pl.BlockSpec(memory_space=pl.ANY)
    spec = pltpu.PrefetchScalarGridSpec(
        num_scalar_prefetch=3,
        grid=(count,),
        in_specs=[anywhere] * 4 + [pl.BlockSpec((1, 8, part), lambda i, *_: (i, 0, 0))] + [anywhere] * len(deps),
        out_specs=anywhere,
        scratch_shapes=[
            pltpu.VMEM((2, part, width), BF16),
            pltpu.VMEM((2, rows, width), BF16),
            pltpu.SemaphoreType.DMA((2,)),
            pltpu.SemaphoreType.DMA((2, experts)),
        ],
    )
    return pl.pallas_call(
        lambda *refs: gated_kernel(experts, *refs[:8], *refs[8 + len(deps) :]),
        grid_spec=spec,
        out_shape=jax.ShapeDtypeStruct((experts, most, width), BF16),
        compiler_params=params("arbitrary"),
        cost_estimate=pl.CostEstimate(flops=20_000_000_000, bytes_accessed=20_000_000, transcendentals=0),
        name="dispatch_gated",
    )(*tables, *parts, meta, *deps)


def live_rows(ref, c, tot):
    live = c * CHUNK + lax.broadcasted_iota(I32, ref.shape[1:], 0) < tot
    return jnp.where(live, ref[0], jnp.zeros((), BF16))


def expert_forward_kernel(e_ref, c_ref, tot_ref, steps_ref, xs_ref, w_ref, od_ref, pre_ref):
    i = pl.program_id(0)

    @pl.when(i < steps_ref[0])
    def _():
        x = live_rows(xs_ref, c_ref[i], tot_ref[e_ref[i]])
        pre = dot_nn(x, w_ref[0, 0])
        pre_ref[0] = pre
        t = jnp.tanh(GELU_A * pre * (1.0 + GELU_B * (pre * pre)))
        act = (0.5 * pre * (1.0 + t)).astype(BF16)
        od_ref[0] = dot_nt(act, w_ref[0, 1]).astype(BF16)


def expert_backward_kernel(split, e_ref, c_ref, tot_ref, steps_ref, out_ref, xs_ref, gs_ref, pre_ref, w_ref, od_ref, *refs):
    dw_refs, (din_s, dout_s) = refs[:-2], refs[-2:]
    i = pl.program_id(0)

    @pl.when(i < steps_ref[0])
    def _():
        e = e_ref[i]
        c = c_ref[i]
        tot = tot_ref[e]
        width = xs_ref.shape[2]
        x = live_rows(xs_ref, c, tot)
        g = live_rows(gs_ref, c, tot)
        pre = pre_ref[0]
        dact = dot_nn(g, w_ref[0, 1])
        square = pre * pre
        t = jnp.tanh(GELU_A * pre * (1.0 + GELU_B * square))
        half = 0.5 * (1.0 + t)
        act = pre * half
        slope = half + (0.5 * GELU_A) * pre * (1.0 - t * t) * (1.0 + (3.0 * GELU_B) * square)
        act_low = act.astype(BF16)
        dpre = (slope * dact).astype(BF16)
        od_ref[0, :, :width] = dot_nt(dpre, w_ref[0, 0]).astype(BF16)
        dot_row = jnp.sum(act * dact, axis=1, keepdims=True)
        lane = lax.broadcasted_iota(I32, (CHUNK, 128), 1)
        od_ref[0, :, width:] = jnp.where(lane == e, dot_row, 0.0).astype(BF16)
        last = (c + 1) * CHUNK >= tot

        @pl.when(c == 0)
        def _():
            din_s[...] = dot_tn(x, dpre)
            dout_s[...] = dot_tn(g, act_low)

        if split:
            @pl.when(c > 0)
            def _():
                din_s[...] += dot_tn(x, dpre)
                dout_s[...] += dot_tn(g, act_low)

            @pl.when(last)
            def _():
                count, rows = dw_refs[0].shape[2:4]
                for which, ref in enumerate(dw_refs):
                    for k in range(count):
                        at = pl.ds(pl.multiple_of(out_ref[which * count + k] * rows, rows), rows)
                        ref[0, 0, k] = din_s[at, :].astype(BF16)
                        ref[0, 1, k] = dout_s[at, :].astype(BF16)
        else:
            @pl.when((c > 0) & jnp.logical_not(last))
            def _():
                din_s[...] += dot_tn(x, dpre)
                dout_s[...] += dot_tn(g, act_low)

            @pl.when((c > 0) & last)
            def _():
                dw_refs[0][0, 0] = (din_s[...] + dot_tn(x, dpre)).astype(BF16)
                dw_refs[0][0, 1] = (dout_s[...] + dot_tn(g, act_low)).astype(BF16)

            @pl.when((c == 0) & last)
            def _():
                dw_refs[0][0, 0] = din_s[...].astype(BF16)
                dw_refs[0][0, 1] = dout_s[...].astype(BF16)


def chunk_list(first, group, totals, chunks):
    need = jnp.maximum((totals[first : first + group] + CHUNK - 1) // CHUNK, 1)
    ends = jnp.cumsum(need)
    at = jnp.minimum(jnp.arange(group * chunks, dtype=I32), ends[-1] - 1)
    which = jnp.sum((at[:, None] >= ends[None, :]).astype(I32), axis=1)
    begin = jnp.sum(jnp.where(which[:, None] == jnp.arange(group), (ends - need)[None, :], 0), axis=1)
    return which + first, at - begin, totals, ends[-1:]


def experts_forward(first, listed, xs, weights, deps=()):
    group, _, width, hidden = weights.shape
    most = xs.shape[1]
    spec = pltpu.PrefetchScalarGridSpec(
        num_scalar_prefetch=4,
        grid=(group * (most // CHUNK),),
        in_specs=[
            pl.BlockSpec((1, CHUNK, width), lambda i, e, c, *_: (e[i], c[i], 0)),
            pl.BlockSpec((1, 2, width, hidden), lambda i, e, c, *_: (e[i] - first, 0, 0, 0)),
        ] + [pl.BlockSpec(memory_space=pl.ANY)] * len(deps),
        out_specs=[
            pl.BlockSpec((1, CHUNK, width), lambda i, e, c, *_: (e[i] - first, c[i], 0)),
            pl.BlockSpec((1, CHUNK, hidden), lambda i, e, c, *_: (e[i] - first, c[i], 0)),
        ],
    )
    return pl.pallas_call(
        lambda *refs: expert_forward_kernel(*refs[:6], *refs[6 + len(deps) :]),
        grid_spec=spec,
        out_shape=[
            jax.ShapeDtypeStruct((group, most, width), BF16),
            jax.ShapeDtypeStruct((group, most, hidden), F32),
        ],
        compiler_params=params("arbitrary"),
        cost_estimate=pl.CostEstimate(flops=group * 6_000_000_000, bytes_accessed=group * 10_000_000, transcendentals=0),
        name="experts_forward",
    )(*listed, xs, weights, *deps)


def experts_backward(first, listed, xs, gs, pre, weights, out_order, split, deps=()):
    group, _, width, hidden = weights.shape
    most = xs.shape[1]
    if split:
        half = (group, 2, out_order.shape[0] // 2, width // out_order.shape[0], hidden)
        dw_shapes = [half, half]
        dw_specs = [pl.BlockSpec((1,) + half[1:], lambda i, e, c, *_: (e[i] - first, 0, 0, 0, 0))] * 2
    else:
        dw_shapes = [weights.shape]
        dw_specs = [pl.BlockSpec((1, 2, width, hidden), lambda i, e, c, *_: (e[i] - first, 0, 0, 0))]
    spec = pltpu.PrefetchScalarGridSpec(
        num_scalar_prefetch=5,
        grid=(group * (most // CHUNK),),
        in_specs=[
            pl.BlockSpec((1, CHUNK, width), lambda i, e, c, *_: (e[i], c[i], 0)),
            pl.BlockSpec((1, CHUNK, width), lambda i, e, c, *_: (e[i], c[i], 0)),
            pl.BlockSpec((1, CHUNK, hidden), lambda i, e, c, *_: (e[i] - first, c[i], 0)),
            pl.BlockSpec((1, 2, width, hidden), lambda i, e, c, *_: (e[i] - first, 0, 0, 0)),
        ] + [pl.BlockSpec(memory_space=pl.ANY)] * len(deps),
        out_specs=[pl.BlockSpec((1, CHUNK, width + 128), lambda i, e, c, *_: (e[i] - first, c[i], 0))] + dw_specs,
        scratch_shapes=[pltpu.VMEM((width, hidden), F32), pltpu.VMEM((width, hidden), F32)],
    )
    return pl.pallas_call(
        lambda *refs: expert_backward_kernel(split, *refs[:9], *refs[9 + len(deps) :]),
        grid_spec=spec,
        out_shape=[jax.ShapeDtypeStruct((group, most, width + 128), BF16)]
        + [jax.ShapeDtypeStruct(shape, BF16) for shape in dw_shapes],
        compiler_params=params("arbitrary"),
        cost_estimate=pl.CostEstimate(flops=group * 10_000_000_000, bytes_accessed=group * 10_000_000, transcendentals=0),
        name="experts_backward",
    )(*listed, out_order, xs, gs, pre, weights, *deps)


def combine_kernel(starts, gated, n_ref, lo_ref, off_ref, *refs):
    od_refs = refs[: len(starts) - 1]
    meta_ref, send_ref, keep_ref, od_l, sems = refs[-5:]
    step = pl.program_id(0)
    slot = step % 2
    rows = od_l.shape[1]
    part = meta_ref.shape[2]

    def moves(at, slot, act):
        for e in range(starts[-1]):
            group = max(i for i, s in enumerate(starts[:-1]) if s <= e)
            n, dst, src = n_ref[at, e], lo_ref[at, e], off_ref[at, e]
            run_copy(n, od_refs[group].at[e - starts[group]], src, od_l.at[slot], dst, sems.at[slot, e], act)

    @pl.when(step == 0)
    def _():
        od_l[...] = jnp.zeros_like(od_l)
        moves(0, 0, "start")

    @pl.when(step < pl.num_programs(0) - 1)
    def _():
        moves(step + 1, 1 - slot, "start")

    meta = meta_ref[0].T
    p0, p1, g0, g1 = (meta[:, i : i + 1] for i in range(4))
    spot = lax.broadcasted_iota(I32, (part, rows), 1).astype(F32)
    is0 = spot == p0
    is1 = spot == p1
    if gated:
        pick = jnp.where(is0, g0, jnp.where(is1, g1, 0.0)).astype(BF16)
    else:
        pick = jnp.where(is0 | is1, 1.0, 0.0).astype(BF16)
    moves(step, slot, "wait")
    out = dot_nn(pick, od_l[slot]).astype(BF16)

    @pl.when(step % 4 < 2)
    def _():
        send_ref[0] = out

    @pl.when(step % 4 >= 2)
    def _():
        keep_ref[0] = out


def combine(tables, ods, meta, gated, deps=()):
    starts = [0]
    for od in ods:
        starts.append(starts[-1] + od.shape[0])
    experts = starts[-1]
    wide = ods[0].shape[2]
    count, _, part = meta.shape
    rows = local_rows(part, experts)
    anywhere = pl.BlockSpec(memory_space=pl.ANY)
    spec = pltpu.PrefetchScalarGridSpec(
        num_scalar_prefetch=3,
        grid=(count,),
        in_specs=[anywhere] * (len(ods) + len(deps)) + [pl.BlockSpec((1, 8, part), lambda i, *_: (i, 0, 0))],
        out_specs=[
            pl.BlockSpec((1, part, wide), lambda i, *_: (i // 4, jnp.minimum(i % 4, 1), 0)),
            pl.BlockSpec((1, part, wide), lambda i, *_: (i // 4, jnp.maximum(i % 4 - 2, 0), 0)),
        ],
        scratch_shapes=[pltpu.VMEM((2, rows, wide), BF16), pltpu.SemaphoreType.DMA((2, experts))],
    )
    return pl.pallas_call(
        lambda *refs: combine_kernel(starts, gated, *refs),
        grid_spec=spec,
        out_shape=[jax.ShapeDtypeStruct((count // 4, 2 * part, wide), BF16)] * 2,
        compiler_params=params("arbitrary"),
        cost_estimate=pl.CostEstimate(flops=20_000_000_000, bytes_accessed=20_000_000, transcendentals=0),
        name="combine",
    )(*tables, *ods, *deps, meta)


def routing(routes, capacity, me, part):
    micro = routes.shape[0]
    experts = capacity.shape[0]
    picks = routes.reshape(micro, 4, part, 2).transpose(0, 1, 3, 2)
    names = jnp.arange(experts, dtype=I32)[:, None]
    named = picks[:, :, :, None, :] == names
    either = named[:, :, 0] | named[:, :, 1]
    earlier = jnp.arange(part)[:, None] < jnp.arange(part)[None, :]
    before = jnp.einsum("mbet,ts->mbes", either.astype(BF16), earlier.astype(BF16), preferred_element_type=F32)
    before = before.astype(I32)
    count = jnp.sum(either.astype(I32), axis=3)
    carry = jnp.cumsum(count, axis=1) - count
    kept = jnp.clip(capacity[None, None, :] - carry, 0, count)
    n = (kept + ROW_TILE - 1) // ROW_TILE * ROW_TILE
    lo = jnp.cumsum(n, axis=2) - n
    place = jnp.where(before < kept[..., None], lo[..., None] + before, -1)
    pos = jnp.max(jnp.where(named, place[:, :, None], -1), axis=3)
    order = me ^ jnp.array([1, 3, 0, 2], I32)
    spots = jnp.concatenate([pos, picks, jnp.zeros_like(pos), jnp.zeros_like(pos)], axis=2)
    spots = jnp.take(spots, order, axis=1)
    n = jnp.take(n, order, axis=1)
    lo = jnp.take(lo, order, axis=1)
    flat = n.reshape(micro * 4, experts)
    off = (jnp.cumsum(flat, axis=0) - flat).reshape(n.shape)
    return n, lo, off, jnp.sum(flat, axis=0), spots


def split_low(v):
    high = v.astype(BF16)
    return high, (v - high.astype(F32)).astype(BF16)


BACK = 34
FAR_STEPS = (3, 6, 10, 17, 20, 23, 28, 32)
BACK_NAMES = (
    "a_dx", "b_dx", "g_over", "g_side", "g_far", "p_far", "p_own", "p_over"
)


def backward_kernel(heads, ring, dxs, dxk, hid_ref, cot_ref, tok_ref, moe_ref, xn_ref,
                    gain1_ref, gain2_ref, router_ref, full_ref, w_ref, lo_ref, mixed_ref, lse_ref, wsend_ref, wkeep_ref,
                    gt_ref, cat_out, small_out, wy_ref, wz_ref, wl_ref, adx_s, bdx_s, kp_s, hid_s, cot_s, moe_s, g_s,
                    part_s, xn_s, k_s, kt_s, v_s, dqt_s, dkt_s, dvt_s, dcat_s, small_s, cat_s, caty_s, catz_s, sm_s,
                    stage_s, send_sem, recv_sem, load_sem):
    micro, part, width = tok_ref.shape
    seq = part * 4
    cols = heads * 3 * HEAD_DIM
    per = part // QB
    nq = seq // QB
    step = pl.program_id(0)
    me = lax.axis_index("tp").astype(I32)
    side = {"tp": me ^ 1}
    over = {"tp": me ^ 2}
    sems = (send_sem, recv_sem)
    mine = pl.ds(pl.multiple_of(me * part, part), part)
    theirs = pl.ds(pl.multiple_of((me ^ 2) * part, part), part)
    top, low = pl.ds(0, part), pl.ds(part, part)
    flat = pl.ds(0, width)

    def copy(name, k):
        table = {
            "a_dx": (0, dxs.at[k], adx_s.at[k], side),
            "b_dx": (1, adx_s.at[k, low], bdx_s.at[k], over),
            "g_over": (4, g_s.at[k, mine], g_s.at[k, mine], over),
            "g_side": (5, g_s.at[k, mine], g_s.at[k, mine], side),
            "g_far": (6, g_s.at[k, theirs], g_s.at[k, theirs], side),
            "p_far": (7, part_s.at[3], adx_s.at[k, top, flat], side),
            "p_own": (8, part_s.at[1], adx_s.at[k, low, flat], side),
            "p_over": (9, part_s.at[2], bdx_s.at[k, :, flat], over),
        }
        at, source, target, peer = table[name]
        return remote(source, target, sems, 10 * k + at, peer)

    def load(name, k):
        table = {
            "keep": (0, dxk.at[k], kp_s),
            "hid": (1, hid_ref.at[k], hid_s),
            "cot": (2, cot_ref.at[k], cot_s),
            "moe": (3, moe_ref.at[k, 2], moe_s),
            "xn": (4, xn_ref.at[k], xn_s),
            "tok": (2, tok_ref.at[k], cot_s),
        }
        at, source, target = table[name]
        return pltpu.make_async_copy(source, target, load_sem.at[at])

    def start(names, k):
        for name in names:
            load(name, k).start()

    def wait(names, k):
        for name in names:
            load(name, k).wait()

    def rows_of(i):
        return pl.ds(pl.multiple_of(i * 128, 128), 128)

    def half_sum(k):
        copy("a_dx", k).wait_recv()
        wait(("keep",), k)

        def body(i, _):
            at = pl.ds(pl.multiple_of(part + i * 128, 128), 128)
            adx_s[k, at, :] = (adx_s[k, at, :].astype(F32) + kp_s[at, :].astype(F32)).astype(BF16)
            return 0

        lax.fori_loop(0, part // 128, body, 0)
        copy("b_dx", k).start()

    def hidden_grad(k):
        copy("b_dx", k).wait_recv()
        wait(("hid", "cot", "moe"), k)

        def body(i, _):
            at = rows_of(i)
            total = adx_s[k, at, :].astype(F32) + kp_s[at, :].astype(F32) + bdx_s[k, at, :].astype(F32)
            products = total[:, width:]
            glog = products - full_ref[k, at, :] * jnp.sum(products, axis=1, keepdims=True)
            high, rest = split_low(glog)
            moe = moe_s[at, :]
            small_s[0:8, :] += (dot_tn(high, moe) + dot_tn(rest, moe))[0:8]
            gm = total[:, :width] + dot_nt(high, router_ref[...]) + dot_nt(rest, router_ref[...])
            hid = hid_s[at, :]
            r = lax.rsqrt(jnp.mean(hid * hid, axis=1, keepdims=True) + EPS)
            u = gm * gain2_ref[...]
            grad = cot_s[at, :].astype(F32) + r * u - hid * (r * r * r * jnp.mean(u * hid, axis=1, keepdims=True))
            small_s[16:24, :] += jnp.sum((gm * hid * r).reshape(16, 8, width), axis=0)
            g_s[k, pl.ds(pl.multiple_of(me * part + i * 128, 128), 128), :] = grad.astype(BF16)
            return 0

        lax.fori_loop(0, part // 128, body, 0)
        copy("b_dx", k).wait_send()
        copy("g_over", k).start()
        copy("g_side", k).start()

    def token_grad(k):
        copy("p_own", k).wait_recv()
        copy("p_over", k).wait_recv()
        wait(("tok",), k)

        def body(i, _):
            at = rows_of(i)
            gn = (
                part_s[0, at, :].astype(F32)
                + adx_s[k, pl.ds(pl.multiple_of(part + i * 128, 128), 128), flat].astype(F32)
                + bdx_s[k, at, flat].astype(F32)
            )
            x = cot_s[at, :].astype(F32)
            r = lax.rsqrt(jnp.mean(x * x, axis=1, keepdims=True) + EPS)
            w = gn * gain1_ref[...]
            back = r * w - x * (r * r * r * jnp.mean(w * x, axis=1, keepdims=True))
            mine_at = pl.ds(pl.multiple_of(me * part + i * 128, 128), 128)
            gt_ref[k, at, :] = (g_s[k, mine_at, :].astype(F32) + back).astype(BF16)
            return 0

        lax.fori_loop(0, part // 128, body, 0)

    if ring:
        here = lax.axis_index("fsdp").astype(I32)
        pair = {"fsdp": here ^ 1}
        line = [{"fsdp": here ^ (2 * k)} for k in range(1, 4)]
        tp_peers = [{"tp": me ^ k} for k in range(1, 4)]

        def extra(name, k=0):
            table = {
                "cat_y": (20, lambda: (cat_s, caty_s, pair)),
                "cat_z": (21 + k, lambda: (cat_s.at[k + 1], catz_s.at[k], line[k])),
                "sm_tp": (24 + k, lambda: (small_s, sm_s.at[k], tp_peers[k])),
                "sm_y": (27, lambda: (small_s, sm_s.at[3], pair)),
                "sm_z": (28 + k, lambda: (small_s, sm_s.at[4 + k], line[k])),
            }
            at, parts = table[name]
            return remote(*parts()[:2], sems, at, parts()[2])

        pieces_w = wy_ref.shape[0]

        def far_y(i):
            return remote(wsend_ref.at[i], wy_ref.at[i], sems, 31 + i, pair)

        def far_z(i, k):
            return remote(wz_ref.at[i, k + 1], wl_ref.at[k, i], sems, 31 + pieces_w + 3 * i + k, line[k])

        def far_load(i, which):
            source = wkeep_ref.at[i] if which == 0 else wy_ref.at[i]
            return pltpu.make_async_copy(source, stage_s.at[which], load_sem.at[8 + which])

        def far_store(i):
            return pltpu.make_async_copy(stage_s.at[2], wz_ref.at[i], load_sem.at[10])

        def far_first(i):
            far_y(i).wait_recv()
            if i + 4 < pieces_w:
                far_y(i + 4).start()
            far_load(i, 0).start()
            far_load(i, 1).start()

        def far_second(i):
            far_load(i, 0).wait()
            far_load(i, 1).wait()
            for k in range(4):
                stage_s[2, k] = (stage_s[0, k].astype(F32) + stage_s[1, k].astype(F32)).astype(BF16)
            far_store(i).start()

        def far_third(i):
            far_store(i).wait()
            for k in range(3):
                far_z(i, k).start()

    def far_piece(i):
        if ring and i < wy_ref.shape[0]:
            far_first(i)
            far_second(i)
            far_third(i)

    @pl.when(step == 0)
    def _():
        peers = [side, over]
        if ring:
            peers += [pair] + line + [tp_peers[2]]
        greet(peers)
        copy("a_dx", 0).start()
        start(("keep", "hid", "cot", "moe", "xn"), 0)
        dcat_s[...] = jnp.zeros_like(dcat_s)
        small_s[...] = jnp.zeros_like(small_s)
        dkt_s[...] = jnp.zeros_like(dkt_s)
        dvt_s[...] = jnp.zeros_like(dvt_s)
        half_sum(0)
        copy("a_dx", 1).start()
        if ring:
            for i in range(min(4, pieces_w)):
                far_y(i).start()
        far_piece(0)
        hidden_grad(0)
        start(("keep", "hid", "cot", "moe"), 1)
        far_piece(1)
        far_piece(2)
        copy("g_over", 0).wait_recv()
        copy("g_far", 0).start()
        half_sum(1)
        far_piece(3)
        copy("g_side", 0).wait_recv()
        copy("g_far", 0).wait_recv()
        wait(("xn",), 0)

    def attend(m, blk):
        rows = pl.ds(pl.multiple_of(blk * QB, QB), QB)
        most = WINDOW // QB + 1

        def window(nk):
            begin = pl.multiple_of((blk - (nk - 1)) * QB, QB)
            keys = pl.ds(begin, nk * QB)
            proj = dot_nn(xn_s[rows, :], w_ref[:, :cols]).astype(BF16)
            g = g_s[m, rows, :]
            gm_t = dot_nn(g, w_ref[:, cols:]).astype(BF16).T
            mixed_t = mixed_ref[m, :, rows]
            dcat_s[cols:, :] += dot_nn(mixed_t, g)
            prod = gm_t.astype(F32) * mixed_t.astype(F32)
            lo = lo_ref[m, :, rows]
            kpos = begin + lax.broadcasted_iota(I32, (nk * QB, QB), 0)
            qpos = blk * QB + lax.broadcasted_iota(I32, (QB, QB), 1)
            for h in range(heads):
                base = h * 3 * HEAD_DIM
                at = slice(h * HEAD_DIM, (h + 1) * HEAD_DIM)
                q = proj[:, base : base + HEAD_DIM] * 0.125
                k_new = proj[:, base + HEAD_DIM : base + 2 * HEAD_DIM]
                k_s[h, rows, :] = k_new
                kt_s[h, :, rows] = k_new.T
                v_s[h, rows, :] = proj[:, base + 2 * HEAD_DIM : base + 3 * HEAD_DIM]
                drow = jnp.sum(prod[at], axis=0, keepdims=True)
                s = dot_nt(k_s[h, keys, :], q)
                s = jnp.where(kpos >= lo, s, NEG)
                last = jnp.where(kpos[(nk - 1) * QB :] <= qpos, s[(nk - 1) * QB :], NEG)
                s = last if nk == 1 else jnp.concatenate([s[: (nk - 1) * QB], last], axis=0)
                p = jnp.exp(s - lse_ref[m, h : h + 1, rows])
                dp = dot_nn(v_s[h, keys, :], gm_t[at])
                ds = (p * (dp - drow)).astype(BF16)
                dvt_s[h, :, keys] += dot_nt(gm_t[at], p.astype(BF16))
                dkt_s[h, :, keys] += dot_nt(q.T, ds)
                dqt_s[h, :, rows] = (dot_nn(kt_s[h, :, keys], ds) * 0.125).astype(BF16)

        for nk in range(1, most + 1):
            cond = (blk == nk - 1) if nk < most else (blk >= most - 1)

            @pl.when(cond)
            def _(nk=nk):
                window(nk)

    def finalize(m, at):
        slot = 3 - at // per
        blk = (me ^ slot) * per + at % per
        rows = pl.ds(pl.multiple_of(blk * QB, QB), QB)
        pieces = []
        for h in range(heads):
            pieces += [dqt_s[h, :, rows], dkt_s[h, :, rows].astype(BF16), dvt_s[h, :, rows].astype(BF16)]
            dkt_s[h, :, rows] = jnp.zeros((HEAD_DIM, QB), F32)
            dvt_s[h, :, rows] = jnp.zeros((HEAD_DIM, QB), F32)
        dproj_t = jnp.concatenate(pieces, axis=0)
        x = xn_s[rows, :]
        dcat_s[:cols, :] += dot_nn(dproj_t, x)
        gn = dot_nt(dproj_t.T, w_ref[:, :cols])
        small_s[8:16, :] += jnp.sum((gn * x.astype(F32)).reshape(QB // 8, 8, width), axis=0)
        part_s[slot, pl.ds(pl.multiple_of(at % per * QB, QB), QB), :] = gn.astype(BF16)

    phase = (step - 1) // nq
    m_now = phase // 2

    @pl.when((step > 0) & (step < BACK - 1) & (phase % 2 == 0))
    def _():
        attend(m_now, (step - 1) % nq)

    @pl.when((step > 0) & (step < BACK - 1) & (phase % 2 == 1))
    def _():
        finalize(m_now, (step - 1) % nq)

    def event(at):
        return pl.when(step == at)

    if ring:
        for i, first in zip(range(4, pieces_w), FAR_STEPS):
            @event(first)
            def _(i=i):
                far_first(i)

            @event(first + 1)
            def _(i=i):
                far_second(i)

            @event(min(first + 2, BACK - 1))
            def _(i=i):
                far_third(i)

    @event(5)
    def _():
        hidden_grad(1)

    @event(10)
    def _():
        copy("g_over", 1).wait_recv()
        copy("g_far", 1).start()

    for k in range(micro):
        first = 16 * k + nq

        @event(first + per)
        def _(k=k):
            copy("p_far", k).start()

        @event(first + 2 * per)
        def _(k=k):
            copy("p_far", k).wait_recv()

            def body(i, _):
                at = rows_of(i)
                part_s[2, at, :] = (part_s[2, at, :].astype(F32) + adx_s[k, at, flat].astype(F32)).astype(BF16)
                return 0

            lax.fori_loop(0, part // 128, body, 0)
            copy("p_over", k).start()

        @event(first + 3 * per)
        def _(k=k):
            copy("p_own", k).start()

    @event(16)
    def _():
        start(("xn",), 1)
        copy("g_side", 1).wait_recv()
        copy("g_far", 1).wait_recv()
        start(("tok",), 0)
        wait(("xn",), 1)

    @event(20)
    def _():
        token_grad(0)
        start(("tok",), 1)
        for name in ("p_far", "p_own", "p_over"):
            copy(name, 0).wait_send()

    @event(BACK - 1)
    def _():
        if ring:
            dcat = dcat_s[...].T
            dcat_s[...] = dcat
            rows = width // 8
            y, z = here % 2, here // 2

            def block(k, parity):
                at = pl.multiple_of((2 * (z ^ k) + parity) * rows, rows)
                return dcat_s[pl.ds(at, rows), :]

            for k in range(4):
                cat_s[k] = block(k, 1 - y).astype(BF16)
            extra("cat_y").start()
            for k in range(3):
                extra("sm_tp", k).start()
            extra("cat_y").wait()
            for k in range(4):
                cat_s[k] = (block(k, y) + caty_s[k].astype(F32)).astype(BF16)
            for k in range(3):
                extra("cat_z", k).start()
            for k in range(3):
                extra("sm_tp", k).wait()
            small_s[...] = (small_s[...] + sm_s[0]) + (sm_s[1] + sm_s[2])
            extra("sm_y").start()
            extra("sm_y").wait()
            small_s[...] += sm_s[3]
            for k in range(3):
                extra("sm_z", k).start()
            for k in range(3):
                extra("sm_z", k).wait()
            small_out[...] = (small_s[...] + sm_s[4]) + (sm_s[5] + sm_s[6])
            for k in range(3):
                extra("cat_z", k).wait()
            token_grad(1)
            cat_out[...] = (
                cat_s[0].astype(F32) + catz_s[0].astype(F32) + catz_s[1].astype(F32) + catz_s[2].astype(F32)
            )
        else:
            token_grad(1)
            small_out[...] = small_s[...]
            cat_out[...] = dcat_s[...].T
        if ring:
            for i in range(pieces_w):
                far_y(i).wait_send()
                for k in range(3):
                    far_z(i, k).wait()
        for k in range(micro):
            for name in BACK_NAMES:
                if name != "b_dx" and not (k == 0 and name in ("p_far", "p_own", "p_over")):
                    copy(name, k).wait_send()


def backward_half(dxs, dxk, hidden, cotangent, tokens, moe, xn, gain1, gain2, router, full, w_cat, low, mixed_t,
                  lse, wsend, wkeep, ring, deps=()):
    micro, part, width = tokens.shape
    seq = part * 4
    wide = w_cat.shape[1]
    heads = wide // (4 * HEAD_DIM)
    hc = heads * HEAD_DIM
    dxw = dxs.shape[2]
    pieces, block = (wsend.shape[0], wsend.shape[1:]) if ring else (1, (8, 128))
    anywhere = pl.BlockSpec(memory_space=pl.ANY)

    def once(shape):
        zeros = (0,) * len(shape)
        return pl.BlockSpec(shape, lambda *_: zeros, pipeline_mode=pl.Buffered(1))

    cat_shape = (width // 8, wide) if ring else (width, wide)
    return pl.pallas_call(
        lambda *refs: backward_kernel(heads, ring, *refs[:17], *refs[17 + len(deps) :]),
        grid=(BACK,),
        in_specs=[anywhere] * 7 + [
            once((1, width)), once((1, width)), once(router.shape), once(full.shape), once(w_cat.shape), once(low.shape),
            once(mixed_t.shape), once(lse.shape),
        ] + [anywhere] * (2 + len(deps)),
        out_specs=[once((micro, part, width)), once(cat_shape), once((24, width))] + [anywhere] * 3,
        out_shape=[
            jax.ShapeDtypeStruct((micro, part, width), BF16),
            jax.ShapeDtypeStruct(cat_shape, F32),
            jax.ShapeDtypeStruct((24, width), F32),
            jax.ShapeDtypeStruct((pieces,) + block, BF16),
            jax.ShapeDtypeStruct((pieces,) + block, BF16),
            jax.ShapeDtypeStruct((3, pieces) + block[1:], BF16),
        ],
        scratch_shapes=[
            pltpu.VMEM((micro, 2 * part, dxw), BF16),
            pltpu.VMEM((micro, part, dxw), BF16),
            pltpu.VMEM((2 * part, dxw), BF16),
            pltpu.VMEM((part, width), F32),
            pltpu.VMEM((part, width), BF16),
            pltpu.VMEM((part, width), BF16),
            pltpu.VMEM((micro, seq, width), BF16),
            pltpu.VMEM((4, part, width), BF16),
            pltpu.VMEM((seq, width), BF16),
            pltpu.VMEM((heads, seq, HEAD_DIM), BF16),
            pltpu.VMEM((heads, HEAD_DIM, seq), BF16),
            pltpu.VMEM((heads, seq, HEAD_DIM), BF16),
            pltpu.VMEM((heads, HEAD_DIM, seq), BF16),
            pltpu.VMEM((heads, HEAD_DIM, seq), F32),
            pltpu.VMEM((heads, HEAD_DIM, seq), F32),
            pltpu.VMEM((wide, width), F32),
            pltpu.VMEM((24, width), F32),
            pltpu.VMEM((4, width // 8, wide), BF16),
            pltpu.VMEM((4, width // 8, wide), BF16),
            pltpu.VMEM((3, width // 8, wide), BF16),
            pltpu.VMEM((7, 24, width), F32),
            pltpu.VMEM((3,) + block, BF16),
            pltpu.SemaphoreType.DMA((31 + 4 * pieces,)),
            pltpu.SemaphoreType.DMA((31 + 4 * pieces,)),
            pltpu.SemaphoreType.DMA((11,)),
        ],
        compiler_params=pltpu.CompilerParams(
            dimension_semantics=("arbitrary",), vmem_limit_bytes=60 * 1024 * 1024, collective_id=2, has_side_effects=True
        ),
        cost_estimate=pl.CostEstimate(flops=150_000_000_000, bytes_accessed=100_000_000, transcendentals=0),
        name="backward_half",
    )(dxs, dxk, hidden, cotangent, tokens, moe, xn, gain1, gain2, router, full, w_cat, low, mixed_t, lse, wsend, wkeep, *deps)


def local(tokens, cotangent, gain_attn, gain_moe, qkv_weight, out_weight, router, w_in, w_out, doc_lengths, routes,
          capacity):
    micro, part, width = tokens.shape
    seq = part * 4
    experts = w_in.shape[0]
    n_fsdp = lax.axis_size("fsdp")
    ring = n_fsdp == 8
    me = lax.axis_index("tp").astype(I32)
    most = -(-micro * (CAP + 4 * ROW_TILE) // CHUNK) * CHUNK
    cat = jnp.concatenate([qkv_weight, out_weight.T], axis=1)
    w_pair = jnp.stack([w_in, w_out.transpose(0, 2, 1)], axis=1)
    if ring:
        row_index = lax.axis_index("fsdp").astype(I32)
        near = 2 * ((row_index // 2) ^ jnp.arange(4, dtype=I32))
        out_order = jnp.concatenate([near + row_index % 2, near + (1 - row_index % 2)])
    else:
        cat = lax.all_gather(cat, "fsdp", axis=0, tiled=True)
        out_order = jnp.zeros((1,), I32)
    near, far = w_pair[:NEAR], w_pair[NEAR:]

    n, lo_at, off, totals, spots = routing(routes, capacity, me, part)
    places = jnp.arange(seq, dtype=I32)
    ends = jnp.cumsum(doc_lengths.reshape(micro, -1), axis=1)
    begins = ends - doc_lengths.reshape(micro, -1)
    doc_start = jnp.max(jnp.where(places >= begins[:, :, None], begins[:, :, None], 0), axis=1)
    low = jnp.maximum(doc_start, places - (WINDOW - 1)).astype(I32)
    router_t = router.T

    low = low[:, None, :]
    xn, moe, cot, mixed_t, lse, hidden, w_cat, w_far, near = forward_half(
        tokens, cotangent, gain_attn[None], gain_moe[None], cat, low, far, near, ring
    )
    w_near = lax.all_gather(near, "fsdp", axis=2, tiled=True)
    if not ring:
        w_far = lax.all_gather(far, "fsdp", axis=2, tiled=True)
    core, chip = [(i, i ^ 1) for i in range(4)], [(i, i ^ 2) for i in range(4)]
    cot_over = lax.ppermute(cot, "tp", chip)
    cot_side = lax.ppermute(cot, "tp", core)
    cot_far = lax.ppermute(cot_over, "tp", core)
    blocks = micro * 4
    tables = tuple(table.reshape(blocks, experts) for table in (n, lo_at, off))
    xs, meta = dispatch(tables, moe.reshape(blocks, part, width), router_t, spots.reshape(blocks, 8, part), most)
    list_near = chunk_list(0, NEAR, totals, most // CHUNK)
    list_far = chunk_list(NEAR, experts - NEAR, totals, most // CHUNK)
    fwd_far, pre_far = experts_forward(NEAR, list_far, xs, w_far)
    fwd_near, pre_near = experts_forward(0, list_near, xs, w_near, (fwd_far,))
    out_send, out_keep = combine(tables, (fwd_near, fwd_far), meta, True)
    gs = dispatch_gated(tables, (cot_side, cot_far, cot, cot_over), meta, experts, most, (out_keep,))
    out_got = lax.ppermute(out_send, "tp", core)
    out_both = out_keep.astype(F32) + out_got.astype(F32)
    out_away = lax.ppermute(out_both[:, part:].astype(BF16), "tp", chip)
    output = (hidden + out_both[:, :part] + out_away.astype(F32)).astype(BF16)
    back_near, dw_near = experts_backward(0, list_near, xs, gs, pre_near, w_near, out_order, False)
    dw_near = lax.psum_scatter(dw_near, "fsdp", scatter_dimension=2, tiled=True).astype(F32)
    back_far, *dw_far = experts_backward(NEAR, list_far, xs, gs, pre_far, w_far, out_order, ring, (back_near, out_both))
    if ring:
        wkeep, wsend = (d.reshape((-1,) + d.shape[2:]) for d in dw_far)
    else:
        dw_far = lax.psum_scatter(dw_far[0], "fsdp", scatter_dimension=2, tiled=True).astype(F32)
        wkeep = wsend = jnp.zeros((8, 128), BF16)

    lanes = jnp.arange(128, dtype=I32)
    mine = lax.dynamic_slice_in_dim(routes, me * part, part, 1)
    gates = meta.reshape(micro, 4, 8, part)[:, 2, 2:4]
    full = jnp.sum(jnp.where(mine[..., None] == lanes, gates.transpose(0, 2, 1)[..., None], 0.0), axis=2)
    router_wide = jnp.pad(router, ((0, 0), (0, 128 - experts)))
    dxs, dxk = combine(tables, (back_near, back_far), meta, False)
    grad_tokens, grad_cat, small, _, wz, wl = backward_half(
        dxs, dxk, hidden, cotangent, tokens, moe, xn, gain_attn[None], gain_moe[None], router_wide, full, w_cat, low, mixed_t,
        lse, wsend, wkeep, ring, (output,)
    )
    cols = qkv_weight.shape[1]
    if not ring:
        grad_cat = lax.psum_scatter(grad_cat.astype(BF16), "fsdp", scatter_dimension=0, tiled=True).astype(F32)
        small = lax.psum(small, ("fsdp", "tp"))
    if ring:
        dw_far = (wz[:, 0].astype(F32) + wl[0].astype(F32)) + (wl[1].astype(F32) + wl[2].astype(F32))
        dw_far = dw_far.reshape((experts - NEAR, 2) + dw_far.shape[1:])
    dw = jnp.concatenate([dw_near, dw_far], axis=0)
    return (
        output,
        grad_tokens,
        jnp.sum(small[8:16], axis=0) / gain_attn,
        jnp.sum(small[16:24], axis=0),
        grad_cat[:, :cols],
        grad_cat[:, cols:].T,
        small[:8].T,
        dw[:, 0],
        dw[:, 1].transpose(0, 2, 1),
    )


def solution(mesh):
    rows = P(None, ("fsdp", "tp"), None)
    in_specs = (
        rows,
        rows,
        P(),
        P(),
        P("fsdp", "tp"),
        P("tp", "fsdp"),
        P(),
        P(None, "fsdp", "tp"),
        P(None, "tp", "fsdp"),
        P(None, "fsdp", None),
        P(None, "fsdp", None),
        P(),
    )
    out_specs = (
        rows,
        rows,
        P(),
        P(),
        P("fsdp", "tp"),
        P("tp", "fsdp"),
        P(),
        P(None, "fsdp", "tp"),
        P(None, "tp", "fsdp"),
    )
    return jax.shard_map(local, mesh=mesh, in_specs=in_specs, out_specs=out_specs, check_vma=False)
```

time: 832 us -> 681 us (0.82)
  waiting for transfers between devices: 219 us -> 2.95 us
  Pallas kernels: 433 us -> 602 us
  other arithmetic: 62.2 us -> 28.2 us
  local copies, waits for them, and re-layouts: 48.5 us -> 18.5 us
  starting transfers between devices: 28.8 us -> 4.81 us
  matrix products: 9.65 us -> 0.21 us
    pallas_call x10 -> x9, Pallas kernels: 271 us -> 433 us  [the longest x1 209 us: backward_half(): pl.pallas_call(lambda *refs: backward_kernel(heads, ring, *refs[:17], *re...]
    ppermute x35 -> x5, waiting for transfers between devices: 160 us -> 0.01 us  [the longest x1 0.01 us: local(): out_got = lax.ppermute(out_send, 'tp', core)]
    all_gather x4 -> x1, waiting for transfers between devices: 57.7 us -> 2.88 us  [local(): w_near = lax.all_gather(near, 'fsdp', axis=2, tiled=True)]
    ppermute x35 -> x5, starting transfers between devices: 28.3 us -> 4.55 us  [the longest x1 2.7 us: local(): cot_over = lax.ppermute(cot, 'tp', chip)]
    another operation x7 -> x3, other arithmetic: 18 us -> 0.44 us
    add x17 -> x5, other arithmetic: 18.3 us -> 7.11 us  [the longest x1 3.54 us: local(): out_both = out_keep.astype(F32) + out_got.astype(F32)]
    dot_general x4 -> x0, matrix products: 9.45 us -> none  [the longest x2 6.01 us: local(): jnp.einsum('te,de->td', grad_logits, router_float, precision=lax.Precisio...]
  transfers between devices with their start and end apart: 41 -> 7, of which waited for: 14 -> 1; matrix products, arithmetic and copies ran while one was open for 12% -> 5% of each run, Pallas kernels for 53% -> 64%
where the time goes in v3:
time: 681 us; the launch traced here: 673 us
  Pallas kernels  602 us (88%)
  other arithmetic  28.2 us (4%)
  local copies, waits for them, and re-layouts  18.5 us (3%)
  between operations  16.1 us (2%)
    pallas_call x1, Pallas kernels, backward_half(): pl.pallas_call(lambda *refs: backward_kernel(heads, ring, *refs[:17], *re...  209 us
    pallas_call x1, Pallas kernels, forward_half(): pl.pallas_call(lambda *refs: forward_kernel(heads, ring, *refs), grid=(2...  169 us
    pallas_call x2, Pallas kernels, experts_backward(): pl.pallas_call(lambda *refs: expert_backward_kernel(split, *refs[:9], *re...  86.5 us
    pallas_call x2, Pallas kernels, experts_forward(): pl.pallas_call(lambda *refs: expert_forward_kernel(*refs[:6], *refs[6 + l...  54.9 us
    pallas_call x2, Pallas kernels, combine(): pl.pallas_call(lambda *refs: combine_kernel(starts, gated, *refs), grid_s...  43.8 us
    pallas_call x1, Pallas kernels, dispatch(): pl.pallas_call(lambda *refs: dispatch_kernel(experts, *refs), grid_spec=s...  21.8 us
    pallas_call x1, Pallas kernels, dispatch_gated(): pl.pallas_call(lambda *refs: gated_kernel(experts, *refs[:8], *refs[8 + l...  16.7 us
  transfers between devices with their start and end apart: 7, of which 1 were waited for; matrix products, arithmetic and copies ran while one was open for 5% of the time, Pallas kernels for 64%

profile of v3, /device:TPU:0, one launch (start us, length us, event | category | flops | bytes accessed | tf_op | source)
XLA Modules:
  0.0 672.5 jit_solution(9143556128466442935)
XLA Ops:
  7.3 3.0 fusion.5.refs_6_
  14.1 168.9 %forward_half.1 = (bf16[2,2048,768]{2,1,0:T(8,128)(2,1)}, bf16[2,4,512,768]{3,2,1,0:T(8,128)(2,1)}, bf16[2,512,768]{2,1,0:T(8,128)(2,1)}, bf16[2,192,2048]{2,1,0...) custom-call(bf16[2,512,768]{2,1,0:T(8,128)(2,1)} %refs_4_.1, ...), custom_call_target="tpu_custom_call" | custom-call | flops 99999997952 | bytes 100000000 | tf_op jit(solution)/shard_map/forward_half/pallas_call | solution.py:376
  183.1 2.7 collective-permute-start.3
  194.2 21.8 %dispatch.1 = (bf16[8,1792,768]{2,1,0:T(8,128)(2,1)}, f32[8,8,512]{2,1,0:T(8,128)}) custom-call(s32[8,8]{1,0:T(8,128)} %bitcast.84, s32[8,8]{1,0:T(8,128)} %bitcast.91, s32[8,8]{1,0:T(8,128)} %sub.114.refs_2_, bf16[8,512,768]{2,1,0:T(8,128)(2,1)} %bitcast.98, bf16[8,768]{1,0:T(8,128)(2,1)} %bitcast.88, s32[8,8,512]{2,1,0:T(8,128)} %bitcast_select_fusion.refs_5_), custom_call_target="tpu_custom_call" | custom-call | flops 20000000000 | bytes 20000000 | tf_op jit(solution)/shard_map/dispatch/pallas_call | solution.py:523
  216.0 40.1 %experts_forward.2 = (bf16[6,1792,768]{2,1,0:T(8,128)(2,1)}, f32[6,1792,768]{2,1,0:T(8,128)}) custom-call(s32[42]{0:T(128)} %get-tuple-element.115.refs_0_, s32[42]{0:T(128)} %get-tuple-element.116.refs_1_, s32[8]{0:T(128)} %copy-done.19, s32[1]{0:T(128)} %bitcast.26.refs_3_, bf16[8,1792,768]{2,1,0:T(8,128)(2,1)} %get-tuple-element.41.refs_4_.refs_5_, ...), custom_call_target="tpu_custom_call" | custom-call | flops 35999997952 | bytes 60000000 | tf_op jit(solution)/shard_map/experts_forward/pallas_call | solution.py:668
  260.1 1.5 select_reduce_fusion.refs_10_
  262.4 2.9 all-gather.2.cloned.1.call-done.refs_5_.refs_8_
  265.3 14.8 %experts_forward.3 = (bf16[2,1792,768]{2,1,0:T(8,128)(2,1)}, f32[2,1792,768]{2,1,0:T(8,128)}) custom-call(s32[14]{0:T(128)} %copy-done.24, s32[14]{0:T(128)} %fusion.22.refs_1_, s32[8]{0:T(128)} %copy-done.19, s32[1]{0:T(128)} %bitcast.15.refs_3_, bf16[8,1792,768]{2,1,0:T(8,128)(2,1)} %get-tuple-element.41.refs_4_.refs_5_, ...), custom_call_target="tpu_custom_call" | custom-call | flops 12000000000 | bytes 20000000 | tf_op jit(solution)/shard_map/experts_forward/pallas_call | solution.py:668
  280.2 20.5 %combine.2 = (bf16[2,1024,768]{2,1,0:T(8,128)(2,1)}, bf16[2,1024,768]{2,1,0:T(8,128)(2,1)}) custom-call(s32[8,8]{1,0:T(8,128)} %bitcast.85, s32[8,8]{1,0:T(8,128)} %bitcast.92, s32[8,8]{1,0:T(8,128)} %sub.114.refs_2_, bf16[2,1792,768]{2,1,0:T(8,128)(2,1)} %get-tuple-element.45.refs_3_, bf16[6,1792,768]{2,1,0:T(8,128)(2,1)} %get-tuple-element.44.refs_6_.refs_4_, ...), custom_call_target="tpu_custom_call" | custom-call | flops 20000000000 | bytes 20000000 | tf_op jit(solution)/shard_map/combine/pallas_call | solution.py:777
  301.9 16.7 %dispatch_gated.1.refs_6_ = bf16[8,1792,768]{2,1,0:T(8,128)(2,1)} custom-call(s32[8,8]{1,0:T(8,128)} %bitcast.86, s32[8,8]{1,0:T(8,128)} %bitcast.93, s32[8,8]{1,0:T(8,128)} %sub.114.refs_2_, bf16[2,512,768]{2,1,0:T(8,128)(2,1)} %collective-permute-done.2.refs_3_, bf16[2,512,768]{2,1,0:T(8,128)(2,1)} %copy-done.23, ...), custom_call_target="tpu_custom_call" | custom-call | flops 20000000000 | bytes 20000000 | tf_op jit(solution)/shard_map/dispatch_gated/pallas_call | solution.py:553
  318.7 22.9 %experts_backward.2 = (bf16[2,1792,896]{2,1,0:T(8,128)(2,1)}, bf16[2,2,768,768]{3,2,1,0:T(8,128)(2,1)}) custom-call(s32[14]{0:T(128)} %copy-done.24, s32[14]{0:T(128)} %fusion.22.refs_1_, s32[8]{0:T(128)} %copy-done.19, s32[1]{0:T(128)} %bitcast.15.refs_3_, s32[8]{0:T(128)} %pad_add_fusion.refs_4_, bf16[8,1792,768]{2,1,0:T(8,128)(2,1)} %get-tuple-element.41.refs_4_.refs_5_, ...), custom_call_target="tpu_custom_call" | custom-call | flops 20000000000 | bytes 20000000 | tf_op jit(solution)/shard_map/experts_backward/pallas_call | solution.py:703
  341.6 3.5 convert_add_fusion.refs_10_
  345.1 1.4 slice.153
  346.5 1.4 collective-permute-start.1
  348.3 63.7 %experts_backward.3 = (bf16[6,1792,896]{2,1,0:T(8,128)(2,1)}, bf16[6,2,4,96,768]{4,3,2,1,0:T(8,128)(2,1)}, bf16[6,2,4,96,768]{4,3,2,1,0:T(8,128)(2,1)}) custom-call(s32[42]{0:T(128)} %get-tuple-element.115.refs_0_, s32[42]{0:T(128)} %get-tuple-element.116.refs_1_, s32[8]{0:T(128)} %copy-done.19, s32[1]{0:T(128)} %bitcast.26.refs_3_, s32[8]{0:T(128)} %pad_add_fusion.refs_4_, ...), custom_call_target="tpu_custom_call" | custom-call | flops 60000002048 | bytes 60000000 | tf_op jit(solution)/shard_map/experts_backward/pallas_call | solution.py:703
  412.0 23.3 %combine.3 = (bf16[2,1024,896]{2,1,0:T(8,128)(2,1)}, bf16[2,1024,896]{2,1,0:T(8,128)(2,1)}) custom-call(s32[8,8]{1,0:T(8,128)} %bitcast.87, s32[8,8]{1,0:T(8,128)} %bitcast.94, s32[8,8]{1,0:T(8,128)} %sub.114.refs_2_, bf16[2,1792,896]{2,1,0:T(8,128)(2,1)} %get-tuple-element.51.refs_9_.refs_3_, bf16[6,1792,896]{2,1,0:T(8,128)(2,1)} %get-tuple-element.53.refs_4_, ...), custom_call_target="tpu_custom_call" | custom-call | flops 20000000000 | bytes 20000000 | tf_op jit(solution)/shard_map/combine/pallas_call | solution.py:777
  435.3 3.6 fusion.1.refs_17_
  438.9 209.0 %backward_half.1 = (bf16[2,512,768]{2,1,0:T(8,128)(2,1)}, f32[96,768]{1,0:T(8,128)}, f32[24,768]{1,0:T(8,128)}, bf16[12,4,96,768]{3,2,1,0:T(8,128)(2,1)}, bf16[1...) custom-call(bf16[2,1024,896]{2,1,0:T(8,128)(2,1)} %get-tuple-element.54.refs_0_, ...), custom_call_target="tpu_custom_call" | custom-call | flops 149999992832 | bytes 100000000 | tf_op jit(solution)/shard_map/backward_half/pallas_call | solution.py:1234
  647.9 2.8 slice.94
  650.8 2.8 slice.93
  655.1 1.2 slice_reduce_fusion
  657.0 2.6 convert_add_fusion.1
  660.5 3.8 fusion.4
  664.4 1.1 copy.97
  (129 shorter events, 20.3 us)
Async XLA Ops:
  7.2 258.1 %all-gather.2.cloned.1.call-start = ((), (), s32[]{:S(2)}) async-start(), calls=%async_computation.1 | async-start | bytes 5308416 | tf_op jit(solution)/shard_map/all_gather | solution.py:1317
  7.3 4.2 copy-start.13
  7.3 4.8 copy-start.16
  7.3 5.4 copy-start.11
  7.3 6.1 copy-start.9
  14.1 172.0 %copy-start.8 = (s32[2,2048,2]{1,2,0:T(2,128)S(1)}, s32[2,2048,2]{1,2,0:T(2,128)}, u32[]{:S(2)}) copy-start(s32[2,2048,2]{1,2,0:T(2,128)} %param.25) | copy-start | bytes 98308
  14.1 172.3 %copy-start.21 = (s32[4]{0:T(128)S(1)}, s32[4]{0:T(128)}, u32[]{:S(2)}) copy-start(s32[4]{0:T(128)} %constant.151.clone) | copy-start | bytes 52
  14.1 172.3 %copy-start.18 = (s32[8]{0:T(128)S(1)}, s32[8]{0:T(128)}, u32[]{:S(2)}) copy-start(s32[8]{0:T(128)} %param.26) | copy-start | bytes 100
  183.1 79.1 %collective-permute-start.3 = (bf16[2,512,768]{2,1,0:T(8,128)(2,1)}, bf16[2,512,768]{2,1,0:T(8,128)(2,1)S(1)}, u32[]{:S(2)}, u32[]{:S(2)}) collective-permute-start(bf16[2,512,768]{2,1,0:T(8,128)(2,1)} %get-tuple-element.49.refs_5_), channel_id=1, source_target_pairs={{0,2},{1,3},{2,0},{3,1},{4,6},{5,7},{6,4},{7,5},{8,10},{9,11},{10,... | collective-permute-start | bytes 4718600 | tf_op jit(solution)/shard_map/ppermute | solution.py:1321
  185.8 115.0 %collective-permute-start.2 = (bf16[2,512,768]{2,1,0:T(8,128)(2,1)}, bf16[2,512,768]{2,1,0:T(8,128)(2,1)}, u32[]{:S(2)}, u32[]{:S(2)}) collective-permute-start(bf16[2,512,768]{2,1,0:T(8,128)(2,1)} %get-tuple-element.49.refs_5_), channel_id=1, source_target_pairs={{0,1},{1,0},{2,3},{3,2},{4,5},{5,4},{6,7},{7,6},{8,9},{9,8},{10,11... | collective-permute-start | bytes 4718600 | tf_op jit(solution)/shard_map/ppermute | solution.py:1322
  185.9 474.6 %reduce-scatter.2.cloned.1.call-start = ((), (), s32[]{:S(2)}) async-start(), calls=%async_computation.2 | async-start | bytes 5308416 | tf_op jit(solution)/shard_map/reduce_scatter | solution.py:1338
  188.4 27.5 %copy-start.19 = (s32[8]{0:T(128)}, s32[8]{0:T(128)S(1)}, u32[]{:S(2)}) copy-start(s32[8]{0:T(128)S(1)} %get-tuple-element.106.refs_2_) | copy-start | bytes 100
  190.0 4.2 copy-start.12
  216.0 40.1 %copy-start.20 = (s32[8]{0:T(128)S(1)}, s32[8]{0:T(128)}, u32[]{:S(2)}) copy-start(s32[8]{0:T(128)} %copy-done.19) | copy-start | bytes 100
  216.0 40.1 %copy-start.15 = (bf16[768,8]{0,1:T(8,128)(2,1)S(1)}, bf16[768,8]{0,1:T(8,128)(2,1)}, u32[]{:S(2)}) copy-start(bf16[768,8]{0,1:T(8,128)(2,1)} %param.21) | copy-start | bytes 36868
  259.2 6.1 copy-start.24
  262.2 18.0 %copy-start.22 = (bf16[2,512,768]{2,1,0:T(8,128)(2,1)}, bf16[2,512,768]{2,1,0:T(8,128)(2,1)S(1)}, u32[]{:S(2)}) copy-start(bf16[2,512,768]{2,1,0:T(8,128)(2,1)S(1)} %collective-permute-done.3.refs_6_) | copy-start | bytes 4718596
  262.2 38.6 %collective-permute-start.4 = (bf16[2,512,768]{2,1,0:T(8,128)(2,1)S(1)}, bf16[2,512,768]{2,1,0:T(8,128)(2,1)S(1)}, u32[]{:S(2)}, u32[]{:S(2)}) collective-permute-start(bf16[2,512,768]{2,1,0:T(8,128)(2,1)S(1)} %collective-permute-done.3.refs_6_), channel_id=1, source_target_pairs={{0,1},{1,0},{2,3},{3,2},{4,5},{5,4},{6,7},{7,6},{8,9},{9,8},{10,11... | collective-permute-start | bytes 4718600 | tf_op jit(solution)/shard_map/ppermute | solution.py:1323
  300.7 40.9 %collective-permute-start = (bf16[2,1024,768]{2,1,0:T(8,128)(2,1)}, bf16[2,1024,768]{2,1,0:T(8,128)(2,1)}, u32[]{:S(2)}, u32[]{:S(2)}) collective-permute-start(bf16[2,1024,768]{2,1,0:T(8,128)(2,1)} %get-tuple-element.48), channel_id=1, source_target_pairs={{0,1},{1,0},{2,3},{3,2},{4,5},{5,4},{6,7},{7,6},{8,9},{9,8},{10,11... | collective-permute-start | bytes 9437192 | tf_op jit(solution)/shard_map/ppermute | solution.py:1333
  346.5 88.8 %collective-permute-start.1 = (bf16[2,512,768]{2,1,0:T(8,128)(2,1)}, bf16[2,512,768]{2,1,0:T(8,128)(2,1)S(1)}, u32[]{:S(2)}, u32[]{:S(2)}) collective-permute-start(bf16[2,512,768]{2,1,0:T(8,128)(2,1)} %slice.153), channel_id=1, source_target_pairs={{0,2},{1,3},{2,0},{3,1},{4,6},{5,7},{6,4},{7,5},{8,10},{9,11},{10,... | collective-permute-start | bytes 4718600 | tf_op jit(solution)/shard_map/ppermute | solution.py:1335
  412.0 23.3 %copy-start.1 = (f32[2,1024,768]{2,1,0:T(8,128)S(1)}, f32[2,1024,768]{2,1,0:T(8,128)}, u32[]{:S(2)}) copy-start(f32[2,1024,768]{2,1,0:T(8,128)} %copy-done) | copy-start | bytes 18874372
  647.9 5.7 copy-start.7
  647.9 7.2 %copy-start.10 = (f32[24,768]{1,0:T(8,128)S(1)}, f32[24,768]{1,0:T(8,128)}, u32[]{:S(2)}) copy-start(f32[24,768]{1,0:T(8,128)} %get-tuple-element.63) | copy-start | bytes 221188
  650.8 5.6 copy-start.14
  (8 other events, 23.9 us)
Sparse Core Ops, SparseCore 0:
  186.0 79.2 all-gather.1
  341.7 94.1 reduce-scatter.1

commit v4 on v3

--- a/solution.py
+++ b/solution.py
@@ -167,6 +167,11 @@
             held = far_ref.at[c] if k < 2 else far_out.at[c, :, at]
             return remote(held, far_out.at[c, :, at], sems, 31 + 7 * c + k, peer)
 
+        def chain_starts(first, last):
+            for c in range(min(first, chains), min(last, chains)):
+                far_hop(c, 0, here, {"fsdp": ahead}).start()
+                far_hop(c, 1, here, {"fsdp": behind}).start()
+
         def far_last(c, one, two):
             return far_hop(c, 6, one, {"fsdp": ahead}) if c < onward else far_hop(c, 6, two, {"fsdp": behind})
 
@@ -193,9 +198,7 @@
             hop(0, here, {"fsdp": ahead}).start()
             hop(1, here, {"fsdp": behind}).start()
             far_own().start()
-            for c in range(chains):
-                far_hop(c, 0, here, {"fsdp": ahead}).start()
-                far_hop(c, 1, here, {"fsdp": behind}).start()
+            chain_starts(0, 1)
         else:
             wcat_ref[...] = cat_ref[...]
         for k in range(micro):
@@ -220,31 +223,18 @@
                 hop(2 * k - 1, two, {"fsdp": behind}).wait_recv()
                 if k < 3:
                     hop(2 * k + 1, two, {"fsdp": behind}).start()
+                chain_starts(k, k + 1)
         copy("n_over", 0).wait_recv()
         copy("n_far", 0).start()
         copy("n_over", 1).start()
         copy("n_side", 1).start()
         if ring:
             hop(6, before_on_cycle(one), {"fsdp": ahead}).wait_recv()
+            chain_starts(4, chains)
         copy("n_side", 0).wait_recv()
         copy("n_far", 0).wait_recv()
         for k in range(micro):
             keep(0, k).start()
-
-    if ring:
-        for turn in range(3 * chains):
-            k, c = turn // chains + 1, turn % chains
-
-            @pl.when(step == 2 + turn * 16 // (3 * chains))
-            def _(k=k, c=c):
-                one, two = along(k)
-                far_hop(c, 2 * k - 2, one, {"fsdp": ahead}).wait_recv()
-                far_hop(c, 2 * k - 1, two, {"fsdp": behind}).wait_recv()
-                if k < 3:
-                    far_hop(c, 2 * k, one, {"fsdp": ahead}).start()
-                    far_hop(c, 2 * k + 1, two, {"fsdp": behind}).start()
-                else:
-                    far_last(c, one, two).start()
 
     @pl.when(step == STEPS)
     def _():
@@ -322,6 +312,21 @@
             copy("m_side", c).start()
             keep(1, c).start()
             keep(2, c).start()
+
+    if ring:
+        for turn in range(3 * chains):
+            k, c = turn // chains + 1, turn % chains
+
+            @pl.when(step == 2 + turn * 16 // (3 * chains))
+            def _(k=k, c=c):
+                one, two = along(k)
+                far_hop(c, 2 * k - 2, one, {"fsdp": ahead}).wait_recv()
+                far_hop(c, 2 * k - 1, two, {"fsdp": behind}).wait_recv()
+                if k < 3:
+                    far_hop(c, 2 * k, one, {"fsdp": ahead}).start()
+                    far_hop(c, 2 * k + 1, two, {"fsdp": behind}).start()
+                else:
+                    far_last(c, one, two).start()
 
     def keep_near():
         return pltpu.make_async_copy(near_ref, near_out, local_sem.at[8])
@@ -819,14 +824,14 @@
 BACK = 34
 FAR_STEPS = (3, 6, 10, 17, 20, 23, 28, 32)
 BACK_NAMES = (
-    "a_dx", "b_dx", "g_over", "g_side", "g_far", "p_far", "p_own", "p_over"
+    "a_dx", "a_own", "b_dx", "g_over", "g_side", "g_far", "p_far", "p_own", "p_over"
 )
 
 
 def backward_kernel(heads, ring, dxs, dxk, hid_ref, cot_ref, tok_ref, moe_ref, xn_ref,
                     gain1_ref, gain2_ref, router_ref, full_ref, w_ref, lo_ref, mixed_ref, lse_ref, wsend_ref, wkeep_ref,
-                    gt_ref, cat_out, small_out, wy_ref, wz_ref, wl_ref, adx_s, bdx_s, kp_s, hid_s, cot_s, moe_s, g_s,
-                    part_s, xn_s, k_s, kt_s, v_s, dqt_s, dkt_s, dvt_s, dcat_s, small_s, cat_s, caty_s, catz_s, sm_s,
+                    gt_ref, cat_out, small_out, wy_ref, wz_ref, wo_ref, wl0_ref, wl1_ref, wl2_ref, adx_s, bdx_s, kp_s, hid_s, cot_s, moe_s, g_s,
+                    part_s, xn_s, q_s, k_s, kt_s, v_s, dqt_s, dkt_s, dvt_s, dcat_s, small_s, cat_s, caty_s, catz_s, sm_s,
                     stage_s, send_sem, recv_sem, load_sem):
     micro, part, width = tok_ref.shape
     seq = part * 4
@@ -838,6 +843,7 @@
     side = {"tp": me ^ 1}
     over = {"tp": me ^ 2}
     sems = (send_sem, recv_sem)
+    wl_refs = (wl0_ref, wl1_ref, wl2_ref)
     mine = pl.ds(pl.multiple_of(me * part, part), part)
     theirs = pl.ds(pl.multiple_of((me ^ 2) * part, part), part)
     top, low = pl.ds(0, part), pl.ds(part, part)
@@ -845,7 +851,8 @@
 
     def copy(name, k):
         table = {
-            "a_dx": (0, dxs.at[k], adx_s.at[k], side),
+            "a_dx": (0, dxs.at[k, low], adx_s.at[k, low], side),
+            "a_own": (2, dxs.at[k, top], adx_s.at[k, top], side),
             "b_dx": (1, adx_s.at[k, low], bdx_s.at[k], over),
             "g_over": (4, g_s.at[k, mine], g_s.at[k, mine], over),
             "g_side": (5, g_s.at[k, mine], g_s.at[k, mine], side),
@@ -893,6 +900,7 @@
         copy("b_dx", k).start()
 
     def hidden_grad(k):
+        copy("a_own", k).wait_recv()
         copy("b_dx", k).wait_recv()
         wait(("hid", "cot", "moe"), k)
 
@@ -963,14 +971,17 @@
             return remote(wsend_ref.at[i], wy_ref.at[i], sems, 31 + i, pair)
 
         def far_z(i, k):
-            return remote(wz_ref.at[i, k + 1], wl_ref.at[k, i], sems, 31 + pieces_w + 3 * i + k, line[k])
+            return remote(wz_ref.at[i, k], wl_refs[k].at[i], sems, 31 + pieces_w + 3 * i + k, line[k])
 
         def far_load(i, which):
             source = wkeep_ref.at[i] if which == 0 else wy_ref.at[i]
             return pltpu.make_async_copy(source, stage_s.at[which], load_sem.at[8 + which])
 
         def far_store(i):
-            return pltpu.make_async_copy(stage_s.at[2], wz_ref.at[i], load_sem.at[10])
+            return (
+                pltpu.make_async_copy(stage_s.at[2, 1:4], wz_ref.at[i], load_sem.at[10]),
+                pltpu.make_async_copy(stage_s.at[2, 0], wo_ref.at[i], load_sem.at[11]),
+            )
 
         def far_first(i):
             far_y(i).wait_recv()
@@ -984,12 +995,29 @@
             far_load(i, 1).wait()
             for k in range(4):
                 stage_s[2, k] = (stage_s[0, k].astype(F32) + stage_s[1, k].astype(F32)).astype(BF16)
-            far_store(i).start()
+            for store in far_store(i):
+                store.start()
 
         def far_third(i):
-            far_store(i).wait()
+            for store in far_store(i):
+                store.wait()
             for k in range(3):
                 far_z(i, k).start()
+
+    def project():
+        def body(i, _):
+            rows = pl.ds(pl.multiple_of(i * QB, QB), QB)
+            proj = dot_nn(xn_s[rows, :], w_ref[:, :cols]).astype(BF16)
+            for h in range(heads):
+                base = h * 3 * HEAD_DIM
+                q_s[h, rows, :] = proj[:, base : base + HEAD_DIM] * 0.125
+                k_new = proj[:, base + HEAD_DIM : base + 2 * HEAD_DIM]
+                k_s[h, rows, :] = k_new
+                kt_s[h, :, rows] = k_new.T
+                v_s[h, rows, :] = proj[:, base + 2 * HEAD_DIM : base + 3 * HEAD_DIM]
+            return 0
+
+        lax.fori_loop(0, nq, body, 0)
 
     def far_piece(i):
         if ring and i < wy_ref.shape[0]:
@@ -1004,6 +1032,7 @@
             peers += [pair] + line + [tp_peers[2]]
         greet(peers)
         copy("a_dx", 0).start()
+        copy("a_own", 0).start()
         start(("keep", "hid", "cot", "moe", "xn"), 0)
         dcat_s[...] = jnp.zeros_like(dcat_s)
         small_s[...] = jnp.zeros_like(small_s)
@@ -1011,9 +1040,12 @@
         dvt_s[...] = jnp.zeros_like(dvt_s)
         half_sum(0)
         copy("a_dx", 1).start()
+        copy("a_own", 1).start()
         if ring:
             for i in range(min(4, pieces_w)):
                 far_y(i).start()
+        wait(("xn",), 0)
+        project()
         far_piece(0)
         hidden_grad(0)
         start(("keep", "hid", "cot", "moe"), 1)
@@ -1025,7 +1057,6 @@
         far_piece(3)
         copy("g_side", 0).wait_recv()
         copy("g_far", 0).wait_recv()
-        wait(("xn",), 0)
 
     def attend(m, blk):
         rows = pl.ds(pl.multiple_of(blk * QB, QB), QB)
@@ -1034,7 +1065,6 @@
         def window(nk):
             begin = pl.multiple_of((blk - (nk - 1)) * QB, QB)
             keys = pl.ds(begin, nk * QB)
-            proj = dot_nn(xn_s[rows, :], w_ref[:, :cols]).astype(BF16)
             g = g_s[m, rows, :]
             gm_t = dot_nn(g, w_ref[:, cols:]).astype(BF16).T
             mixed_t = mixed_ref[m, :, rows]
@@ -1044,13 +1074,8 @@
             kpos = begin + lax.broadcasted_iota(I32, (nk * QB, QB), 0)
             qpos = blk * QB + lax.broadcasted_iota(I32, (QB, QB), 1)
             for h in range(heads):
-                base = h * 3 * HEAD_DIM
                 at = slice(h * HEAD_DIM, (h + 1) * HEAD_DIM)
-                q = proj[:, base : base + HEAD_DIM] * 0.125
-                k_new = proj[:, base + HEAD_DIM : base + 2 * HEAD_DIM]
-                k_s[h, rows, :] = k_new
-                kt_s[h, :, rows] = k_new.T
-                v_s[h, rows, :] = proj[:, base + 2 * HEAD_DIM : base + 3 * HEAD_DIM]
+                q = q_s[h, rows, :]
                 drow = jnp.sum(prod[at], axis=0, keepdims=True)
                 s = dot_nt(k_s[h, keys, :], q)
                 s = jnp.where(kpos >= lo, s, NEG)
@@ -1153,6 +1178,7 @@
         copy("g_far", 1).wait_recv()
         start(("tok",), 0)
         wait(("xn",), 1)
+        project()
 
     @event(20)
     def _():
@@ -1238,15 +1264,14 @@
             once((1, width)), once((1, width)), once(router.shape), once(full.shape), once(w_cat.shape), once(low.shape),
             once(mixed_t.shape), once(lse.shape),
         ] + [anywhere] * (2 + len(deps)),
-        out_specs=[once((micro, part, width)), once(cat_shape), once((24, width))] + [anywhere] * 3,
+        out_specs=[once((micro, part, width)), once(cat_shape), once((24, width))] + [anywhere] * 6,
         out_shape=[
             jax.ShapeDtypeStruct((micro, part, width), BF16),
             jax.ShapeDtypeStruct(cat_shape, F32),
             jax.ShapeDtypeStruct((24, width), F32),
             jax.ShapeDtypeStruct((pieces,) + block, BF16),
-            jax.ShapeDtypeStruct((pieces,) + block, BF16),
-            jax.ShapeDtypeStruct((3, pieces) + block[1:], BF16),
-        ],
+            jax.ShapeDtypeStruct((pieces, 3) + block[1:], BF16),
+        ] + [jax.ShapeDtypeStruct((pieces,) + block[1:], BF16)] * 4,
         scratch_shapes=[
             pltpu.VMEM((micro, 2 * part, dxw), BF16),
             pltpu.VMEM((micro, part, dxw), BF16),
@@ -1257,6 +1282,7 @@
             pltpu.VMEM((micro, seq, width), BF16),
             pltpu.VMEM((4, part, width), BF16),
             pltpu.VMEM((seq, width), BF16),
+            pltpu.VMEM((heads, seq, HEAD_DIM), BF16),
             pltpu.VMEM((heads, seq, HEAD_DIM), BF16),
             pltpu.VMEM((heads, HEAD_DIM, seq), BF16),
             pltpu.VMEM((heads, seq, HEAD_DIM), BF16),
@@ -1272,7 +1298,7 @@
             pltpu.VMEM((3,) + block, BF16),
             pltpu.SemaphoreType.DMA((31 + 4 * pieces,)),
             pltpu.SemaphoreType.DMA((31 + 4 * pieces,)),
-            pltpu.SemaphoreType.DMA((11,)),
+            pltpu.SemaphoreType.DMA((12,)),
         ],
         compiler_params=pltpu.CompilerParams(
             dimension_semantics=("arbitrary",), vmem_limit_bytes=60 * 1024 * 1024, collective_id=2, has_side_effects=True
@@ -1349,7 +1375,7 @@
     full = jnp.sum(jnp.where(mine[..., None] == lanes, gates.transpose(0, 2, 1)[..., None], 0.0), axis=2)
     router_wide = jnp.pad(router, ((0, 0), (0, 128 - experts)))
     dxs, dxk = combine(tables, (back_near, back_far), meta, False)
-    grad_tokens, grad_cat, small, _, wz, wl = backward_half(
+    grad_tokens, grad_cat, small, _, _, *shares = backward_half(
         dxs, dxk, hidden, cotangent, tokens, moe, xn, gain_attn[None], gain_moe[None], router_wide, full, w_cat, low, mixed_t,
         lse, wsend, wkeep, ring, (output,)
     )
@@ -1358,7 +1384,7 @@
         grad_cat = lax.psum_scatter(grad_cat.astype(BF16), "fsdp", scatter_dimension=0, tiled=True).astype(F32)
         small = lax.psum(small, ("fsdp", "tp"))
     if ring:
-        dw_far = (wz[:, 0].astype(F32) + wl[0].astype(F32)) + (wl[1].astype(F32) + wl[2].astype(F32))
+        dw_far = sum(share.astype(F32) for share in shares)
         dw_far = dw_far.reshape((experts - NEAR, 2) + dw_far.shape[1:])
     dw = jnp.concatenate([dw_near, dw_far], axis=0)
     return (

time: 681 us -> 662 us (0.972)
  Pallas kernels: 602 us -> 590 us
    pallas_call x1, Pallas kernels: 169 us -> 156 us  [forward_half(): pl.pallas_call(lambda *refs: forward_kernel(heads, ring, *refs), grid=(2...]
  transfers between devices with their start and end apart: 7 -> 7, of which waited for: 1 -> 1; matrix products, arithmetic and copies ran while one was open for 5% -> 5% of each run, Pallas kernels for 64% -> 66%
where the time goes in v4:
time: 662 us; the launch traced here: 654 us
  Pallas kernels  590 us (89%)
  other arithmetic  29.8 us (5%)
  between operations  16.1 us (2%)
  local copies, waits for them, and re-layouts  14.2 us (2%)
    pallas_call x1, Pallas kernels, backward_half(): pl.pallas_call(lambda *refs: backward_kernel(heads, ring, *refs[:17], *re...  207 us
    pallas_call x1, Pallas kernels, forward_half(): pl.pallas_call(lambda *refs: forward_kernel(heads, ring, *refs), grid=(2...  156 us
    pallas_call x2, Pallas kernels, experts_backward(): pl.pallas_call(lambda *refs: expert_backward_kernel(split, *refs[:9], *re...  88.5 us
    pallas_call x2, Pallas kernels, experts_forward(): pl.pallas_call(lambda *refs: expert_forward_kernel(*refs[:6], *refs[6 + l...  56.6 us
    pallas_call x2, Pallas kernels, combine(): pl.pallas_call(lambda *refs: combine_kernel(starts, gated, *refs), grid_s...  43.5 us
    pallas_call x1, Pallas kernels, dispatch(): pl.pallas_call(lambda *refs: dispatch_kernel(experts, *refs), grid_spec=s...  21.7 us
    pallas_call x1, Pallas kernels, dispatch_gated(): pl.pallas_call(lambda *refs: gated_kernel(experts, *refs[:8], *refs[8 + l...  16.7 us
  transfers between devices with their start and end apart: 7, of which 1 were waited for; matrix products, arithmetic and copies ran while one was open for 5% of the time, Pallas kernels for 66%

profile of v4, /device:TPU:0, one launch (start us, length us, event | category | flops | bytes accessed | tf_op | source)
XLA Modules:
  0.0 654.2 jit_solution(16397595272509279810)
XLA Ops:
  7.3 3.0 fusion.5.refs_6_
  14.1 155.5 %forward_half.1 = (bf16[2,2048,768]{2,1,0:T(8,128)(2,1)}, bf16[2,4,512,768]{3,2,1,0:T(8,128)(2,1)}, bf16[2,512,768]{2,1,0:T(8,128)(2,1)}, bf16[2,192,2048]{2,1,0...) custom-call(bf16[2,512,768]{2,1,0:T(8,128)(2,1)} %refs_4_.1, ...), custom_call_target="tpu_custom_call" | custom-call | flops 99999997952 | bytes 100000000 | tf_op jit(solution)/shard_map/forward_half/pallas_call | solution.py:381
  169.7 1.6 collective-permute-start.3
  179.6 21.7 %dispatch.1 = (bf16[8,1792,768]{2,1,0:T(8,128)(2,1)}, f32[8,8,512]{2,1,0:T(8,128)}) custom-call(s32[8,8]{1,0:T(8,128)} %bitcast.78, s32[8,8]{1,0:T(8,128)} %bitcast.85, s32[8,8]{1,0:T(8,128)} %sub.114.refs_2_, bf16[8,512,768]{2,1,0:T(8,128)(2,1)} %bitcast.92, bf16[8,768]{1,0:T(8,128)(2,1)} %bitcast.82, s32[8,8,512]{2,1,0:T(8,128)} %bitcast_select_fusion.refs_5_), custom_call_target="tpu_custom_call" | custom-call | flops 20000000000 | bytes 20000000 | tf_op jit(solution)/shard_map/dispatch/pallas_call | solution.py:528
  201.3 42.8 %experts_forward.2 = (bf16[6,1792,768]{2,1,0:T(8,128)(2,1)}, f32[6,1792,768]{2,1,0:T(8,128)}) custom-call(s32[42]{0:T(128)} %get-tuple-element.119.refs_0_, s32[42]{0:T(128)} %get-tuple-element.120.refs_1_, s32[8]{0:T(128)} %copy-done.15, s32[1]{0:T(128)} %bitcast.26.refs_3_, bf16[8,1792,768]{2,1,0:T(8,128)(2,1)} %get-tuple-element.43.refs_4_.refs_5_, ...), custom_call_target="tpu_custom_call" | custom-call | flops 35999997952 | bytes 60000000 | tf_op jit(solution)/shard_map/experts_forward/pallas_call | solution.py:673
  248.1 1.5 select_reduce_fusion.refs_10_
  250.8 13.9 %experts_forward.3 = (bf16[2,1792,768]{2,1,0:T(8,128)(2,1)}, f32[2,1792,768]{2,1,0:T(8,128)}) custom-call(s32[14]{0:T(128)} %copy-done.20, s32[14]{0:T(128)} %fusion.22.refs_1_, s32[8]{0:T(128)} %copy-done.15, s32[1]{0:T(128)} %bitcast.15.refs_3_, bf16[8,1792,768]{2,1,0:T(8,128)(2,1)} %get-tuple-element.43.refs_4_.refs_5_, ...), custom_call_target="tpu_custom_call" | custom-call | flops 12000000000 | bytes 20000000 | tf_op jit(solution)/shard_map/experts_forward/pallas_call | solution.py:673
  264.7 20.5 %combine.2 = (bf16[2,1024,768]{2,1,0:T(8,128)(2,1)}, bf16[2,1024,768]{2,1,0:T(8,128)(2,1)}) custom-call(s32[8,8]{1,0:T(8,128)} %bitcast.79, s32[8,8]{1,0:T(8,128)} %bitcast.86, s32[8,8]{1,0:T(8,128)} %sub.114.refs_2_, bf16[2,1792,768]{2,1,0:T(8,128)(2,1)} %get-tuple-element.47.refs_3_, bf16[6,1792,768]{2,1,0:T(8,128)(2,1)} %get-tuple-element.46.refs_6_.refs_4_, ...), custom_call_target="tpu_custom_call" | custom-call | flops 20000000000 | bytes 20000000 | tf_op jit(solution)/shard_map/combine/pallas_call | solution.py:782
  285.3 1.1 copy-done.19
  286.5 16.7 %dispatch_gated.1.refs_6_ = bf16[8,1792,768]{2,1,0:T(8,128)(2,1)} custom-call(s32[8,8]{1,0:T(8,128)} %bitcast.80, s32[8,8]{1,0:T(8,128)} %bitcast.87, s32[8,8]{1,0:T(8,128)} %sub.114.refs_2_, bf16[2,512,768]{2,1,0:T(8,128)(2,1)} %collective-permute-done.2.refs_3_, bf16[2,512,768]{2,1,0:T(8,128)(2,1)} %copy-done.19, ...), custom_call_target="tpu_custom_call" | custom-call | flops 20000000000 | bytes 20000000 | tf_op jit(solution)/shard_map/dispatch_gated/pallas_call | solution.py:558
  303.2 20.9 %experts_backward.2 = (bf16[2,1792,896]{2,1,0:T(8,128)(2,1)}, bf16[2,2,768,768]{3,2,1,0:T(8,128)(2,1)}) custom-call(s32[14]{0:T(128)} %copy-done.20, s32[14]{0:T(128)} %fusion.22.refs_1_, s32[8]{0:T(128)} %copy-done.15, s32[1]{0:T(128)} %bitcast.15.refs_3_, s32[8]{0:T(128)} %pad_add_fusion.refs_4_, bf16[8,1792,768]{2,1,0:T(8,128)(2,1)} %get-tuple-element.43.refs_4_.refs_5_, ...), custom_call_target="tpu_custom_call" | custom-call | flops 20000000000 | bytes 20000000 | tf_op jit(solution)/shard_map/experts_backward/pallas_call | solution.py:708
  324.1 3.5 convert_add_fusion.refs_10_
  327.7 1.4 slice.135
  329.1 1.4 collective-permute-start.1
  330.8 67.6 %experts_backward.3 = (bf16[6,1792,896]{2,1,0:T(8,128)(2,1)}, bf16[6,2,4,96,768]{4,3,2,1,0:T(8,128)(2,1)}, bf16[6,2,4,96,768]{4,3,2,1,0:T(8,128)(2,1)}) custom-call(s32[42]{0:T(128)} %get-tuple-element.119.refs_0_, s32[42]{0:T(128)} %get-tuple-element.120.refs_1_, s32[8]{0:T(128)} %copy-done.15, s32[1]{0:T(128)} %bitcast.26.refs_3_, s32[8]{0:T(128)} %pad_add_fusion.refs_4_, ...), custom_call_target="tpu_custom_call" | custom-call | flops 60000002048 | bytes 60000000 | tf_op jit(solution)/shard_map/experts_backward/pallas_call | solution.py:708
  398.4 23.0 %combine.3 = (bf16[2,1024,896]{2,1,0:T(8,128)(2,1)}, bf16[2,1024,896]{2,1,0:T(8,128)(2,1)}) custom-call(s32[8,8]{1,0:T(8,128)} %bitcast.81, s32[8,8]{1,0:T(8,128)} %bitcast.88, s32[8,8]{1,0:T(8,128)} %sub.114.refs_2_, bf16[2,1792,896]{2,1,0:T(8,128)(2,1)} %get-tuple-element.53.refs_9_.refs_3_, bf16[6,1792,896]{2,1,0:T(8,128)(2,1)} %get-tuple-element.55.refs_4_, ...), custom_call_target="tpu_custom_call" | custom-call | flops 20000000000 | bytes 20000000 | tf_op jit(solution)/shard_map/combine/pallas_call | solution.py:782
  421.4 3.6 fusion.1.refs_17_
  425.0 207.3 %backward_half.1 = (bf16[2,512,768]{2,1,0:T(8,128)(2,1)}, f32[96,768]{1,0:T(8,128)}, f32[24,768]{1,0:T(8,128)}, bf16[12,4,96,768]{3,2,1,0:T(8,128)(2,1)}, bf16[1...) custom-call(bf16[2,1024,896]{2,1,0:T(8,128)(2,1)} %get-tuple-element, ...), custom_call_target="tpu_custom_call" | custom-call | flops 149999992832 | bytes 100000000 | tf_op jit(solution)/shard_map/backward_half/pallas_call | solution.py:1260
  632.3 1.7 slice.78
  635.7 2.0 slice_reduce_fusion
  638.2 4.0 convert_add_fusion.1
  642.2 1.2 convert_element_type.52
  643.4 2.6 fusion.4
  646.0 1.1 copy.85
  (119 shorter events, 18.6 us)
Async XLA Ops:
  7.2 243.6 %all-gather.2.cloned.1.call-start = ((), (), s32[]{:S(2)}) async-start(), calls=%async_computation.1 | async-start | bytes 5308416 | tf_op jit(solution)/shard_map/all_gather | solution.py:1343
  7.3 3.9 copy-start.13
  7.3 4.2 copy-start.9
  7.3 4.8 copy-start.12
  7.3 5.4 copy-start.7
  7.3 6.1 copy-start.6
  14.1 157.4 %copy-start.5 = (s32[2,2048,2]{1,2,0:T(2,128)S(1)}, s32[2,2048,2]{1,2,0:T(2,128)}, u32[]{:S(2)}) copy-start(s32[2,2048,2]{1,2,0:T(2,128)} %param.25) | copy-start | bytes 98308
  14.1 157.7 %copy-start.17 = (s32[4]{0:T(128)S(1)}, s32[4]{0:T(128)}, u32[]{:S(2)}) copy-start(s32[4]{0:T(128)} %constant.151.clone) | copy-start | bytes 52
  14.1 157.7 %copy-start.14 = (s32[8]{0:T(128)S(1)}, s32[8]{0:T(128)}, u32[]{:S(2)}) copy-start(s32[8]{0:T(128)} %param.26) | copy-start | bytes 100
  169.7 80.5 %collective-permute-start.3 = (bf16[2,512,768]{2,1,0:T(8,128)(2,1)}, bf16[2,512,768]{2,1,0:T(8,128)(2,1)S(1)}, u32[]{:S(2)}, u32[]{:S(2)}) collective-permute-start(bf16[2,512,768]{2,1,0:T(8,128)(2,1)} %get-tuple-element.51.refs_5_), channel_id=1, source_target_pairs={{0,2},{1,3},{2,0},{3,1},{4,6},{5,7},{6,4},{7,5},{8,10},{9,11},{10,... | collective-permute-start | bytes 4718600 | tf_op jit(solution)/shard_map/ppermute | solution.py:1347
  171.3 114.1 %collective-permute-start.2 = (bf16[2,512,768]{2,1,0:T(8,128)(2,1)}, bf16[2,512,768]{2,1,0:T(8,128)(2,1)}, u32[]{:S(2)}, u32[]{:S(2)}) collective-permute-start(bf16[2,512,768]{2,1,0:T(8,128)(2,1)} %get-tuple-element.51.refs_5_), channel_id=1, source_target_pairs={{0,1},{1,0},{2,3},{3,2},{4,5},{5,4},{6,7},{7,6},{8,9},{9,8},{10,11... | collective-permute-start | bytes 4718600 | tf_op jit(solution)/shard_map/ppermute | solution.py:1348
  171.3 471.0 %reduce-scatter.2.cloned.1.call-start = ((), (), s32[]{:S(2)}) async-start(), calls=%async_computation.2 | async-start | bytes 5308416 | tf_op jit(solution)/shard_map/reduce_scatter | solution.py:1364
  173.8 27.5 %copy-start.15 = (s32[8]{0:T(128)}, s32[8]{0:T(128)S(1)}, u32[]{:S(2)}) copy-start(s32[8]{0:T(128)S(1)} %get-tuple-element.110.refs_2_) | copy-start | bytes 100
  175.4 4.2 copy-start.8
  201.3 42.8 %copy-start.16 = (s32[8]{0:T(128)S(1)}, s32[8]{0:T(128)}, u32[]{:S(2)}) copy-start(s32[8]{0:T(128)} %copy-done.15) | copy-start | bytes 100
  201.3 42.8 %copy-start.11 = (bf16[768,8]{0,1:T(8,128)(2,1)S(1)}, bf16[768,8]{0,1:T(8,128)(2,1)}, u32[]{:S(2)}) copy-start(bf16[768,8]{0,1:T(8,128)(2,1)} %param.21) | copy-start | bytes 36868
  247.2 3.6 copy-start.20
  250.2 14.5 %copy-start.18 = (bf16[2,512,768]{2,1,0:T(8,128)(2,1)}, bf16[2,512,768]{2,1,0:T(8,128)(2,1)S(1)}, u32[]{:S(2)}) copy-start(bf16[2,512,768]{2,1,0:T(8,128)(2,1)S(1)} %collective-permute-done.3.refs_6_) | copy-start | bytes 4718596
  250.2 35.1 %collective-permute-start.4 = (bf16[2,512,768]{2,1,0:T(8,128)(2,1)S(1)}, bf16[2,512,768]{2,1,0:T(8,128)(2,1)S(1)}, u32[]{:S(2)}, u32[]{:S(2)}) collective-permute-start(bf16[2,512,768]{2,1,0:T(8,128)(2,1)S(1)} %collective-permute-done.3.refs_6_), channel_id=1, source_target_pairs={{0,1},{1,0},{2,3},{3,2},{4,5},{5,4},{6,7},{7,6},{8,9},{9,8},{10,11... | collective-permute-start | bytes 4718600 | tf_op jit(solution)/shard_map/ppermute | solution.py:1349
  285.2 38.9 %collective-permute-start = (bf16[2,1024,768]{2,1,0:T(8,128)(2,1)}, bf16[2,1024,768]{2,1,0:T(8,128)(2,1)}, u32[]{:S(2)}, u32[]{:S(2)}) collective-permute-start(bf16[2,1024,768]{2,1,0:T(8,128)(2,1)} %get-tuple-element.50), channel_id=1, source_target_pairs={{0,1},{1,0},{2,3},{3,2},{4,5},{5,4},{6,7},{7,6},{8,9},{9,8},{10,11... | collective-permute-start | bytes 9437192 | tf_op jit(solution)/shard_map/ppermute | solution.py:1359
  327.6 3.2 copy-start
  329.1 92.3 %collective-permute-start.1 = (bf16[2,512,768]{2,1,0:T(8,128)(2,1)}, bf16[2,512,768]{2,1,0:T(8,128)(2,1)S(1)}, u32[]{:S(2)}, u32[]{:S(2)}) collective-permute-start(bf16[2,512,768]{2,1,0:T(8,128)(2,1)} %slice.135), channel_id=1, source_target_pairs={{0,2},{1,3},{2,0},{3,1},{4,6},{5,7},{6,4},{7,5},{8,10},{9,11},{10,... | collective-permute-start | bytes 4718600 | tf_op jit(solution)/shard_map/ppermute | solution.py:1361
  398.4 23.0 %copy-start.1 = (f32[2,1024,768]{2,1,0:T(8,128)S(1)}, f32[2,1024,768]{2,1,0:T(8,128)}, u32[]{:S(2)}) copy-start(f32[2,1024,768]{2,1,0:T(8,128)} %copy-done) | copy-start | bytes 18874372
  425.0 212.7 %copy-start.10 = (f32[768]{0:T(1024)S(1)}, f32[768]{0:T(1024)}, u32[]{:S(2)}) copy-start(f32[768]{0:T(1024)} %param.17) | copy-start | bytes 9220
  (4 other events, 9.9 us)
Sparse Core Ops, SparseCore 0:
  171.4 79.3 all-gather.1
  324.2 96.5 reduce-scatter.1

commit v5 on v4

--- a/solution.py
+++ b/solution.py
@@ -21,7 +21,7 @@
 VMEM_LIMIT = 56 * 1024 * 1024
 GELU_A = math.sqrt(2.0 / math.pi)
 GELU_B = 0.044715
-NEAR = 2
+NEAR = 3
 
 
 def dot_nn(a, b):
@@ -1353,9 +1353,9 @@
     list_near = chunk_list(0, NEAR, totals, most // CHUNK)
     list_far = chunk_list(NEAR, experts - NEAR, totals, most // CHUNK)
     fwd_far, pre_far = experts_forward(NEAR, list_far, xs, w_far)
-    fwd_near, pre_near = experts_forward(0, list_near, xs, w_near, (fwd_far,))
+    gs = dispatch_gated(tables, (cot_side, cot_far, cot, cot_over), meta, experts, most, (fwd_far,))
+    fwd_near, pre_near = experts_forward(0, list_near, xs, w_near, (gs,))
     out_send, out_keep = combine(tables, (fwd_near, fwd_far), meta, True)
-    gs = dispatch_gated(tables, (cot_side, cot_far, cot, cot_over), meta, experts, most, (out_keep,))
     out_got = lax.ppermute(out_send, "tp", core)
     out_both = out_keep.astype(F32) + out_got.astype(F32)
     out_away = lax.ppermute(out_both[:, part:].astype(BF16), "tp", chip)

time: 662 us -> 658 us (level)
  Pallas kernels: 590 us -> 562 us
  waiting for transfers between devices: 0.39 us -> 23.5 us
    all_gather x1, waiting for transfers between devices: 0.32 us -> 19.9 us  [local(): w_near = lax.all_gather(near, 'fsdp', axis=2, tiled=True)]
    pallas_call x1, Pallas kernels: 156 us -> 141 us  [forward_half(): pl.pallas_call(lambda *refs: forward_kernel(heads, ring, *refs), grid=(2...]
    pallas_call x1, Pallas kernels: 207 us -> 197 us  [backward_half(): pl.pallas_call(lambda *refs: backward_kernel(heads, ring, *refs[:17], *re...]
  transfers between devices with their start and end apart: 7 -> 7, of which waited for: 1 -> 2; matrix products, arithmetic and copies ran while one was open for 5% -> 5% of each run, Pallas kernels for 66% -> 58%
where the time goes in v5:
time: 658 us; the launch traced here: 649 us
  Pallas kernels  562 us (85%)
  other arithmetic  29.3 us (4%)
  waiting for transfers between devices  23.5 us (4%)
  local copies, waits for them, and re-layouts  16.2 us (2%)
  between operations  15.8 us (2%)
    pallas_call x1, Pallas kernels, backward_half(): pl.pallas_call(lambda *refs: backward_kernel(heads, ring, *refs[:17], *re...  197 us
    pallas_call x1, Pallas kernels, forward_half(): pl.pallas_call(lambda *refs: forward_kernel(heads, ring, *refs), grid=(2...  141 us
    pallas_call x2, Pallas kernels, experts_backward(): pl.pallas_call(lambda *refs: expert_backward_kernel(split, *refs[:9], *re...  86 us
    pallas_call x2, Pallas kernels, experts_forward(): pl.pallas_call(lambda *refs: expert_forward_kernel(*refs[:6], *refs[6 + l...  55.5 us
    pallas_call x2, Pallas kernels, combine(): pl.pallas_call(lambda *refs: combine_kernel(starts, gated, *refs), grid_s...  43.5 us
    pallas_call x1, Pallas kernels, dispatch(): pl.pallas_call(lambda *refs: dispatch_kernel(experts, *refs), grid_spec=s...  21.7 us
    all_gather x1, waiting for transfers between devices, local(): w_near = lax.all_gather(near, 'fsdp', axis=2, tiled=True)  19.9 us
    pallas_call x1, Pallas kernels, dispatch_gated(): pl.pallas_call(lambda *refs: gated_kernel(experts, *refs[:8], *refs[8 + l...  16.7 us
  transfers between devices with their start and end apart: 7, of which 2 were waited for; matrix products, arithmetic and copies ran while one was open for 5% of the time, Pallas kernels for 58%

profile of v5, /device:TPU:0, one launch (start us, length us, event | category | flops | bytes accessed | tf_op | source)
XLA Modules:
  0.0 648.7 jit_solution(13900732749748888806)
XLA Ops:
  7.3 2.7 fusion.5.refs_6_
  14.0 141.1 %forward_half.1 = (bf16[2,2048,768]{2,1,0:T(8,128)(2,1)}, bf16[2,4,512,768]{3,2,1,0:T(8,128)(2,1)}, bf16[2,512,768]{2,1,0:T(8,128)(2,1)}, bf16[2,192,2048]{2,1,0...) custom-call(bf16[2,512,768]{2,1,0:T(8,128)(2,1)} %refs_4_.1, ...), custom_call_target="tpu_custom_call" | custom-call | flops 99999997952 | bytes 100000000 | tf_op jit(solution)/shard_map/forward_half/pallas_call | solution.py:381
  167.4 21.7 %dispatch.1 = (bf16[8,1792,768]{2,1,0:T(8,128)(2,1)}, f32[8,8,512]{2,1,0:T(8,128)}) custom-call(s32[8,8]{1,0:T(8,128)} %bitcast.78, s32[8,8]{1,0:T(8,128)} %bitcast.85, s32[8,8]{1,0:T(8,128)} %sub.114.refs_2_, bf16[8,512,768]{2,1,0:T(8,128)(2,1)} %bitcast.90, bf16[8,768]{1,0:T(8,128)(2,1)} %bitcast.82, s32[8,8,512]{2,1,0:T(8,128)} %bitcast_select_fusion.refs_5_), custom_call_target="tpu_custom_call" | custom-call | flops 20000000000 | bytes 20000000 | tf_op jit(solution)/shard_map/dispatch/pallas_call | solution.py:528
  189.1 3.5 collective-permute-done.1.refs_6_
  192.7 33.5 %experts_forward.2 = (bf16[5,1792,768]{2,1,0:T(8,128)(2,1)}, f32[5,1792,768]{2,1,0:T(8,128)}) custom-call(s32[35]{0:T(128)} %get-tuple-element.119.refs_0_, s32[35]{0:T(128)} %get-tuple-element.120.refs_1_, s32[8]{0:T(128)} %copy-done.16, s32[1]{0:T(128)} %bitcast.26.refs_3_, bf16[8,1792,768]{2,1,0:T(8,128)(2,1)} %get-tuple-element.43.refs_4_.refs_5_, ...), custom_call_target="tpu_custom_call" | custom-call | flops 30000001024 | bytes 50000000 | tf_op jit(solution)/shard_map/experts_forward/pallas_call | solution.py:673
  227.8 16.7 %dispatch_gated.1.refs_6_ = bf16[8,1792,768]{2,1,0:T(8,128)(2,1)} custom-call(s32[8,8]{1,0:T(8,128)} %bitcast.79, s32[8,8]{1,0:T(8,128)} %bitcast.86, s32[8,8]{1,0:T(8,128)} %sub.114.refs_2_, bf16[2,512,768]{2,1,0:T(8,128)(2,1)} %copy-done.18, bf16[2,512,768]{2,1,0:T(8,128)(2,1)} %copy-done.19, bf16[2,512,768]{2,1,0:T(8,128)(2,1)} %get-tuple-element.45.refs_5_, ...), custom_call_target="tpu_custom_call" | custom-call | flops 20000000000 | bytes 20000000 | tf_op jit(solution)/shard_map/dispatch_gated/pallas_call | solution.py:558
  244.5 19.9 %all-gather.2.cloned.1.call-done.refs_5_.refs_8_ = bf16[3,2,768,768]{3,2,1,0:T(8,128)(2,1)} async-done(((bf16[3,2,96,768]{3,2,1,0:T(8,128)(2,1)}), bf16[3,2,768,768]{3,2,1,0:T(8,128)(2,1)}) %all-gather.2.cloned.1.call-update) | async-done | bytes 7077904 | tf_op jit(solution)/shard_map/all_gather | solution.py:1343
  264.4 22.0 %experts_forward.3 = (bf16[3,1792,768]{2,1,0:T(8,128)(2,1)}, f32[3,1792,768]{2,1,0:T(8,128)}) custom-call(s32[21]{0:T(128)} %copy-done.20, s32[21]{0:T(128)} %fusion.20.refs_1_, s32[8]{0:T(128)} %copy-done.16, s32[1]{0:T(128)} %bitcast.15.refs_3_, bf16[8,1792,768]{2,1,0:T(8,128)(2,1)} %get-tuple-element.43.refs_4_.refs_5_, ...), custom_call_target="tpu_custom_call" | custom-call | flops 17999998976 | bytes 30000000 | tf_op jit(solution)/shard_map/experts_forward/pallas_call | solution.py:673
  286.4 20.5 %combine.2 = (bf16[2,1024,768]{2,1,0:T(8,128)(2,1)}, bf16[2,1024,768]{2,1,0:T(8,128)(2,1)}) custom-call(s32[8,8]{1,0:T(8,128)} %bitcast.80, s32[8,8]{1,0:T(8,128)} %bitcast.87, s32[8,8]{1,0:T(8,128)} %sub.114.refs_2_, bf16[3,1792,768]{2,1,0:T(8,128)(2,1)} %get-tuple-element.49.refs_3_, bf16[5,1792,768]{2,1,0:T(8,128)(2,1)} %get-tuple-element.48.refs_8_.refs_4_, ...), custom_call_target="tpu_custom_call" | custom-call | flops 20000000000 | bytes 20000000 | tf_op jit(solution)/shard_map/combine/pallas_call | solution.py:782
  307.8 1.5 select_reduce_fusion.refs_10_
  309.3 33.5 %experts_backward.2 = (bf16[3,1792,896]{2,1,0:T(8,128)(2,1)}, bf16[3,2,768,768]{3,2,1,0:T(8,128)(2,1)}) custom-call(s32[21]{0:T(128)} %copy-done.20, s32[21]{0:T(128)} %fusion.20.refs_1_, s32[8]{0:T(128)} %copy-done.16, s32[1]{0:T(128)} %bitcast.15.refs_3_, s32[8]{0:T(128)} %pad_add_fusion.refs_4_, bf16[8,1792,768]{2,1,0:T(8,128)(2,1)} %get-tuple-element.43.refs_4_.refs_5_, ...), custom_call_target="tpu_custom_call" | custom-call | flops 30000001024 | bytes 30000000 | tf_op jit(solution)/shard_map/experts_backward/pallas_call | solution.py:708
  342.8 1.6 copy-done.4
  344.5 3.5 convert_add_fusion.refs_10_
  348.0 1.4 slice.135
  349.4 1.3 collective-permute-start.4
  351.1 52.5 %experts_backward.3 = (bf16[5,1792,896]{2,1,0:T(8,128)(2,1)}, bf16[5,2,4,96,768]{4,3,2,1,0:T(8,128)(2,1)}, bf16[5,2,4,96,768]{4,3,2,1,0:T(8,128)(2,1)}) custom-call(s32[35]{0:T(128)} %get-tuple-element.119.refs_0_, s32[35]{0:T(128)} %get-tuple-element.120.refs_1_, s32[8]{0:T(128)} %copy-done.16, s32[1]{0:T(128)} %bitcast.26.refs_3_, s32[8]{0:T(128)} %pad_add_fusion.refs_4_, ...), custom_call_target="tpu_custom_call" | custom-call | flops 49999998976 | bytes 50000000 | tf_op jit(solution)/shard_map/experts_backward/pallas_call | solution.py:708
  403.6 23.0 %combine.3 = (bf16[2,1024,896]{2,1,0:T(8,128)(2,1)}, bf16[2,1024,896]{2,1,0:T(8,128)(2,1)}) custom-call(s32[8,8]{1,0:T(8,128)} %bitcast.81, s32[8,8]{1,0:T(8,128)} %bitcast.88, s32[8,8]{1,0:T(8,128)} %sub.114.refs_2_, bf16[3,1792,896]{2,1,0:T(8,128)(2,1)} %get-tuple-element.53.refs_9_.refs_3_, bf16[5,1792,896]{2,1,0:T(8,128)(2,1)} %get-tuple-element.55.refs_4_, ...), custom_call_target="tpu_custom_call" | custom-call | flops 20000000000 | bytes 20000000 | tf_op jit(solution)/shard_map/combine/pallas_call | solution.py:782
  426.6 3.6 fusion.1.refs_17_
  430.2 197.0 %backward_half.1 = (bf16[2,512,768]{2,1,0:T(8,128)(2,1)}, f32[96,768]{1,0:T(8,128)}, f32[24,768]{1,0:T(8,128)}, bf16[10,4,96,768]{3,2,1,0:T(8,128)(2,1)}, bf16[1...) custom-call(bf16[2,1024,896]{2,1,0:T(8,128)(2,1)} %get-tuple-element, ...), custom_call_target="tpu_custom_call" | custom-call | flops 149999992832 | bytes 100000000 | tf_op jit(solution)/shard_map/backward_half/pallas_call | solution.py:1260
  627.2 2.0 slice_reduce_fusion
  629.8 1.7 slice.78
  633.2 3.4 convert_add_fusion.1
  636.6 1.3 convert_element_type.52
  637.9 2.6 fusion.4
  (119 shorter events, 21.3 us)
Async XLA Ops:
  7.2 2.9 copy-start.2
  7.2 2.9 copy-start.3
  7.2 257.2 %all-gather.2.cloned.1.call-start = ((), (), s32[]{:S(2)}) async-start(), calls=%async_computation.1 | async-start | bytes 7962624 | tf_op jit(solution)/shard_map/all_gather | solution.py:1343
  7.3 3.8 copy-start.10
  7.3 4.4 copy-start.13
  7.3 4.9 copy-start.8
  7.3 5.0 copy-start.14
  7.3 5.4 copy-start.7
  14.0 141.9 %copy-start.6 = (s32[2,2048,2]{1,2,0:T(2,128)S(1)}, s32[2,2048,2]{1,2,0:T(2,128)}, u32[]{:S(2)}) copy-start(s32[2,2048,2]{1,2,0:T(2,128)} %param.25) | copy-start | bytes 98308
  14.0 142.2 %copy-start.15 = (s32[8]{0:T(128)S(1)}, s32[8]{0:T(128)}, u32[]{:S(2)}) copy-start(s32[8]{0:T(128)} %param.26) | copy-start | bytes 100
  14.0 142.9 %copy-start.17 = (s32[4]{0:T(128)S(1)}, s32[4]{0:T(128)}, u32[]{:S(2)}) copy-start(s32[4]{0:T(128)} %constant.151.clone) | copy-start | bytes 52
  155.2 8.3 %copy-start.12 = (bf16[768,8]{0,1:T(8,128)(2,1)S(1)}, bf16[768,8]{0,1:T(8,128)(2,1)}, u32[]{:S(2)}) copy-start(bf16[768,8]{0,1:T(8,128)(2,1)} %param.21) | copy-start | bytes 36868
  155.2 481.3 %reduce-scatter.2.cloned.1.call-start = ((), (), s32[]{:S(2)}) async-start(), calls=%async_computation.2 | async-start | bytes 7962624 | tf_op jit(solution)/shard_map/reduce_scatter | solution.py:1364
  155.5 70.7 %collective-permute-start = (bf16[2,512,768]{2,1,0:T(8,128)(2,1)}, bf16[2,512,768]{2,1,0:T(8,128)(2,1)S(1)}, u32[]{:S(2)}, u32[]{:S(2)}) collective-permute-start(bf16[2,512,768]{2,1,0:T(8,128)(2,1)} %get-tuple-element.45.refs_5_), channel_id=1, source_target_pairs={{0,1},{1,0},{2,3},{3,2},{4,5},{5,4},{6,7},{7,6},{8,9},{9,8},{10,11... | collective-permute-start | bytes 4718600 | tf_op jit(solution)/shard_map/ppermute | solution.py:1348
  155.9 36.7 %collective-permute-start.1 = (bf16[2,512,768]{2,1,0:T(8,128)(2,1)}, bf16[2,512,768]{2,1,0:T(8,128)(2,1)}, u32[]{:S(2)}, u32[]{:S(2)}) collective-permute-start(bf16[2,512,768]{2,1,0:T(8,128)(2,1)} %get-tuple-element.45.refs_5_), channel_id=1, source_target_pairs={{0,2},{1,3},{2,0},{3,1},{4,6},{5,7},{6,4},{7,5},{8,10},{9,11},{10,... | collective-permute-start | bytes 4718600 | tf_op jit(solution)/shard_map/ppermute | solution.py:1347
  158.3 30.8 %copy-start.16 = (s32[8]{0:T(128)}, s32[8]{0:T(128)S(1)}, u32[]{:S(2)}) copy-start(s32[8]{0:T(128)S(1)} %get-tuple-element.110.refs_2_) | copy-start | bytes 100
  158.3 9.1 %copy-start.9 = (s32[2,4,8]{2,1,0:T(4,128)}, s32[2,4,8]{2,1,0:T(4,128)S(1)}, u32[]{:S(2)}) copy-start(s32[2,4,8]{2,1,0:T(4,128)S(1)} %copy.66) | copy-start | bytes 772
  165.2 23.9 %copy-start.20 = (s32[21]{0:T(128)}, s32[21]{0:T(128)S(1)}, u32[]{:S(2)}) copy-start(s32[21]{0:T(128)S(1)} %convert_reduce_fusion.2.refs_0_) | copy-start | bytes 256
  192.7 33.5 %collective-permute-start.2 = (bf16[2,512,768]{2,1,0:T(8,128)(2,1)}, bf16[2,512,768]{2,1,0:T(8,128)(2,1)S(1)}, u32[]{:S(2)}, u32[]{:S(2)}) collective-permute-start(bf16[2,512,768]{2,1,0:T(8,128)(2,1)} %collective-permute-done.1.refs_6_), channel_id=1, source_target_pairs={{0,1},{1,0},{2,3},{3,2},{4,5},{5,4},{6,7},{7,6},{8,9},{9,8},{10,11... | collective-permute-start | bytes 4718600 | tf_op jit(solution)/shard_map/ppermute | solution.py:1349
  306.9 35.9 %collective-permute-start.3 = (bf16[2,1024,768]{2,1,0:T(8,128)(2,1)}, bf16[2,1024,768]{2,1,0:T(8,128)(2,1)S(1)}, u32[]{:S(2)}, u32[]{:S(2)}) collective-permute-start(bf16[2,1024,768]{2,1,0:T(8,128)(2,1)} %get-tuple-element.51), channel_id=1, source_target_pairs={{0,1},{1,0},{2,3},{3,2},{4,5},{5,4},{6,7},{7,6},{8,9},{9,8},{10,11... | collective-permute-start | bytes 9437192 | tf_op jit(solution)/shard_map/ppermute | solution.py:1359
  348.0 3.1 copy-start
  349.4 77.2 %collective-permute-start.4 = (bf16[2,512,768]{2,1,0:T(8,128)(2,1)}, bf16[2,512,768]{2,1,0:T(8,128)(2,1)S(1)}, u32[]{:S(2)}, u32[]{:S(2)}) collective-permute-start(bf16[2,512,768]{2,1,0:T(8,128)(2,1)} %slice.135), channel_id=1, source_target_pairs={{0,2},{1,3},{2,0},{3,1},{4,6},{5,7},{6,4},{7,5},{8,10},{9,11},{10,... | collective-permute-start | bytes 4718600 | tf_op jit(solution)/shard_map/ppermute | solution.py:1361
  403.6 23.0 %copy-start.1 = (f32[2,1024,768]{2,1,0:T(8,128)S(1)}, f32[2,1024,768]{2,1,0:T(8,128)}, u32[]{:S(2)}) copy-start(f32[2,1024,768]{2,1,0:T(8,128)} %copy-done) | copy-start | bytes 18874372
  430.2 199.0 %copy-start.11 = (f32[768]{0:T(1024)S(1)}, f32[768]{0:T(1024)}, u32[]{:S(2)}) copy-start(f32[768]{0:T(1024)} %param.17) | copy-start | bytes 9220
  (4 other events, 7.1 us)
Sparse Core Ops, SparseCore 0:
  155.4 108.9 all-gather.1
  342.9 153.6 reduce-scatter.1
